TPU v7x, 32 devices: a whole 2x2x4 slice. The times are simulated.
32 devices in a mesh: groups: 2 (over x), tile: 16 (over z, y, core).
Axes of the slice: x: 2, y: 2, z: 4, core: 2. Of those that a mesh axis runs over, the one named last changes fastest.
Arguments:
- queries: bfloat16 [2, 256, 8192], P(None, ('groups', 'tile')), parts along dimension 1, may hold values from -120 to 120
- fresh_kv: bfloat16 [2, 2, 256, 512], P(None, None, ('groups', 'tile')), parts along dimension 2, may hold values from -6 to 6
- cache: bfloat16 [2, 256, 512, 512], P(None, ('groups', 'tile')), parts along dimension 1, may hold values from -6 to 6
- lengths: int32 [256], P(('groups', 'tile')), parts along dimension 0, may hold values from 1 to 510, 16384 in all
- out_weight: bfloat16 [16, 1024, 8192], P('tile'), may hold values from -0.0625 to 0.0625
Outputs:
- projected: bfloat16 [2, 256, 16384], P(None, ('groups', 'tile')), parts along dimension 1
There are 2 independent parts, one for each index of `groups`. A program takes and returns all parts, laid end to end along the dimension named above; an argument that names none is the same for every part. Nothing has to cross between parts.
Inputs may be any that keep to these rules, and one draw needn't show every extreme that they name: `lengths`: the longest request has exactly 510 cached tokens.
All inputs are finite; a program needn't handle non-finite values. No bound on the sum of `lengths` on one device may be relied on, other than what follows from the above.
Results may differ from a plain program's by a relative error of at most 0.0057.
Values may be sent and summed in bfloat16 or wider, within the bound.
No kernel may reach another device: no remote copies, remote signals or barrier semaphores. Data moves between devices by JAX's collectives and lax.ppermute only.
A program may use at most 128 MiB of HBM per device.

v0:
```python
import math

import jax
import jax.numpy as jnp
from jax import lax
from jax.sharding import PartitionSpec as P

QH = 64
KVH = 4
HD = 128
DECODE_STEPS = 2
GRID_ROWS = 8


def full_attention(query, cache_keys, cache_values, fresh_scores, fresh_values, lengths, factor):
    capacity = cache_keys.shape[1]
    cached_scores = (
        jnp.einsum("rkgd,rckd->rkgc", query, cache_keys, preferred_element_type=jnp.float32)
        * factor
    )
    visible = jnp.arange(capacity)[None, :] < lengths[:, None]
    cached_scores = jnp.where(visible[:, None, None, :], cached_scores, -jnp.inf)
    top = jnp.maximum(cached_scores.max(-1), fresh_scores.max(-1))[..., None]
    cached_exp = jnp.exp(cached_scores - top)
    fresh_exp = jnp.exp(fresh_scores - top)
    total = cached_exp.sum(-1, keepdims=True) + fresh_exp.sum(-1, keepdims=True)
    cached_weights = (cached_exp / total).astype(jnp.bfloat16)
    fresh_weights = (fresh_exp / total).astype(jnp.bfloat16)
    mixed = jnp.einsum(
        "rkgc,rckd->rkgd", cached_weights, cache_values, preferred_element_type=jnp.float32
    )
    mixed = mixed + jnp.einsum(
        "rkgs,srkd->rkgd", fresh_weights, fresh_values, preferred_element_type=jnp.float32
    )
    return mixed.astype(jnp.bfloat16)


def per_device(queries, fresh_kv, cache, lengths, out_weight):
    slots = cache.shape[1]
    capacity = cache.shape[2]
    per_group = QH // KVH
    factor = 1.0 / math.sqrt(HD)
    devices = lax.axis_size("tile")
    grid_cols = devices // GRID_ROWS
    row_width = out_weight.shape[1]
    col_width = out_weight.shape[2]
    block = out_weight[0]
    cache_keys = cache[0].reshape(slots, capacity, KVH, HD)
    cache_values = cache[1].reshape(slots, capacity, KVH, HD)
    results = []
    for step_index in range(DECODE_STEPS):
        seen = step_index + 1
        query = queries[step_index].reshape(slots, KVH, per_group, HD)
        fresh_keys = fresh_kv[:seen, 0].reshape(seen, slots, KVH, HD)
        fresh_values = fresh_kv[:seen, 1].reshape(seen, slots, KVH, HD)
        fresh_scores = (
            jnp.einsum("rkgd,srkd->rkgs", query, fresh_keys, preferred_element_type=jnp.float32)
            * factor
        )
        attended = full_attention(
            query, cache_keys, cache_values, fresh_scores, fresh_values, lengths, factor
        )
        own_rows = attended.reshape(slots, QH * HD)
        blocks = jnp.transpose(own_rows.reshape(slots, GRID_ROWS, row_width), (1, 0, 2))
        outgoing = jnp.broadcast_to(blocks[None], (grid_cols, GRID_ROWS, slots, row_width))
        outgoing = outgoing.reshape(devices, slots, row_width)
        partials = jnp.einsum(
            "nkf,fc->nkc",
            lax.all_to_all(outgoing, "tile", split_axis=0, concat_axis=0, tiled=True),
            block,
            preferred_element_type=jnp.float32,
        )
        returned = lax.all_to_all(partials, "tile", split_axis=0, concat_axis=0, tiled=True)
        summed = returned.reshape(grid_cols, GRID_ROWS, slots, col_width).sum(1)
        projected = jnp.transpose(summed, (1, 0, 2)).reshape(slots, grid_cols * col_width)
        results.append(projected.astype(jnp.bfloat16))
    return jnp.stack(results)


def solution(mesh):
    return jax.shard_map(
        per_device,
        mesh=mesh,
        in_specs=(
            P(None, ("groups", "tile"), None),
            P(None, None, ("groups", "tile"), None),
            P(None, ("groups", "tile"), None, None),
            P(("groups", "tile")),
            P("tile", None, None),
        ),
        out_specs=P(None, ("groups", "tile"), None),
        check_vma=False,
    )
```

profile of v0, /device:TPU:15, one launch (start us, length us, event | category | flops | bytes accessed | tf_op | source)
XLA Modules:
  0.0 257.4 jit_solution(4504851266009058107)
XLA Ops:
  0.0 0.7 iota_compare_fusion
  0.7 0.7 slice_bitcast_fusion.2
  1.5 1.0 slice_bitcast_fusion.1
  2.5 5.8 %fusion.24 = (bf16[1,8,512,512]{3,2,1,0:T(8,128)(2,1)}, bf16[1,8,512,512]{3,2,1,0:T(8,128)(2,1)}) fusion(bf16[2,8,512,512]{3,2,1,0:T(8,128)(2,1)} %param.7), kind=kLoop, calls=%fused_computation.48 | loop fusion | bytes 16777216 | tf_op jit(solution)/shard_map/slice | solution.py:49
  8.3 6.5 %copy.29 = bf16[1,8,512,512]{2,3,1,0:T(8,128)(2,1)} copy(bf16[1,8,512,512]{3,2,1,0:T(8,128)(2,1)} %get-tuple-element.5) | data formatting | bytes 8388608
  14.7 6.5 %copy.28 = bf16[1,8,512,512]{2,3,1,0:T(8,128)(2,1)} copy(bf16[1,8,512,512]{3,2,1,0:T(8,128)(2,1)} %get-tuple-element.6) | data formatting | bytes 8388608
  21.4 3.1 %fusion.25 = (f32[8,4,16]{2,1,0:T(4,128)S(1)}, f32[8,4,16,512]{3,2,1,0:T(8,128)S(1)}) fusion(bf16[8,4,16,128]{3,2,1,0:T(8,128)(2,1)S(1)} %bitcast.70, bf16[8,512,4,128]{1,3,2,0:T(8,128)(2,1)} %bitcast.63, pred[8,512]{1,0:T(8,128)(4,1)S(1)} %iota_compare_fusion), kind=kOutput, calls=%fused_computation.49 | convolution fusion | flops 67894784 | bytes 5380096 | tf_op jit(solution)/shard_map/rkgd,rckd->rkgc/dot_general | solution.py:18
  25.2 1.2 fusion.7
  26.6 0.7 broadcast_in_dim.23
  27.4 6.6 %all-to-all-start.2 = ((bf16[16,8,1024]{2,1,0:T(8,128)(2,1)}), bf16[16,8,1024]{2,1,0:T(8,128)(2,1)S(1)}, u32[]{:S(2)}, u32[]{:S(2)}) async-start(bf16[16,8,1024]{2,1,0:T(8,128)(2,1)} %bitcast.17), calls=%async_computation.2 | async-start | bytes 524288 | tf_op jit(solution)/shard_map/all_to_all | solution.py:69
  34.0 3.1 %fusion.27 = (f32[8,4,16]{2,1,0:T(4,128)S(1)}, f32[8,4,16,512]{3,2,1,0:T(8,128)S(1)}) fusion(bf16[8,4,16,128]{3,2,1,0:T(8,128)(2,1)S(1)} %bitcast.71, bf16[8,512,4,128]{1,3,2,0:T(8,128)(2,1)} %bitcast.64, pred[8,512]{1,0:T(8,128)(4,1)S(1)} %iota_compare_fusion), kind=kOutput, calls=%fused_computation.51 | convolution fusion | flops 67894784 | bytes 5380096 | tf_op jit(solution)/shard_map/rkgd,rckd->rkgc/dot_general | solution.py:18
  37.7 1.2 fusion.6
  39.1 2.8 %all-to-all-done.2 = bf16[16,8,1024]{2,1,0:T(8,128)(2,1)S(1)} async-done(((bf16[16,8,1024]{2,1,0:T(8,128)(2,1)}), bf16[16,8,1024]{2,1,0:T(8,128)(2,1)S(1)}, u32[]{:S(2)}, u32[]{:S(2)}) %all-to-all-start.2) | async-done | bytes 262176 | tf_op jit(solution)/shard_map/all_to_all | solution.py:69
  41.9 0.7 broadcast_in_dim.22
  42.6 5.5 %all-to-all-start = ((bf16[16,8,1024]{2,1,0:T(8,128)(2,1)}), bf16[16,8,1024]{2,1,0:T(8,128)(2,1)S(1)}, u32[]{:S(2)}, u32[]{:S(2)}) async-start(bf16[16,8,1024]{2,1,0:T(8,128)(2,1)} %bitcast.8), calls=%async_computation | async-start | bytes 524288 | tf_op jit(solution)/shard_map/all_to_all | solution.py:69
  48.2 10.1 %fusion = f32[16,8,8192]{2,1,0:T(8,128)} fusion(bf16[16,8,1024]{2,1,0:T(8,128)(2,1)S(1)} %all-to-all-done.2, bf16[1,1024,8192]{2,1,0:T(8,128)(2,1)} %param.9), kind=kOutput, calls=%fused_computation | convolution fusion | flops 2147483648 | bytes 21233664 | tf_op jit(solution)/shard_map/nkf,fc->nkc/dot_general | solution.py:67
  58.2 6.1 %all-to-all-start.3 = ((f32[16,8,8192]{2,1,0:T(8,128)}), f32[16,8,8192]{2,1,0:T(8,128)}, u32[]{:S(2)}, u32[]{:S(2)}) async-start(f32[16,8,8192]{2,1,0:T(8,128)} %fusion), calls=%async_computation.3 | async-start | bytes 8388608 | tf_op jit(solution)/shard_map/all_to_all | solution.py:73
  64.3 10.1 %fusion.2 = f32[16,8,8192]{2,1,0:T(8,128)} fusion(bf16[16,8,1024]{2,1,0:T(8,128)(2,1)S(1)} %all-to-all-done, bf16[1,1024,8192]{2,1,0:T(8,128)(2,1)} %param.9), kind=kOutput, calls=%fused_computation.2 | convolution fusion | flops 2147483648 | bytes 21233664 | tf_op jit(solution)/shard_map/nkf,fc->nkc/dot_general | solution.py:67
  74.4 82.4 %all-to-all-done.3 = f32[16,8,8192]{2,1,0:T(8,128)} async-done(((f32[16,8,8192]{2,1,0:T(8,128)}), f32[16,8,8192]{2,1,0:T(8,128)}, u32[]{:S(2)}, u32[]{:S(2)}) %all-to-all-start.3) | async-done | bytes 4194336 | tf_op jit(solution)/shard_map/all_to_all | solution.py:73
  156.8 4.9 %all-to-all-start.1 = ((f32[16,8,8192]{2,1,0:T(8,128)}), f32[16,8,8192]{2,1,0:T(8,128)}, u32[]{:S(2)}, u32[]{:S(2)}) async-start(f32[16,8,8192]{2,1,0:T(8,128)} %fusion.2), calls=%async_computation.1 | async-start | bytes 8388608 | tf_op jit(solution)/shard_map/all_to_all | solution.py:73
  161.7 2.4 bitcast_reduce_fusion
  164.1 90.1 %all-to-all-done.1 = f32[16,8,8192]{2,1,0:T(8,128)} async-done(((f32[16,8,8192]{2,1,0:T(8,128)}), f32[16,8,8192]{2,1,0:T(8,128)}, u32[]{:S(2)}, u32[]{:S(2)}) %all-to-all-start.1) | async-done | bytes 4194336 | tf_op jit(solution)/shard_map/all_to_all | solution.py:73
  254.2 2.4 bitcast_reduce_fusion.1
  256.6 0.8 pad_maximum_fusion
  (25 shorter events, 1.9 us)
Async XLA Ops:
  21.2 4.0 %copy-start = (bf16[1,8,512,512]{2,3,1,0:T(8,128)(2,1)S(1)}, bf16[1,8,512,512]{2,3,1,0:T(8,128)(2,1)}, u32[]{:S(2)}) copy-start(bf16[1,8,512,512]{2,3,1,0:T(8,128)(2,1)} %copy.29) | copy-start | bytes 12582916
  25.2 8.7 %copy-start.2 = (bf16[2,2,8,512]{3,2,1,0:T(8,128)(2,1)S(1)}, bf16[2,2,8,512]{3,2,1,0:T(8,128)(2,1)}, u32[]{:S(2)}) copy-start(bf16[2,2,8,512]{3,2,1,0:T(8,128)(2,1)} %param.6) | copy-start | bytes 98308
  27.4 14.5 %all-to-all-start.2 = ((bf16[16,8,1024]{2,1,0:T(8,128)(2,1)}), bf16[16,8,1024]{2,1,0:T(8,128)(2,1)S(1)}, u32[]{:S(2)}, u32[]{:S(2)}) async-start(bf16[16,8,1024]{2,1,0:T(8,128)(2,1)} %bitcast.17), calls=%async_computation.2 | async-start | bytes 524288 | tf_op jit(solution)/shard_map/all_to_all | solution.py:69
  33.9 3.8 %copy-start.1 = (bf16[1,8,512,512]{2,3,1,0:T(8,128)(2,1)S(1)}, bf16[1,8,512,512]{2,3,1,0:T(8,128)(2,1)}, u32[]{:S(2)}) copy-start(bf16[1,8,512,512]{2,3,1,0:T(8,128)(2,1)} %copy.29) | copy-start | bytes 12582916
  42.6 15.6 %all-to-all-start = ((bf16[16,8,1024]{2,1,0:T(8,128)(2,1)}), bf16[16,8,1024]{2,1,0:T(8,128)(2,1)S(1)}, u32[]{:S(2)}, u32[]{:S(2)}) async-start(bf16[16,8,1024]{2,1,0:T(8,128)(2,1)} %bitcast.8), calls=%async_computation | async-start | bytes 524288 | tf_op jit(solution)/shard_map/all_to_all | solution.py:69
  58.2 98.5 %all-to-all-start.3 = ((f32[16,8,8192]{2,1,0:T(8,128)}), f32[16,8,8192]{2,1,0:T(8,128)}, u32[]{:S(2)}, u32[]{:S(2)}) async-start(f32[16,8,8192]{2,1,0:T(8,128)} %fusion), calls=%async_computation.3 | async-start | bytes 8388608 | tf_op jit(solution)/shard_map/all_to_all | solution.py:73
  156.8 97.4 %all-to-all-start.1 = ((f32[16,8,8192]{2,1,0:T(8,128)}), f32[16,8,8192]{2,1,0:T(8,128)}, u32[]{:S(2)}, u32[]{:S(2)}) async-start(f32[16,8,8192]{2,1,0:T(8,128)} %fusion.2), calls=%async_computation.1 | async-start | bytes 8388608 | tf_op jit(solution)/shard_map/all_to_all | solution.py:73
where the time goes:
time: 258 us; the launch traced here: 257 us
  waiting for transfers between devices  175 us (68%)
  matrix products  29.4 us (11%)
  starting transfers between devices  23.1 us (9%)
  local copies, waits for them, and re-layouts  22.3 us (9%)
  other arithmetic  7.24 us (3%)
    all_to_all x2, waiting for transfers between devices, per_device(): lax.all_to_all(partials, 'tile', split_axis=0, concat_axis=0, tiled=True)  172 us
    dot_general x2, matrix products, per_device(): jnp.einsum('nkf,fc->nkc', lax.all_to_all(outgoing, 'tile', split_axis=0,...  20.2 us
    unnamed x11, local copies, waits for them, and re-layouts  14 us
    all_to_all x2, starting transfers between devices, per_device(): lax.all_to_all(outgoing, 'tile', split_axis=0, concat_axis=0, tiled=True)  12.1 us
    all_to_all x2, starting transfers between devices, per_device(): lax.all_to_all(partials, 'tile', split_axis=0, concat_axis=0, tiled=True)  11 us
    dot_general x2, matrix products, full_attention(): jnp.einsum('rkgd,rckd->rkgc', query, cache_keys, preferred_element_type=j...  6.16 us
    slice x1, local copies, waits for them, and re-layouts, per_device(): cache_values = cache[1].reshape(slots, capacity, KVH, HD)  5.79 us
  transfers between devices with their start and end apart: 4, of which 3 were waited for; matrix products, arithmetic and copies ran while one was open for 11% of the time, Pallas kernels for 0%

commit v1 on v0

v1 whole, which is shorter than its diff:
```python
import functools
import math

import jax
import jax.numpy as jnp
from jax import lax
from jax.experimental import pallas as pl
from jax.experimental.pallas import tpu as pltpu
from jax.sharding import PartitionSpec as P

QH = 64
KVH = 4
HD = 128
DECODE_STEPS = 2
GRID_ROWS = 8
GROUP = QH // KVH
BLOCK_HEADS = QH // GRID_ROWS
CHUNKS = 2
TILE_N = 512
MIB = 1 << 20


def attention_kernel(lengths_ref, query_ref, fresh_ref, cache_ref, out_ref, cached, sems):
    slots, capacity = cached.shape[1], cached.shape[2]
    factor = 1.0 / math.sqrt(HD)
    rows = DECODE_STEPS * GROUP

    def copy(which, slot):
        return pltpu.make_async_copy(
            cache_ref.at[which, slot], cached.at[which, slot], sems.at[which, slot]
        )

    for slot in range(slots):
        for which in range(2):
            copy(which, slot).start()
    position = lax.broadcasted_iota(jnp.int32, (rows, capacity), 1)
    step = lax.broadcasted_iota(jnp.int32, (rows, capacity), 0) // GROUP
    window_row = lax.broadcasted_iota(jnp.int32, (32, cached.shape[3]), 0)
    for slot in range(slots):
        length = lengths_ref[slot]
        base = pl.multiple_of(jnp.minimum((length // 16) * 16, capacity - 32), 16)
        for which in range(2):
            copy(which, slot).wait()
            window = cached[which, slot, pl.ds(base, 32), :].astype(jnp.float32)
            for t in range(DECODE_STEPS):
                fresh = fresh_ref[t, which].astype(jnp.float32)[slot : slot + 1]
                window = jnp.where(window_row + base == length + t, fresh, window)
            cached[which, slot, pl.ds(base, 32), :] = window.astype(jnp.bfloat16)
        visible = position < length + 1 + step
        for head in range(KVH):
            lanes = slice(head * HD, (head + 1) * HD)
            scores = lax.dot_general(
                query_ref[slot, head],
                cached[0, slot, :, lanes],
                (((1,), (1,)), ((), ())),
                preferred_element_type=jnp.float32,
            )
            scores = jnp.where(visible, scores * factor, -jnp.inf)
            weights = jnp.exp(scores - scores.max(-1, keepdims=True))
            weights = weights / weights.sum(-1, keepdims=True)
            mixed = jnp.dot(
                weights.astype(jnp.bfloat16),
                cached[1, slot, :, lanes],
                preferred_element_type=jnp.float32,
            )
            out_ref[slot, head] = mixed.astype(jnp.bfloat16)


def attend(queries, fresh_kv, cache, lengths):
    slots, capacity, width = cache.shape[1:]
    rows = DECODE_STEPS * GROUP
    query = queries.reshape(DECODE_STEPS, slots, KVH, GROUP, HD)
    query = jnp.transpose(query, (1, 2, 0, 3, 4)).reshape(slots, KVH, rows, HD)
    vmem = pl.BlockSpec(memory_space=pltpu.VMEM)
    return pl.pallas_call(
        attention_kernel,
        out_shape=jax.ShapeDtypeStruct((slots, KVH, rows, HD), jnp.bfloat16),
        in_specs=[
            pl.BlockSpec(memory_space=pltpu.SMEM),
            vmem,
            vmem,
            pl.BlockSpec(memory_space=pl.ANY),
        ],
        out_specs=vmem,
        scratch_shapes=[
            pltpu.VMEM((2, slots, capacity, width), jnp.bfloat16),
            pltpu.SemaphoreType.DMA((2, slots)),
        ],
        compiler_params=pltpu.CompilerParams(vmem_limit_bytes=32 * MIB),
        name="attention",
    )(lengths, query, fresh_kv, cache)


def project_kernel(place_ref, x_ref, w_ref, fg_ref, fk_ref, ng_ref, nk_ref, ordered):
    devices, _, slot_rows, _ = x_ref.shape
    cols = devices // GRID_ROWS
    far = GRID_ROWS * (cols - 1) * slot_rows

    def place(source, row):
        for head in range(BLOCK_HEADS):
            ordered[row : row + slot_rows, head * HD : (head + 1) * HD] = x_ref[source, head]

    @pl.when(pl.program_id(0) == 0)
    def _():
        own_block, own_row = place_ref[0], place_ref[1]
        order = [0, 2, 4, 6, 1, 3, 5, 7]
        for index, distance in enumerate(order):
            row = jnp.bitwise_xor(own_row, distance)
            for shift in range(1, cols):
                block = lax.rem(own_block + shift, cols)
                place(block * GRID_ROWS + row, (index * (cols - 1) + shift - 1) * slot_rows)
            place(own_block * GRID_ROWS + row, far + index * slot_rows)

    product = jnp.dot(ordered[...], w_ref[0], preferred_element_type=jnp.float32)
    product = product.astype(jnp.bfloat16)
    half = far // 2
    fk_ref[...] = product[:half].reshape(fk_ref.shape)
    fg_ref[...] = product[half:far].reshape(fg_ref.shape)
    nk_ref[...] = product[far : far + slot_rows * 4].reshape(nk_ref.shape)
    ng_ref[...] = product[far + slot_rows * 4 :].reshape(ng_ref.shape)


def project(x, place, out_weight, chunk, chunks):
    devices, _, slot_rows, _ = x.shape
    cols = devices // GRID_ROWS
    width = out_weight.shape[2] // chunks
    tile = min(TILE_N, width)
    steps = width // tile
    far = (4, (cols - 1) * slot_rows, width)
    near = (4, slot_rows, width)

    def spec(shape):
        return pl.BlockSpec(shape[:2] + (tile,), lambda i, place: (0, 0, i))

    return pl.pallas_call(
        project_kernel,
        grid_spec=pltpu.PrefetchScalarGridSpec(
            num_scalar_prefetch=1,
            grid=(steps,),
            in_specs=[
                pl.BlockSpec(x.shape, lambda i, place: (0, 0, 0, 0)),
                pl.BlockSpec(
                    (1, out_weight.shape[1], tile), lambda i, place: (0, 0, chunk * steps + i)
                ),
            ],
            out_specs=[spec(far), spec(far), spec(near), spec(near)],
            scratch_shapes=[pltpu.VMEM((devices * slot_rows, BLOCK_HEADS * HD), jnp.bfloat16)],
        ),
        out_shape=[jax.ShapeDtypeStruct(s, jnp.bfloat16) for s in (far, far, near, near)],
        compiler_params=pltpu.CompilerParams(vmem_limit_bytes=40 * MIB),
        name="project",
    )(place, x, out_weight)


def swap(value, distance):
    devices = lax.axis_size("tile")
    return lax.ppermute(value, "tile", [(i, i ^ distance) for i in range(devices)])


def add(kept, arrived):
    return kept.astype(jnp.float32) + arrived.astype(jnp.float32)


def reduce_square(give, keep):
    half = give.shape[2] // 2
    total = add(keep, swap(give, 1)).astype(jnp.bfloat16)
    left, right = total[..., :half], total[..., half:]
    left = left.reshape((2, 2) + left.shape[1:])
    right = right.reshape((2, 2) + right.shape[1:])
    left = add(left[:, 0], swap(left[:, 1], 2)).astype(jnp.bfloat16)
    right = add(right[0], swap(right[1], 4)).astype(jnp.bfloat16)
    left = add(left[0], swap(left[1], 4)).astype(jnp.bfloat16)
    right = add(right[0], swap(right[1], 2)).astype(jnp.bfloat16)
    return jnp.concatenate([left, right], axis=-1)


def per_device(queries, fresh_kv, cache, lengths, out_weight):
    slots = cache.shape[1]
    devices = lax.axis_size("tile")
    cols = devices // GRID_ROWS
    col_width = out_weight.shape[2]
    slot_rows = DECODE_STEPS * slots
    own = lax.axis_index("tile")
    own_block, own_row = own // GRID_ROWS, own % GRID_ROWS

    attended = attend(queries, fresh_kv, cache, lengths)
    blocks = attended.reshape(slots, KVH, DECODE_STEPS, GROUP // BLOCK_HEADS, BLOCK_HEADS, HD)
    blocks = jnp.transpose(blocks, (1, 3, 4, 2, 0, 5))
    blocks = blocks.reshape(GRID_ROWS, BLOCK_HEADS, slot_rows, HD)
    outgoing = jnp.broadcast_to(blocks[None], (cols,) + blocks.shape)
    outgoing = outgoing.reshape((devices,) + blocks.shape[1:])
    arrived = lax.all_to_all(outgoing, "tile", split_axis=0, concat_axis=0, tiled=True)

    place = jnp.stack([own_block, own_row]).astype(jnp.int32)
    pieces = []
    for chunk in range(CHUNKS):
        far_give, far_keep, near_give, near_keep = project(
            arrived, place, out_weight, chunk, CHUNKS
        )
        far = reduce_square(far_give, far_keep).reshape(cols - 1, slot_rows, -1)
        near = reduce_square(near_give, near_keep)
        back = [near]
        for shift in range(1, cols):
            targets = [
                (i, (i // GRID_ROWS + shift) % cols * GRID_ROWS + i % GRID_ROWS)
                for i in range(devices)
            ]
            back.append(lax.ppermute(far[shift - 1], "tile", targets))
        pieces.append(jnp.stack(back))
    stacked = jnp.concatenate(pieces, axis=-1)
    blocks = [
        lax.dynamic_index_in_dim(stacked, lax.rem(own_block - j + cols, cols), 0, False)
        for j in range(cols)
    ]
    return jnp.concatenate(blocks, axis=-1).reshape(DECODE_STEPS, slots, cols * col_width)


def solution(mesh):
    return jax.shard_map(
        per_device,
        mesh=mesh,
        in_specs=(
            P(None, ("groups", "tile"), None),
            P(None, None, ("groups", "tile"), None),
            P(None, ("groups", "tile"), None, None),
            P(("groups", "tile")),
            P("tile", None, None),
        ),
        out_specs=P(None, ("groups", "tile"), None),
        check_vma=False,
    )
```

time: 258 us -> 102 us (0.40)
  the two profiles are of different devices: /device:TPU:15 before, /device:TPU:0 now
where the time goes in v1:
time: 102 us; the launch traced here: 101 us
  waiting for transfers between devices  32.4 us (32%)
  starting transfers between devices  30 us (29%)
  Pallas kernels  29.3 us (29%)
  local copies, waits for them, and re-layouts  7.1 us (7%)
  other arithmetic  1.92 us (2%)
    ppermute x20, starting transfers between devices, swap(): lax.ppermute(value, 'tile', [(i, i ^ distance) for i in range(devices)])  19.6 us
    pallas_call x2, Pallas kernels, project(): pl.pallas_call(project_kernel, grid_spec=pltpu.PrefetchScalarGridSpec(num...  16.2 us
    all_to_all x1, waiting for transfers between devices, per_device(): lax.all_to_all(outgoing, 'tile', split_axis=0, concat_axis=0, tiled=True)  14.4 us
    pallas_call x1, Pallas kernels, attend(): pl.pallas_call(attention_kernel, out_shape=jax.ShapeDtypeStruct((slots, K...  13.1 us
    ppermute x20, waiting for transfers between devices, swap(): lax.ppermute(value, 'tile', [(i, i ^ distance) for i in range(devices)])  10.3 us
    ppermute x2, waiting for transfers between devices, per_device(): back.append(lax.ppermute(far[shift - 1], 'tile', targets))  7.68 us
    all_to_all x1, starting transfers between devices, per_device(): lax.all_to_all(outgoing, 'tile', split_axis=0, concat_axis=0, tiled=True)  7.38 us
    unnamed x6, local copies, waits for them, and re-layouts  4.79 us
  transfers between devices with their start and end apart: 23, of which 12 were waited for; matrix products, arithmetic and copies ran while one was open for 1% of the time, Pallas kernels for 8%

profile of v1, /device:TPU:0, one launch (start us, length us, event | category | flops | bytes accessed | tf_op | source)
XLA Modules:
  0.0 101.2 jit_solution(15443453967290426821)
XLA Ops:
  0.0 1.0 copy.13
  1.0 3.4 %copy-done = bf16[2,8,512,512]{3,2,1,0:T(8,128)(2,1)S(1)} copy-done((bf16[2,8,512,512]{3,2,1,0:T(8,128)(2,1)S(1)}, bf16[2,8,512,512]{3,2,1,0:T(8,128)(2,1)}, u32[]{:S(2)}) %copy-start) | copy-done | bytes 8388632
  5.8 13.1 %attention.1 = bf16[8,4,32,128]{3,2,1,0:T(8,128)(2,1)S(1)} custom-call(s32[8]{0:T(128)S(1)} %copy-done.2, bf16[8,4,32,128]{3,2,1,0:T(8,128)(2,1)S(1)} %bitcast.126, bf16[2,2,8,512]{3,2,1,0:T(8,128)(2,1)S(1)} %copy-done.1, bf16[2,8,512,512]{3,2,1,0:T(8,128)(2,1)S(1)} %copy-done), custom_call_target="tpu_custom_call" | custom-call | tf_op jit(solution)/shard_map/attention/pallas_call | solution.py:75
  20.0 7.4 %all-to-all-start = ((bf16[16,8,16,128]{3,2,1,0:T(8,128)(2,1)}), bf16[16,8,16,128]{3,2,1,0:T(8,128)(2,1)S(1)}, u32[]{:S(2)}, u32[]{:S(2)}) async-start(bf16[16,8,16,128]{3,2,1,0:T(8,128)(2,1)} %bitcast.8), calls=%async_computation | async-start | bytes 1048576 | tf_op jit(solution)/shard_map/all_to_all | solution.py:192
  27.4 14.4 %all-to-all-done.x_ref = bf16[16,8,16,128]{3,2,1,0:T(8,128)(2,1)S(1)} async-done(((bf16[16,8,16,128]{3,2,1,0:T(8,128)(2,1)}), bf16[16,8,16,128]{3,2,1,0:T(8,128)(2,1)S(1)}, u32[]{:S(2)}, u32[]{:S(2)}) %all-to-all-start) | async-done | bytes 524320 | tf_op jit(solution)/shard_map/all_to_all | solution.py:192
  41.8 8.1 %project.2 = (bf16[4,16,4096]{2,1,0:T(8,128)(2,1)S(1)}, bf16[4,16,4096]{2,1,0:T(8,128)(2,1)S(1)}, bf16[4,16,4096]{2,1,0:T(8,128)(2,1)S(1)}, bf16[4,16,4096]{2,1,0:T(8,128)(2,1)S(1)}) custom-call(s32[2]{0:T(128)S(1)} %pad_add_fusion.place_ref, bf16[16,8,16,128]{3,2,1,0:T(8,128)(2,1)S(1)} %all-to-all-done.x_ref, bf16[1,1024,8192]{2,1,0:T(8,128)(2,1)} %w_ref.3), custom_call_target="tpu_custom_call" | custom-call | tf_op jit(solution)/shard_map/project/pallas_call | solution.py:135
  50.5 8.1 %project.3 = (bf16[4,16,4096]{2,1,0:T(8,128)(2,1)S(1)}, bf16[4,16,4096]{2,1,0:T(8,128)(2,1)S(1)}, bf16[4,16,4096]{2,1,0:T(8,128)(2,1)S(1)}, bf16[4,16,4096]{2,1,0:T(8,128)(2,1)S(1)}) custom-call(s32[2]{0:T(128)S(1)} %pad_add_fusion.place_ref, bf16[16,8,16,128]{3,2,1,0:T(8,128)(2,1)S(1)} %all-to-all-done.x_ref, bf16[1,1024,8192]{2,1,0:T(8,128)(2,1)} %w_ref.3), custom_call_target="tpu_custom_call" | custom-call | tf_op jit(solution)/shard_map/project/pallas_call | solution.py:135
  59.6 1.0 %collective-permute-done.11 = bf16[4,16,4096]{2,1,0:T(8,128)(2,1)S(1)} collective-permute-done((bf16[4,16,4096]{2,1,0:T(8,128)(2,1)S(1)}, bf16[4,16,4096]{2,1,0:T(8,128)(2,1)S(1)}, u32[]{:S(2)}, u32[]{:S(2)}) %collective-permute-start.11) | collective-permute-done | bytes 524320 | tf_op jit(solution)/shard_map/ppermute | solution.py:157
  62.4 1.6 %collective-permute-start.3 = (bf16[2,16,2048]{2,1,0:T(8,128)(2,1)S(1)}, bf16[2,16,2048]{2,1,0:T(8,128)(2,1)S(1)}, u32[]{:S(2)}, u32[]{:S(2)}) collective-permute-start(bf16[2,16,2048]{2,1,0:T(8,128)(2,1)S(1)} %slice.170), channel_id=1, source_target_pairs={{0,4},{1,5},{2,6},{3,7},{4,0},{5,1},{6,2},{7,3},{8,12},{9,13},{10,... | collective-permute-start | bytes 393224 | tf_op jit(solution)/shard_map/ppermute | solution.py:157
  64.0 1.1 %collective-permute-start.6 = (bf16[2,16,2048]{2,1,0:T(8,128)(2,1)S(1)}, bf16[2,16,2048]{2,1,0:T(8,128)(2,1)S(1)}, u32[]{:S(2)}, u32[]{:S(2)}) collective-permute-start(bf16[2,16,2048]{2,1,0:T(8,128)(2,1)S(1)} %slice_bitcast_fusion.4), channel_id=1, source_target_pairs={{0,2},{1,3},{2,0},{3,1},{4,6},{5,7},{6,4},{7,5},{8,10},{9,11},{10,... | collective-permute-start | bytes 393224 | tf_op jit(solution)/shard_map/ppermute | solution.py:157
  66.6 1.2 %collective-permute-done.1 = bf16[2,16,2048]{2,1,0:T(8,128)(2,1)S(1)} collective-permute-done((bf16[2,16,2048]{2,1,0:T(8,128)(2,1)S(1)}, bf16[2,16,2048]{2,1,0:T(8,128)(2,1)S(1)}, u32[]{:S(2)}, u32[]{:S(2)}) %collective-permute-start.1) | collective-permute-done | bytes 131104 | tf_op jit(solution)/shard_map/ppermute | solution.py:157
  67.9 1.4 %collective-permute-start.14 = (bf16[2,16,2048]{2,1,0:T(8,128)(2,1)S(1)}, bf16[2,16,2048]{2,1,0:T(8,128)(2,1)S(1)}, u32[]{:S(2)}, u32[]{:S(2)}) collective-permute-start(bf16[2,16,2048]{2,1,0:T(8,128)(2,1)S(1)} %slice.188), channel_id=1, source_target_pairs={{0,4},{1,5},{2,6},{3,7},{4,0},{5,1},{6,2},{7,3},{8,12},{9,13},{10,... | collective-permute-start | bytes 393224 | tf_op jit(solution)/shard_map/ppermute | solution.py:157
  69.4 1.0 %collective-permute-start.17 = (bf16[2,16,2048]{2,1,0:T(8,128)(2,1)S(1)}, bf16[2,16,2048]{2,1,0:T(8,128)(2,1)S(1)}, u32[]{:S(2)}, u32[]{:S(2)}) collective-permute-start(bf16[2,16,2048]{2,1,0:T(8,128)(2,1)S(1)} %slice_bitcast_fusion), channel_id=1, source_target_pairs={{0,2},{1,3},{2,0},{3,1},{4,6},{5,7},{6,4},{7,5},{8,10},{9,11},{10,... | collective-permute-start | bytes 393224 | tf_op jit(solution)/shard_map/ppermute | solution.py:157
  70.7 1.4 %collective-permute-start.19 = (bf16[2,16,2048]{2,1,0:T(8,128)(2,1)S(1)}, bf16[2,16,2048]{2,1,0:T(8,128)(2,1)S(1)}, u32[]{:S(2)}, u32[]{:S(2)}) collective-permute-start(bf16[2,16,2048]{2,1,0:T(8,128)(2,1)S(1)} %slice.197), channel_id=1, source_target_pairs={{0,4},{1,5},{2,6},{3,7},{4,0},{5,1},{6,2},{7,3},{8,12},{9,13},{10,... | collective-permute-start | bytes 393224 | tf_op jit(solution)/shard_map/ppermute | solution.py:157
  72.2 1.0 collective-permute-start.2
  74.4 1.6 %collective-permute-start.7 = (bf16[16,2048]{1,0:T(8,128)(2,1)S(1)}, bf16[16,2048]{1,0:T(8,128)(2,1)S(1)}, u32[]{:S(2)}, u32[]{:S(2)}) collective-permute-start(bf16[16,2048]{1,0:T(8,128)(2,1)S(1)} %slice_bitcast_fusion.18), channel_id=1, source_target_pairs={{0,4},{1,5},{2,6},{3,7},{4,0},{5,1},{6,2},{7,3},{8,12},{9,13},{10,... | collective-permute-start | bytes 196616 | tf_op jit(solution)/shard_map/ppermute | solution.py:157
  77.3 1.6 %collective-permute-start.13 = (bf16[16,2048]{1,0:T(8,128)(2,1)S(1)}, bf16[16,2048]{1,0:T(8,128)(2,1)S(1)}, u32[]{:S(2)}, u32[]{:S(2)}) collective-permute-start(bf16[16,2048]{1,0:T(8,128)(2,1)S(1)} %slice_bitcast_fusion.14), channel_id=1, source_target_pairs={{0,4},{1,5},{2,6},{3,7},{4,0},{5,1},{6,2},{7,3},{8,12},{9,13},{10,... | collective-permute-start | bytes 196616 | tf_op jit(solution)/shard_map/ppermute | solution.py:157
  79.6 1.1 %collective-permute-start.15 = (bf16[16,2048]{1,0:T(8,128)(2,1)S(1)}, bf16[16,2048]{1,0:T(8,128)(2,1)S(1)}, u32[]{:S(2)}, u32[]{:S(2)}) collective-permute-start(bf16[16,2048]{1,0:T(8,128)(2,1)S(1)} %slice_bitcast_fusion.12), channel_id=1, source_target_pairs={{0,2},{1,3},{2,0},{3,1},{4,6},{5,7},{6,4},{7,5},{8,10},{9,11},{10,... | collective-permute-start | bytes 196616 | tf_op jit(solution)/shard_map/ppermute | solution.py:157
  80.7 1.6 %collective-permute-start.18 = (bf16[16,2048]{1,0:T(8,128)(2,1)S(1)}, bf16[16,2048]{1,0:T(8,128)(2,1)S(1)}, u32[]{:S(2)}, u32[]{:S(2)}) collective-permute-start(bf16[16,2048]{1,0:T(8,128)(2,1)S(1)} %slice_bitcast_fusion.10), channel_id=1, source_target_pairs={{0,4},{1,5},{2,6},{3,7},{4,0},{5,1},{6,2},{7,3},{8,12},{9,13},{10,... | collective-permute-start | bytes 196616 | tf_op jit(solution)/shard_map/ppermute | solution.py:157
  82.3 2.8 %collective-permute-done.18 = bf16[16,2048]{1,0:T(8,128)(2,1)S(1)} collective-permute-done((bf16[16,2048]{1,0:T(8,128)(2,1)S(1)}, bf16[16,2048]{1,0:T(8,128)(2,1)S(1)}, u32[]{:S(2)}, u32[]{:S(2)}) %collective-permute-start.18) | collective-permute-done | bytes 65568 | tf_op jit(solution)/shard_map/ppermute | solution.py:157
  86.0 3.3 %collective-permute-done.20 = bf16[16,2048]{1,0:T(8,128)(2,1)S(1)} collective-permute-done((bf16[16,2048]{1,0:T(8,128)(2,1)S(1)}, bf16[16,2048]{1,0:T(8,128)(2,1)S(1)}, u32[]{:S(2)}, u32[]{:S(2)}) %collective-permute-start.20) | collective-permute-done | bytes 65568 | tf_op jit(solution)/shard_map/ppermute | solution.py:157
  89.3 2.6 %collective-permute-start.10 = (bf16[16,4096]{1,0:T(8,128)(2,1)S(1)}, bf16[16,4096]{1,0:T(8,128)(2,1)S(1)}, u32[]{:S(2)}, u32[]{:S(2)}) collective-permute-start(bf16[16,4096]{1,0:T(8,128)(2,1)S(1)} %pad_maximum_fusion.1), channel_id=1, source_target_pairs={{0,8},{1,9},{2,10},{3,11},{4,12},{5,13},{6,14},{7,15},{8,0},{9,1},... | collective-permute-start | bytes 393224 | tf_op jit(solution)/shard_map/ppermute | solution.py:208
  92.6 6.3 %collective-permute-done.10 = bf16[16,4096]{1,0:T(8,128)(2,1)S(1)} collective-permute-done((bf16[16,4096]{1,0:T(8,128)(2,1)S(1)}, bf16[16,4096]{1,0:T(8,128)(2,1)S(1)}, u32[]{:S(2)}, u32[]{:S(2)}) %collective-permute-start.10) | collective-permute-done | bytes 131104 | tf_op jit(solution)/shard_map/ppermute | solution.py:208
  98.8 1.4 %collective-permute-done.21 = bf16[16,4096]{1,0:T(8,128)(2,1)S(1)} collective-permute-done((bf16[16,4096]{1,0:T(8,128)(2,1)S(1)}, bf16[16,4096]{1,0:T(8,128)(2,1)S(1)}, u32[]{:S(2)}, u32[]{:S(2)}) %collective-permute-start.21) | collective-permute-done | bytes 131104 | tf_op jit(solution)/shard_map/ppermute | solution.py:208
  (82 shorter events, 13.3 us)
Async XLA Ops:
  1.0 3.4 %copy-start = (bf16[2,8,512,512]{3,2,1,0:T(8,128)(2,1)S(1)}, bf16[2,8,512,512]{3,2,1,0:T(8,128)(2,1)}, u32[]{:S(2)}) copy-start(bf16[2,8,512,512]{3,2,1,0:T(8,128)(2,1)} %cache_ref.1) | copy-start | bytes 25165828
  20.0 21.9 %all-to-all-start = ((bf16[16,8,16,128]{3,2,1,0:T(8,128)(2,1)}), bf16[16,8,16,128]{3,2,1,0:T(8,128)(2,1)S(1)}, u32[]{:S(2)}, u32[]{:S(2)}) async-start(bf16[16,8,16,128]{3,2,1,0:T(8,128)(2,1)} %bitcast.8), calls=%async_computation | async-start | bytes 1048576 | tf_op jit(solution)/shard_map/all_to_all | solution.py:192
  49.9 9.3 %collective-permute-start = (bf16[4,16,4096]{2,1,0:T(8,128)(2,1)S(1)}, bf16[4,16,4096]{2,1,0:T(8,128)(2,1)S(1)}, u32[]{:S(2)}, u32[]{:S(2)}) collective-permute-start(bf16[4,16,4096]{2,1,0:T(8,128)(2,1)S(1)} %get-tuple-element.14), channel_id=1, source_target_pairs={{0,1},{1,0},{2,3},{3,2},{4,5},{5,4},{6,7},{7,6},{8,9},{9,8},{10,11... | collective-permute-start | bytes 1572872 | tf_op jit(solution)/shard_map/ppermute | solution.py:157
  50.0 9.4 %collective-permute-start.5 = (bf16[4,16,4096]{2,1,0:T(8,128)(2,1)S(1)}, bf16[4,16,4096]{2,1,0:T(8,128)(2,1)S(1)}, u32[]{:S(2)}, u32[]{:S(2)}) collective-permute-start(bf16[4,16,4096]{2,1,0:T(8,128)(2,1)S(1)} %get-tuple-element.16), channel_id=1, source_target_pairs={{0,1},{1,0},{2,3},{3,2},{4,5},{5,4},{6,7},{7,6},{8,9},{9,8},{10,11... | collective-permute-start | bytes 1572872 | tf_op jit(solution)/shard_map/ppermute | solution.py:157
  58.6 2.0 %collective-permute-start.11 = (bf16[4,16,4096]{2,1,0:T(8,128)(2,1)S(1)}, bf16[4,16,4096]{2,1,0:T(8,128)(2,1)S(1)}, u32[]{:S(2)}, u32[]{:S(2)}) collective-permute-start(bf16[4,16,4096]{2,1,0:T(8,128)(2,1)S(1)} %get-tuple-element.18), channel_id=1, source_target_pairs={{0,1},{1,0},{2,3},{3,2},{4,5},{5,4},{6,7},{7,6},{8,9},{9,8},{10,11... | collective-permute-start | bytes 1572872 | tf_op jit(solution)/shard_map/ppermute | solution.py:157
  58.8 2.6 %collective-permute-start.16 = (bf16[4,16,4096]{2,1,0:T(8,128)(2,1)S(1)}, bf16[4,16,4096]{2,1,0:T(8,128)(2,1)S(1)}, u32[]{:S(2)}, u32[]{:S(2)}) collective-permute-start(bf16[4,16,4096]{2,1,0:T(8,128)(2,1)S(1)} %get-tuple-element.20), channel_id=1, source_target_pairs={{0,1},{1,0},{2,3},{3,2},{4,5},{5,4},{6,7},{7,6},{8,9},{9,8},{10,11... | collective-permute-start | bytes 1572872 | tf_op jit(solution)/shard_map/ppermute | solution.py:157
  61.5 6.3 %collective-permute-start.1 = (bf16[2,16,2048]{2,1,0:T(8,128)(2,1)S(1)}, bf16[2,16,2048]{2,1,0:T(8,128)(2,1)S(1)}, u32[]{:S(2)}, u32[]{:S(2)}) collective-permute-start(bf16[2,16,2048]{2,1,0:T(8,128)(2,1)S(1)} %slice_bitcast_fusion.6), channel_id=1, source_target_pairs={{0,2},{1,3},{2,0},{3,1},{4,6},{5,7},{6,4},{7,5},{8,10},{9,11},{10,... | collective-permute-start | bytes 393224 | tf_op jit(solution)/shard_map/ppermute | solution.py:157
  62.4 7.0 %collective-permute-start.3 = (bf16[2,16,2048]{2,1,0:T(8,128)(2,1)S(1)}, bf16[2,16,2048]{2,1,0:T(8,128)(2,1)S(1)}, u32[]{:S(2)}, u32[]{:S(2)}) collective-permute-start(bf16[2,16,2048]{2,1,0:T(8,128)(2,1)S(1)} %slice.170), channel_id=1, source_target_pairs={{0,4},{1,5},{2,6},{3,7},{4,0},{5,1},{6,2},{7,3},{8,12},{9,13},{10,... | collective-permute-start | bytes 393224 | tf_op jit(solution)/shard_map/ppermute | solution.py:157
  64.0 6.7 %collective-permute-start.6 = (bf16[2,16,2048]{2,1,0:T(8,128)(2,1)S(1)}, bf16[2,16,2048]{2,1,0:T(8,128)(2,1)S(1)}, u32[]{:S(2)}, u32[]{:S(2)}) collective-permute-start(bf16[2,16,2048]{2,1,0:T(8,128)(2,1)S(1)} %slice_bitcast_fusion.4), channel_id=1, source_target_pairs={{0,2},{1,3},{2,0},{3,1},{4,6},{5,7},{6,4},{7,5},{8,10},{9,11},{10,... | collective-permute-start | bytes 393224 | tf_op jit(solution)/shard_map/ppermute | solution.py:157
  65.1 7.1 %collective-permute-start.8 = (bf16[2,16,2048]{2,1,0:T(8,128)(2,1)S(1)}, bf16[2,16,2048]{2,1,0:T(8,128)(2,1)S(1)}, u32[]{:S(2)}, u32[]{:S(2)}) collective-permute-start(bf16[2,16,2048]{2,1,0:T(8,128)(2,1)S(1)} %slice.179), channel_id=1, source_target_pairs={{0,4},{1,5},{2,6},{3,7},{4,0},{5,1},{6,2},{7,3},{8,12},{9,13},{10,... | collective-permute-start | bytes 393224 | tf_op jit(solution)/shard_map/ppermute | solution.py:157
  65.8 7.7 %collective-permute-start.12 = (bf16[2,16,2048]{2,1,0:T(8,128)(2,1)S(1)}, bf16[2,16,2048]{2,1,0:T(8,128)(2,1)S(1)}, u32[]{:S(2)}, u32[]{:S(2)}) collective-permute-start(bf16[2,16,2048]{2,1,0:T(8,128)(2,1)S(1)} %slice_bitcast_fusion.2), channel_id=1, source_target_pairs={{0,2},{1,3},{2,0},{3,1},{4,6},{5,7},{6,4},{7,5},{8,10},{9,11},{10,... | collective-permute-start | bytes 393224 | tf_op jit(solution)/shard_map/ppermute | solution.py:157
  67.9 6.5 %collective-permute-start.14 = (bf16[2,16,2048]{2,1,0:T(8,128)(2,1)S(1)}, bf16[2,16,2048]{2,1,0:T(8,128)(2,1)S(1)}, u32[]{:S(2)}, u32[]{:S(2)}) collective-permute-start(bf16[2,16,2048]{2,1,0:T(8,128)(2,1)S(1)} %slice.188), channel_id=1, source_target_pairs={{0,4},{1,5},{2,6},{3,7},{4,0},{5,1},{6,2},{7,3},{8,12},{9,13},{10,... | collective-permute-start | bytes 393224 | tf_op jit(solution)/shard_map/ppermute | solution.py:157
  69.4 6.9 %collective-permute-start.17 = (bf16[2,16,2048]{2,1,0:T(8,128)(2,1)S(1)}, bf16[2,16,2048]{2,1,0:T(8,128)(2,1)S(1)}, u32[]{:S(2)}, u32[]{:S(2)}) collective-permute-start(bf16[2,16,2048]{2,1,0:T(8,128)(2,1)S(1)} %slice_bitcast_fusion), channel_id=1, source_target_pairs={{0,2},{1,3},{2,0},{3,1},{4,6},{5,7},{6,4},{7,5},{8,10},{9,11},{10,... | collective-permute-start | bytes 393224 | tf_op jit(solution)/shard_map/ppermute | solution.py:157
  70.7 6.6 %collective-permute-start.19 = (bf16[2,16,2048]{2,1,0:T(8,128)(2,1)S(1)}, bf16[2,16,2048]{2,1,0:T(8,128)(2,1)S(1)}, u32[]{:S(2)}, u32[]{:S(2)}) collective-permute-start(bf16[2,16,2048]{2,1,0:T(8,128)(2,1)S(1)} %slice.197), channel_id=1, source_target_pairs={{0,4},{1,5},{2,6},{3,7},{4,0},{5,1},{6,2},{7,3},{8,12},{9,13},{10,... | collective-permute-start | bytes 393224 | tf_op jit(solution)/shard_map/ppermute | solution.py:157
  72.2 19.8 %collective-permute-start.2 = (bf16[16,2048]{1,0:T(8,128)(2,1)S(1)}, bf16[16,2048]{1,0:T(8,128)(2,1)S(1)}, u32[]{:S(2)}, u32[]{:S(2)}) collective-permute-start(bf16[16,2048]{1,0:T(8,128)(2,1)S(1)} %slice_bitcast_fusion.22), channel_id=1, source_target_pairs={{0,4},{1,5},{2,6},{3,7},{4,0},{5,1},{6,2},{7,3},{8,12},{9,13},{10,... | collective-permute-start | bytes 196616 | tf_op jit(solution)/shard_map/ppermute | solution.py:157
  73.5 18.9 %collective-permute-start.4 = (bf16[16,2048]{1,0:T(8,128)(2,1)S(1)}, bf16[16,2048]{1,0:T(8,128)(2,1)S(1)}, u32[]{:S(2)}, u32[]{:S(2)}) collective-permute-start(bf16[16,2048]{1,0:T(8,128)(2,1)S(1)} %slice_bitcast_fusion.20), channel_id=1, source_target_pairs={{0,2},{1,3},{2,0},{3,1},{4,6},{5,7},{6,4},{7,5},{8,10},{9,11},{10,... | collective-permute-start | bytes 196616 | tf_op jit(solution)/shard_map/ppermute | solution.py:157
  74.4 5.2 %collective-permute-start.7 = (bf16[16,2048]{1,0:T(8,128)(2,1)S(1)}, bf16[16,2048]{1,0:T(8,128)(2,1)S(1)}, u32[]{:S(2)}, u32[]{:S(2)}) collective-permute-start(bf16[16,2048]{1,0:T(8,128)(2,1)S(1)} %slice_bitcast_fusion.18), channel_id=1, source_target_pairs={{0,4},{1,5},{2,6},{3,7},{4,0},{5,1},{6,2},{7,3},{8,12},{9,13},{10,... | collective-permute-start | bytes 196616 | tf_op jit(solution)/shard_map/ppermute | solution.py:157
  76.3 4.5 %collective-permute-start.9 = (bf16[16,2048]{1,0:T(8,128)(2,1)S(1)}, bf16[16,2048]{1,0:T(8,128)(2,1)S(1)}, u32[]{:S(2)}, u32[]{:S(2)}) collective-permute-start(bf16[16,2048]{1,0:T(8,128)(2,1)S(1)} %slice_bitcast_fusion.16), channel_id=1, source_target_pairs={{0,2},{1,3},{2,0},{3,1},{4,6},{5,7},{6,4},{7,5},{8,10},{9,11},{10,... | collective-permute-start | bytes 196616 | tf_op jit(solution)/shard_map/ppermute | solution.py:157
  77.3 15.2 %collective-permute-start.13 = (bf16[16,2048]{1,0:T(8,128)(2,1)S(1)}, bf16[16,2048]{1,0:T(8,128)(2,1)S(1)}, u32[]{:S(2)}, u32[]{:S(2)}) collective-permute-start(bf16[16,2048]{1,0:T(8,128)(2,1)S(1)} %slice_bitcast_fusion.14), channel_id=1, source_target_pairs={{0,4},{1,5},{2,6},{3,7},{4,0},{5,1},{6,2},{7,3},{8,12},{9,13},{10,... | collective-permute-start | bytes 196616 | tf_op jit(solution)/shard_map/ppermute | solution.py:157
  79.6 12.9 %collective-permute-start.15 = (bf16[16,2048]{1,0:T(8,128)(2,1)S(1)}, bf16[16,2048]{1,0:T(8,128)(2,1)S(1)}, u32[]{:S(2)}, u32[]{:S(2)}) collective-permute-start(bf16[16,2048]{1,0:T(8,128)(2,1)S(1)} %slice_bitcast_fusion.12), channel_id=1, source_target_pairs={{0,2},{1,3},{2,0},{3,1},{4,6},{5,7},{6,4},{7,5},{8,10},{9,11},{10,... | collective-permute-start | bytes 196616 | tf_op jit(solution)/shard_map/ppermute | solution.py:157
  80.7 4.3 %collective-permute-start.18 = (bf16[16,2048]{1,0:T(8,128)(2,1)S(1)}, bf16[16,2048]{1,0:T(8,128)(2,1)S(1)}, u32[]{:S(2)}, u32[]{:S(2)}) collective-permute-start(bf16[16,2048]{1,0:T(8,128)(2,1)S(1)} %slice_bitcast_fusion.10), channel_id=1, source_target_pairs={{0,4},{1,5},{2,6},{3,7},{4,0},{5,1},{6,2},{7,3},{8,12},{9,13},{10,... | collective-permute-start | bytes 196616 | tf_op jit(solution)/shard_map/ppermute | solution.py:157
  85.1 4.3 %collective-permute-start.20 = (bf16[16,2048]{1,0:T(8,128)(2,1)S(1)}, bf16[16,2048]{1,0:T(8,128)(2,1)S(1)}, u32[]{:S(2)}, u32[]{:S(2)}) collective-permute-start(bf16[16,2048]{1,0:T(8,128)(2,1)S(1)} %slice_bitcast_fusion.8), channel_id=1, source_target_pairs={{0,2},{1,3},{2,0},{3,1},{4,6},{5,7},{6,4},{7,5},{8,10},{9,11},{10,... | collective-permute-start | bytes 196616 | tf_op jit(solution)/shard_map/ppermute | solution.py:157
  89.3 9.5 %collective-permute-start.10 = (bf16[16,4096]{1,0:T(8,128)(2,1)S(1)}, bf16[16,4096]{1,0:T(8,128)(2,1)S(1)}, u32[]{:S(2)}, u32[]{:S(2)}) collective-permute-start(bf16[16,4096]{1,0:T(8,128)(2,1)S(1)} %pad_maximum_fusion.1), channel_id=1, source_target_pairs={{0,8},{1,9},{2,10},{3,11},{4,12},{5,13},{6,14},{7,15},{8,0},{9,1},... | collective-permute-start | bytes 393224 | tf_op jit(solution)/shard_map/ppermute | solution.py:208
  91.9 8.3 %collective-permute-start.21 = (bf16[16,4096]{1,0:T(8,128)(2,1)S(1)}, bf16[16,4096]{1,0:T(8,128)(2,1)S(1)}, u32[]{:S(2)}, u32[]{:S(2)}) collective-permute-start(bf16[16,4096]{1,0:T(8,128)(2,1)S(1)} %pad_maximum_fusion.2), channel_id=1, source_target_pairs={{0,8},{1,9},{2,10},{3,11},{4,12},{5,13},{6,14},{7,15},{8,0},{9,1},... | collective-permute-start | bytes 393224 | tf_op jit(solution)/shard_map/ppermute | solution.py:208
  (2 other events, 1.4 us)

commit v2 on v0

v2 whole, which is shorter than its diff:
```python
import functools
import math

import jax
import jax.numpy as jnp
from jax import lax
from jax.experimental import pallas as pl
from jax.experimental.pallas import tpu as pltpu
from jax.sharding import PartitionSpec as P

QH = 64
KVH = 4
HD = 128
DECODE_STEPS = 2
GRID_ROWS = 8
GROUP = QH // KVH
BLOCK_HEADS = QH // GRID_ROWS
CHUNKS = 2
TILE_N = 1024
PAGE = 128
MIB = 1 << 20


def attention_kernel(lengths_ref, query_ref, fresh_ref, cache_ref, out_ref, cached, sems):
    slots, capacity, width = cached.shape[1:]
    factor = 1.0 / math.sqrt(HD)
    rows = KVH * DECODE_STEPS * GROUP
    head_rows = rows // KVH
    pages = capacity // PAGE

    def copies(slot, act):
        used = (lengths_ref[slot] + DECODE_STEPS + PAGE - 1) // PAGE
        used = jnp.where(used >= 3, pages, used)
        for page in range(pages):

            @pl.when(page < used)
            def _(page=page):
                span = pl.ds(page * PAGE, PAGE)
                for which in range(2):
                    act(
                        pltpu.make_async_copy(
                            cache_ref.at[which, slot, span],
                            cached.at[which, slot, span],
                            sems.at[which, slot, page],
                        )
                    )

        return used

    for slot in range(slots):
        copies(slot, lambda copy: copy.start())
    own = (
        lax.broadcasted_iota(jnp.int32, (rows, width), 0) // head_rows
        == lax.broadcasted_iota(jnp.int32, (rows, width), 1) // HD
    )
    window_row = lax.broadcasted_iota(jnp.int32, (32, width), 0)

    def mix(slot, count):
        position = lax.broadcasted_iota(jnp.int32, (rows, count), 1)
        step = lax.broadcasted_iota(jnp.int32, (rows, count), 0) // GROUP % DECODE_STEPS
        query = jnp.concatenate([query_ref[slot]] * KVH, axis=1)
        query = jnp.where(own, query, jnp.zeros((), query.dtype))
        scores = lax.dot_general(
            query,
            cached[0, slot, :count, :],
            (((1,), (1,)), ((), ())),
            preferred_element_type=jnp.float32,
        )
        visible = position < lengths_ref[slot] + 1 + step
        scores = jnp.where(visible, scores * factor, -jnp.inf)
        weights = jnp.exp(scores - scores.max(-1, keepdims=True))
        weights = weights * (1.0 / weights.sum(-1, keepdims=True))
        mixed = jnp.dot(
            weights.astype(jnp.bfloat16),
            cached[1, slot, :count, :],
            preferred_element_type=jnp.float32,
        )
        for head in range(KVH):
            own_rows = slice(head * head_rows, (head + 1) * head_rows)
            own_lanes = slice(head * HD, (head + 1) * HD)
            out_ref[slot, own_rows, :] = mixed[own_rows, own_lanes].astype(jnp.bfloat16)

    for slot in range(slots):
        used = copies(slot, lambda copy: copy.wait())
        length = lengths_ref[slot]
        base = pl.multiple_of(jnp.minimum((length // 16) * 16, capacity - 32), 16)
        for which in range(2):
            window = cached[which, slot, pl.ds(base, 32), :].astype(jnp.float32)
            for t in range(DECODE_STEPS):
                fresh = fresh_ref[t, which].astype(jnp.float32)[slot : slot + 1]
                window = jnp.where(window_row + base == length + t, fresh, window)
            cached[which, slot, pl.ds(base, 32), :] = window.astype(jnp.bfloat16)
        for count in (1, 2, pages):
            pl.when(used == count)(functools.partial(mix, slot, count * PAGE))


def attend(queries, fresh_kv, cache, lengths):
    slots, capacity, width = cache.shape[1:]
    rows = KVH * DECODE_STEPS * GROUP
    query = queries.reshape(DECODE_STEPS, slots, KVH, GROUP, HD)
    query = jnp.transpose(query, (1, 2, 0, 3, 4)).reshape(slots, rows, HD)
    vmem = pl.BlockSpec(memory_space=pltpu.VMEM)
    return pl.pallas_call(
        attention_kernel,
        out_shape=jax.ShapeDtypeStruct((slots, rows, HD), jnp.bfloat16),
        in_specs=[
            pl.BlockSpec(memory_space=pltpu.SMEM),
            vmem,
            vmem,
            pl.BlockSpec(memory_space=pl.ANY),
        ],
        out_specs=vmem,
        scratch_shapes=[
            pltpu.VMEM((2, slots, capacity, width), jnp.bfloat16),
            pltpu.SemaphoreType.DMA((2, slots, capacity // PAGE)),
        ],
        compiler_params=pltpu.CompilerParams(vmem_limit_bytes=53 * MIB),
        name="attention",
    )(lengths, query, fresh_kv, cache)


def load_kernel(source_ref, *refs):
    out_refs, sems = refs[:-1], refs[-1]
    width = out_refs[0].shape[1]
    rows = source_ref.shape[1] // sems.shape[1]
    copies = [
        pltpu.make_async_copy(
            source_ref.at[0, pl.ds(i * rows, rows), pl.ds(chunk * width, width)],
            out_ref.at[pl.ds(i * rows, rows)],
            sems.at[chunk, i],
        )
        for chunk, out_ref in enumerate(out_refs)
        for i in range(sems.shape[1])
    ]
    for copy in copies:
        copy.start()
    for copy in copies:
        copy.wait()


def load(weight, chunks):
    _, depth, width = weight.shape
    shape = jax.ShapeDtypeStruct((depth, width // chunks), weight.dtype)
    return pl.pallas_call(
        load_kernel,
        in_specs=[pl.BlockSpec(memory_space=pl.ANY)],
        out_specs=[pl.BlockSpec(memory_space=pl.ANY)] * chunks,
        out_shape=[shape] * chunks,
        scratch_shapes=[pltpu.SemaphoreType.DMA((chunks, 4))],
        compiler_params=pltpu.CompilerParams(vmem_limit_bytes=36 * MIB),
        cost_estimate=pl.CostEstimate(flops=0, bytes_accessed=4 * weight.size, transcendentals=0),
        name="load",
    )(weight)


def project_kernel(*refs):
    x_refs, w_ref = refs[:8], refs[8]
    out_refs, ordered = refs[9:13], refs[13]
    depth, width = w_ref.shape
    tile = min(TILE_N, width)
    row = 0
    for group in (x_refs[:4], x_refs[4:]):
        shifts, _, _, slot_rows, _ = group[0].shape
        for core in range(2):
            for x_ref in group:
                for shift in range(shifts):
                    for head in range(BLOCK_HEADS):
                        ordered[row : row + slot_rows, head * HD : (head + 1) * HD] = x_ref[
                            shift, core, head
                        ]
                    row += slot_rows
    for start in range(0, width, tile):
        lanes = slice(start, start + tile)
        product = jnp.dot(ordered[...], w_ref[:, lanes], preferred_element_type=jnp.float32)
        product = product.astype(jnp.bfloat16)
        row = 0
        for out_ref in out_refs:
            count = out_ref.shape[0] * out_ref.shape[1]
            out_ref[:, :, lanes] = product[row : row + count].reshape(out_ref.shape[:2] + (tile,))
            row += count


def project(far, near, weight):
    shifts, _, _, slot_rows, _ = far[0].shape
    depth, width = weight.shape
    rows = 8 * (shifts + 1) * slot_rows
    far_shape = jax.ShapeDtypeStruct((4, shifts * slot_rows, width), jnp.bfloat16)
    near_shape = jax.ShapeDtypeStruct((4, slot_rows, width), jnp.bfloat16)
    vmem = pl.BlockSpec(memory_space=pltpu.VMEM)
    return pl.pallas_call(
        project_kernel,
        in_specs=[vmem] * 9,
        out_specs=[vmem] * 4,
        scratch_shapes=[pltpu.VMEM((rows, depth), jnp.bfloat16)],
        out_shape=[far_shape] * 2 + [near_shape] * 2,
        compiler_params=pltpu.CompilerParams(vmem_limit_bytes=8 * MIB),
        cost_estimate=pl.CostEstimate(
            flops=2 * rows * depth * width,
            bytes_accessed=2 * depth * width,
            transcendentals=0,
        ),
        name="project",
    )(*far, *near, weight)


def swap(value, distance):
    devices = lax.axis_size("tile")
    return lax.ppermute(value, "tile", [(i, i ^ distance) for i in range(devices)])


def widen(value):
    return value.astype(jnp.float32)


def direct(total):
    sent = total.astype(jnp.bfloat16)
    arrived = [swap(sent[i], 2 * i) for i in range(1, 4)]
    return total[0] + sum(widen(value) for value in arrived)


def per_device(queries, fresh_kv, cache, lengths, out_weight):
    slots = cache.shape[1]
    devices = lax.axis_size("tile")
    cols = devices // GRID_ROWS
    col_width = out_weight.shape[2]
    slot_rows = DECODE_STEPS * slots
    own = lax.axis_index("tile")
    own_block = own // GRID_ROWS
    own_square = own // 2 % 4
    own_core = own % 2

    def send(value, shift, distance):
        def target(i):
            block, row = i // GRID_ROWS, i % GRID_ROWS
            return (block + shift) % cols * GRID_ROWS + (row ^ distance)

        return lax.ppermute(value, "tile", [(i, target(i)) for i in range(devices)])

    attended = attend(queries, fresh_kv, cache, lengths)
    blocks = attended.reshape(slots, KVH, DECODE_STEPS, GROUP // BLOCK_HEADS, BLOCK_HEADS, HD)
    blocks = jnp.transpose(blocks, (3, 1, 4, 2, 0, 5))
    blocks = blocks.reshape(2, 4, BLOCK_HEADS, slot_rows, HD)
    kept = jnp.where(own_core == 0, blocks[0], blocks[1])
    given = jnp.where(own_core == 0, blocks[1], blocks[0])
    cat = jnp.stack([kept, swap(given, 1)], axis=1)
    cat, weight = lax.optimization_barrier((cat, out_weight))
    cat = [
        lax.dynamic_index_in_dim(cat, jnp.bitwise_xor(own_square, distance), 0, False)
        for distance in range(4)
    ]
    far = [
        jnp.stack([send(cat[i], shift, 2 * i) for shift in range(1, cols)]) for i in range(4)
    ]
    near = [(send(cat[i], 0, 2 * i) if i else cat[0])[None] for i in range(4)]
    weights = load(weight, CHUNKS)
    partial = [project(far, near, weight) for weight in weights]
    near_total = jnp.concatenate(
        [widen(keep) + widen(swap(give, 1)) for _, _, keep, give in partial], axis=-1
    )
    backs = []
    for chunk, (keep, give, _, _) in enumerate(partial):
        sums = direct(widen(keep) + widen(swap(give, 1))).astype(jnp.bfloat16)
        if chunk == 0:
            sums, near_total = lax.optimization_barrier((sums, near_total))
        sums = sums.reshape(cols - 1, slot_rows, -1)
        backs.append(jnp.stack([send(sums[s - 1], cols - s, 0) for s in range(1, cols)]))
    near = direct(near_total).astype(jnp.bfloat16)
    stacked = jnp.concatenate([near[None], jnp.concatenate(backs, axis=-1)])
    blocks = [
        lax.dynamic_index_in_dim(stacked, lax.rem(j - own_block + cols, cols), 0, False)
        for j in range(cols)
    ]
    return jnp.concatenate(blocks, axis=-1).reshape(DECODE_STEPS, slots, cols * col_width)


def solution(mesh):
    return jax.shard_map(
        per_device,
        mesh=mesh,
        in_specs=(
            P(None, ("groups", "tile"), None),
            P(None, None, ("groups", "tile"), None),
            P(None, ("groups", "tile"), None, None),
            P(("groups", "tile")),
            P("tile", None, None),
        ),
        out_specs=P(None, ("groups", "tile"), None),
        check_vma=False,
    )
```

time: 258 us -> 73.6 us (0.29)
  the two profiles are of different devices: /device:TPU:15 before, /device:TPU:0 now
where the time goes in v2:
time: 73.6 us; the launch traced here: 73.3 us
  starting transfers between devices  30.7 us (42%)
  Pallas kernels  17.7 us (24%)
  waiting for transfers between devices  15.8 us (21%)
  local copies, waits for them, and re-layouts  6.81 us (9%)
  other arithmetic  1.89 us (3%)
    ppermute x9, starting transfers between devices, send(): return lax.ppermute(value, 'tile', [(i, target(i)) for i in range(devices)])  16 us
    ppermute x14, waiting for transfers between devices, swap(): lax.ppermute(value, 'tile', [(i, i ^ distance) for i in range(devices)])  15.6 us
    ppermute x14, starting transfers between devices, swap(): lax.ppermute(value, 'tile', [(i, i ^ distance) for i in range(devices)])  14.7 us
    pallas_call x1, Pallas kernels, attend(): pl.pallas_call(attention_kernel, out_shape=jax.ShapeDtypeStruct((slots, r...  7.16 us
    pallas_call x1, Pallas kernels, load(): pl.pallas_call(load_kernel, in_specs=[pl.BlockSpec(memory_space=pl.ANY)],...  5.92 us
    unnamed x8, local copies, waits for them, and re-layouts  5.46 us
    pallas_call x2, Pallas kernels, project(): pl.pallas_call(project_kernel, in_specs=[vmem] * 9, out_specs=[vmem] * 4,...  4.66 us
  transfers between devices with their start and end apart: 23, of which 7 were waited for; matrix products, arithmetic and copies ran while one was open for 1% of the time, Pallas kernels for 11%

profile of v2, /device:TPU:0, one launch (start us, length us, event | category | flops | bytes accessed | tf_op | source)
XLA Modules:
  0.0 73.3 jit_solution(13347120888469328592)
XLA Ops:
  0.0 1.0 %copy.6 = bf16[2,8,4,16,128]{4,3,0,2,1:T(8,128)(2,1)S(1)} copy(bf16[2,8,4,16,128]{4,1,3,2,0:T(8,128)(2,1)} %bitcast.89) | data formatting | bytes 524288 | tf_op jit(solution)/shard_map/reshape | solution.py:100
  2.4 7.2 %attention.1 = bf16[8,128,128]{2,1,0:T(8,128)(2,1)S(1)} custom-call(s32[8]{0:T(128)S(1)} %copy-done.3, bf16[8,128,128]{2,1,0:T(8,128)(2,1)S(1)} %bitcast.72, bf16[2,2,8,512]{3,2,1,0:T(8,128)(2,1)S(1)} %copy-done.2, bf16[2,8,512,512]{3,2,1,0:T(8,128)(2,1)} %cache_ref.1), custom_call_target="tpu_custom_call" | custom-call | tf_op jit(solution)/shard_map/attention/pallas_call | solution.py:103
  11.4 4.3 %collective-permute-start.1 = (bf16[2,8,16,128]{3,2,1,0:T(8,128)(2,1)S(1)}, bf16[2,8,16,128]{3,2,1,0:T(8,128)(2,1)S(1)}, u32[]{:S(2)}, u32[]{:S(2)}) collective-permute-start(bf16[2,8,16,128]{3,2,1,0:T(8,128)(2,1)S(1)} %bitcast.73), channel_id=1, source_target_pairs={{0,8},{1,9},{2,10},{3,11},{4,12},{5,13},{6,14},{7,15},{8,0},{9,1},... | collective-permute-start | bytes 196616 | tf_op jit(solution)/shard_map/ppermute | solution.py:237
  15.7 2.3 %collective-permute-start.7 = (bf16[2,8,16,128]{3,2,1,0:T(8,128)(2,1)S(1)}, bf16[2,8,16,128]{3,2,1,0:T(8,128)(2,1)S(1)}, u32[]{:S(2)}, u32[]{:S(2)}) collective-permute-start(bf16[2,8,16,128]{3,2,1,0:T(8,128)(2,1)S(1)} %get-tuple-element.48), channel_id=1, source_target_pairs={{0,6},{1,7},{2,4},{3,5},{4,2},{5,3},{6,0},{7,1},{8,14},{9,15},{10,... | collective-permute-start | bytes 196616 | tf_op jit(solution)/shard_map/ppermute | solution.py:237
  19.0 2.8 %collective-permute-start.3 = (bf16[2,8,16,128]{3,2,1,0:T(8,128)(2,1)S(1)}, bf16[2,8,16,128]{3,2,1,0:T(8,128)(2,1)S(1)}, u32[]{:S(2)}, u32[]{:S(2)}) collective-permute-start(bf16[2,8,16,128]{3,2,1,0:T(8,128)(2,1)S(1)} %get-tuple-element.49), channel_id=1, source_target_pairs={{0,12},{1,13},{2,14},{3,15},{4,8},{5,9},{6,10},{7,11},{8,4},{9,5},... | collective-permute-start | bytes 196616 | tf_op jit(solution)/shard_map/ppermute | solution.py:237
  21.9 1.5 %collective-permute-start.5 = (bf16[2,8,16,128]{3,2,1,0:T(8,128)(2,1)S(1)}, bf16[2,8,16,128]{3,2,1,0:T(8,128)(2,1)S(1)}, u32[]{:S(2)}, u32[]{:S(2)}) collective-permute-start(bf16[2,8,16,128]{3,2,1,0:T(8,128)(2,1)S(1)} %get-tuple-element.50), channel_id=1, source_target_pairs={{0,2},{1,3},{2,0},{3,1},{4,6},{5,7},{6,4},{7,5},{8,10},{9,11},{10,... | collective-permute-start | bytes 196616 | tf_op jit(solution)/shard_map/ppermute | solution.py:237
  23.9 5.9 %load.1 = (bf16[1024,4096]{1,0:T(8,128)(2,1)S(1)}, bf16[1024,4096]{1,0:T(8,128)(2,1)S(1)}) custom-call(bf16[1,1024,8192]{2,1,0:T(8,128)(2,1)} %source_ref), custom_call_target="tpu_custom_call" | custom-call | bytes 33554432 | tf_op jit(solution)/shard_map/load/pallas_call | solution.py:144
  30.1 2.3 %project.2 = (bf16[4,16,4096]{2,1,0:T(8,128)(2,1)S(1)}, bf16[4,16,4096]{2,1,0:T(8,128)(2,1)S(1)}, bf16[4,16,4096]{2,1,0:T(8,128)(2,1)S(1)}, bf16[4,16,4096]{2,1,0:T(8,128)(2,1)S(1)}) custom-call(bf16[1,2,8,16,128]{4,3,2,1,0:T(8,128)(2,1)S(1)} %bitcast.74, bf16[1,2,8,16,128]{4,3,2,1,0:T(8,128)(2,1)S(1)} %bitcast.86, bf16[1,2,8,16,128]{4,3,2,1,0:T(8,128)(2,1)S(1)} %bitcast.82, ...), custom_call_target="tpu_custom_call" | custom-call | flops 2147483648 | bytes 8388608 | tf_op jit(solution)/shard_map/project/pallas_call | solution.py:190
  33.6 3.4 %copy-done.1 = bf16[1024,4096]{1,0:T(8,128)(2,1)S(1)} copy-done((bf16[1024,4096]{1,0:T(8,128)(2,1)S(1)}, bf16[1024,4096]{1,0:T(8,128)(2,1)}, u32[]{:S(2)}) %copy-start.1) | copy-done | bytes 8388632
  37.0 2.3 %project.3 = (bf16[4,16,4096]{2,1,0:T(8,128)(2,1)S(1)}, bf16[4,16,4096]{2,1,0:T(8,128)(2,1)S(1)}, bf16[4,16,4096]{2,1,0:T(8,128)(2,1)S(1)}, bf16[4,16,4096]{2,1,0:T(8,128)(2,1)S(1)}) custom-call(bf16[1,2,8,16,128]{4,3,2,1,0:T(8,128)(2,1)S(1)} %bitcast.75, bf16[1,2,8,16,128]{4,3,2,1,0:T(8,128)(2,1)S(1)} %bitcast.87, bf16[1,2,8,16,128]{4,3,2,1,0:T(8,128)(2,1)S(1)} %bitcast.83, ...), custom_call_target="tpu_custom_call" | custom-call | flops 2147483648 | bytes 8388608 | tf_op jit(solution)/shard_map/project/pallas_call | solution.py:190
  40.1 1.5 %collective-permute-start.9 = (bf16[16,4096]{1,0:T(8,128)(2,1)S(1)}, bf16[16,4096]{1,0:T(8,128)(2,1)S(1)}, u32[]{:S(2)}, u32[]{:S(2)}) collective-permute-start(bf16[16,4096]{1,0:T(8,128)(2,1)S(1)} %get-tuple-element.42), channel_id=1, source_target_pairs={{0,2},{1,3},{2,0},{3,1},{4,6},{5,7},{6,4},{7,5},{8,10},{9,11},{10,... | collective-permute-start | bytes 393224 | tf_op jit(solution)/shard_map/ppermute | solution.py:208
  41.6 2.0 %collective-permute-start.11 = (bf16[16,4096]{1,0:T(8,128)(2,1)S(1)}, bf16[16,4096]{1,0:T(8,128)(2,1)S(1)}, u32[]{:S(2)}, u32[]{:S(2)}) collective-permute-start(bf16[16,4096]{1,0:T(8,128)(2,1)S(1)} %get-tuple-element.43), channel_id=1, source_target_pairs={{0,6},{1,7},{2,4},{3,5},{4,2},{5,3},{6,0},{7,1},{8,14},{9,15},{10,... | collective-permute-start | bytes 393224 | tf_op jit(solution)/shard_map/ppermute | solution.py:208
  44.2 1.3 %collective-permute-start.19 = (bf16[16,4096]{1,0:T(8,128)(2,1)S(1)}, bf16[16,4096]{1,0:T(8,128)(2,1)S(1)}, u32[]{:S(2)}, u32[]{:S(2)}) collective-permute-start(bf16[16,4096]{1,0:T(8,128)(2,1)S(1)} %get-tuple-element.45), channel_id=1, source_target_pairs={{0,2},{1,3},{2,0},{3,1},{4,6},{5,7},{6,4},{7,5},{8,10},{9,11},{10,... | collective-permute-start | bytes 393224 | tf_op jit(solution)/shard_map/ppermute | solution.py:208
  45.6 1.9 %collective-permute-start.21 = (bf16[16,4096]{1,0:T(8,128)(2,1)S(1)}, bf16[16,4096]{1,0:T(8,128)(2,1)S(1)}, u32[]{:S(2)}, u32[]{:S(2)}) collective-permute-start(bf16[16,4096]{1,0:T(8,128)(2,1)S(1)} %get-tuple-element.46), channel_id=1, source_target_pairs={{0,6},{1,7},{2,4},{3,5},{4,2},{5,3},{6,0},{7,1},{8,14},{9,15},{10,... | collective-permute-start | bytes 393224 | tf_op jit(solution)/shard_map/ppermute | solution.py:208
  47.8 1.2 %collective-permute-done.9 = bf16[16,4096]{1,0:T(8,128)(2,1)S(1)} collective-permute-done((bf16[16,4096]{1,0:T(8,128)(2,1)S(1)}, bf16[16,4096]{1,0:T(8,128)(2,1)S(1)}, u32[]{:S(2)}, u32[]{:S(2)}) %collective-permute-start.9) | collective-permute-done | bytes 131104 | tf_op jit(solution)/shard_map/ppermute | solution.py:208
  49.0 2.2 %collective-permute-start.20 = (bf16[16,4096]{1,0:T(8,128)(2,1)S(1)}, bf16[16,4096]{1,0:T(8,128)(2,1)S(1)}, u32[]{:S(2)}, u32[]{:S(2)}) collective-permute-start(bf16[16,4096]{1,0:T(8,128)(2,1)S(1)} %get-tuple-element.47), channel_id=1, source_target_pairs={{0,4},{1,5},{2,6},{3,7},{4,0},{5,1},{6,2},{7,3},{8,12},{9,13},{10,... | collective-permute-start | bytes 393224 | tf_op jit(solution)/shard_map/ppermute | solution.py:208
  51.3 2.0 %collective-permute-start.17 = (bf16[16,4096]{1,0:T(8,128)(2,1)S(1)}, bf16[16,4096]{1,0:T(8,128)(2,1)S(1)}, u32[]{:S(2)}, u32[]{:S(2)}) collective-permute-start(bf16[16,4096]{1,0:T(8,128)(2,1)S(1)} %fusion.5), channel_id=1, source_target_pairs={{0,8},{1,9},{2,10},{3,11},{4,12},{5,13},{6,14},{7,15},{8,0},{9,1},... | collective-permute-start | bytes 393224 | tf_op jit(solution)/shard_map/ppermute | solution.py:237
  53.5 1.9 %collective-permute-start.14 = (bf16[16,8192]{1,0:T(8,128)(2,1)S(1)}, bf16[16,8192]{1,0:T(8,128)(2,1)S(1)}, u32[]{:S(2)}, u32[]{:S(2)}) collective-permute-start(bf16[16,8192]{1,0:T(8,128)(2,1)S(1)} %get-tuple-element.33), channel_id=1, source_target_pairs={{0,2},{1,3},{2,0},{3,1},{4,6},{5,7},{6,4},{7,5},{8,10},{9,11},{10,... | collective-permute-start | bytes 786440 | tf_op jit(solution)/shard_map/ppermute | solution.py:208
  55.4 1.8 %collective-permute-start.16 = (bf16[16,8192]{1,0:T(8,128)(2,1)S(1)}, bf16[16,8192]{1,0:T(8,128)(2,1)S(1)}, u32[]{:S(2)}, u32[]{:S(2)}) collective-permute-start(bf16[16,8192]{1,0:T(8,128)(2,1)S(1)} %get-tuple-element.34), channel_id=1, source_target_pairs={{0,6},{1,7},{2,4},{3,5},{4,2},{5,3},{6,0},{7,1},{8,14},{9,15},{10,... | collective-permute-start | bytes 786440 | tf_op jit(solution)/shard_map/ppermute | solution.py:208
  57.2 1.5 %collective-permute-done.20 = bf16[16,4096]{1,0:T(8,128)(2,1)S(1)} collective-permute-done((bf16[16,4096]{1,0:T(8,128)(2,1)S(1)}, bf16[16,4096]{1,0:T(8,128)(2,1)S(1)}, u32[]{:S(2)}, u32[]{:S(2)}) %collective-permute-start.20) | collective-permute-done | bytes 131104 | tf_op jit(solution)/shard_map/ppermute | solution.py:208
  58.8 1.6 %collective-permute-start.22 = (bf16[16,4096]{1,0:T(8,128)(2,1)S(1)}, bf16[16,4096]{1,0:T(8,128)(2,1)S(1)}, u32[]{:S(2)}, u32[]{:S(2)}) collective-permute-start(bf16[16,4096]{1,0:T(8,128)(2,1)S(1)} %fusion.3), channel_id=1, source_target_pairs={{0,8},{1,9},{2,10},{3,11},{4,12},{5,13},{6,14},{7,15},{8,0},{9,1},... | collective-permute-start | bytes 393224 | tf_op jit(solution)/shard_map/ppermute | solution.py:237
  60.4 2.5 %collective-permute-done.14 = bf16[16,8192]{1,0:T(8,128)(2,1)S(1)} collective-permute-done((bf16[16,8192]{1,0:T(8,128)(2,1)S(1)}, bf16[16,8192]{1,0:T(8,128)(2,1)S(1)}, u32[]{:S(2)}, u32[]{:S(2)}) %collective-permute-start.14) | collective-permute-done | bytes 262176 | tf_op jit(solution)/shard_map/ppermute | solution.py:208
  62.9 5.7 %collective-permute-done.16 = bf16[16,8192]{1,0:T(8,128)(2,1)S(1)} collective-permute-done((bf16[16,8192]{1,0:T(8,128)(2,1)S(1)}, bf16[16,8192]{1,0:T(8,128)(2,1)S(1)}, u32[]{:S(2)}, u32[]{:S(2)}) %collective-permute-start.16) | collective-permute-done | bytes 262176 | tf_op jit(solution)/shard_map/ppermute | solution.py:208
  68.6 3.6 %collective-permute-done.15 = bf16[16,8192]{1,0:T(8,128)(2,1)S(1)} collective-permute-done((bf16[16,8192]{1,0:T(8,128)(2,1)S(1)}, bf16[16,8192]{1,0:T(8,128)(2,1)S(1)}, u32[]{:S(2)}, u32[]{:S(2)}) %collective-permute-start.15) | collective-permute-done | bytes 262176 | tf_op jit(solution)/shard_map/ppermute | solution.py:208
  (54 shorter events, 9.2 us)
Async XLA Ops:
  9.8 1.5 %collective-permute-start = (bf16[4,8,16,128]{3,2,1,0:T(8,128)(2,1)S(1)}, bf16[4,8,16,128]{3,2,1,0:T(8,128)(2,1)S(1)}, u32[]{:S(2)}, u32[]{:S(2)}) collective-permute-start(bf16[4,8,16,128]{3,2,1,0:T(8,128)(2,1)S(1)} %get-tuple-element.53), channel_id=1, source_target_pairs={{0,1},{1,0},{2,3},{3,2},{4,5},{5,4},{6,7},{7,6},{8,9},{9,8},{10,11... | collective-permute-start | bytes 393224 | tf_op jit(solution)/shard_map/ppermute | solution.py:208
  11.4 10.5 %collective-permute-start.1 = (bf16[2,8,16,128]{3,2,1,0:T(8,128)(2,1)S(1)}, bf16[2,8,16,128]{3,2,1,0:T(8,128)(2,1)S(1)}, u32[]{:S(2)}, u32[]{:S(2)}) collective-permute-start(bf16[2,8,16,128]{3,2,1,0:T(8,128)(2,1)S(1)} %bitcast.73), channel_id=1, source_target_pairs={{0,8},{1,9},{2,10},{3,11},{4,12},{5,13},{6,14},{7,15},{8,0},{9,1},... | collective-permute-start | bytes 196616 | tf_op jit(solution)/shard_map/ppermute | solution.py:237
  15.7 7.6 %collective-permute-start.7 = (bf16[2,8,16,128]{3,2,1,0:T(8,128)(2,1)S(1)}, bf16[2,8,16,128]{3,2,1,0:T(8,128)(2,1)S(1)}, u32[]{:S(2)}, u32[]{:S(2)}) collective-permute-start(bf16[2,8,16,128]{3,2,1,0:T(8,128)(2,1)S(1)} %get-tuple-element.48), channel_id=1, source_target_pairs={{0,6},{1,7},{2,4},{3,5},{4,2},{5,3},{6,0},{7,1},{8,14},{9,15},{10,... | collective-permute-start | bytes 196616 | tf_op jit(solution)/shard_map/ppermute | solution.py:237
  18.0 11.8 %collective-permute-start.4 = (bf16[2,8,16,128]{3,2,1,0:T(8,128)(2,1)S(1)}, bf16[2,8,16,128]{3,2,1,0:T(8,128)(2,1)S(1)}, u32[]{:S(2)}, u32[]{:S(2)}) collective-permute-start(bf16[2,8,16,128]{3,2,1,0:T(8,128)(2,1)S(1)} %get-tuple-element.48), channel_id=1, source_target_pairs={{0,14},{1,15},{2,12},{3,13},{4,10},{5,11},{6,8},{7,9},{8,6},{9,7},... | collective-permute-start | bytes 196616 | tf_op jit(solution)/shard_map/ppermute | solution.py:237
  18.2 11.7 %collective-permute-start.6 = (bf16[2,8,16,128]{3,2,1,0:T(8,128)(2,1)S(1)}, bf16[2,8,16,128]{3,2,1,0:T(8,128)(2,1)S(1)}, u32[]{:S(2)}, u32[]{:S(2)}) collective-permute-start(bf16[2,8,16,128]{3,2,1,0:T(8,128)(2,1)S(1)} %get-tuple-element.49), channel_id=1, source_target_pairs={{0,4},{1,5},{2,6},{3,7},{4,0},{5,1},{6,2},{7,3},{8,12},{9,13},{10,... | collective-permute-start | bytes 196616 | tf_op jit(solution)/shard_map/ppermute | solution.py:237
  19.0 10.8 %collective-permute-start.3 = (bf16[2,8,16,128]{3,2,1,0:T(8,128)(2,1)S(1)}, bf16[2,8,16,128]{3,2,1,0:T(8,128)(2,1)S(1)}, u32[]{:S(2)}, u32[]{:S(2)}) collective-permute-start(bf16[2,8,16,128]{3,2,1,0:T(8,128)(2,1)S(1)} %get-tuple-element.49), channel_id=1, source_target_pairs={{0,12},{1,13},{2,14},{3,15},{4,8},{5,9},{6,10},{7,11},{8,4},{9,5},... | collective-permute-start | bytes 196616 | tf_op jit(solution)/shard_map/ppermute | solution.py:237
  21.9 8.0 %collective-permute-start.5 = (bf16[2,8,16,128]{3,2,1,0:T(8,128)(2,1)S(1)}, bf16[2,8,16,128]{3,2,1,0:T(8,128)(2,1)S(1)}, u32[]{:S(2)}, u32[]{:S(2)}) collective-permute-start(bf16[2,8,16,128]{3,2,1,0:T(8,128)(2,1)S(1)} %get-tuple-element.50), channel_id=1, source_target_pairs={{0,2},{1,3},{2,0},{3,1},{4,6},{5,7},{6,4},{7,5},{8,10},{9,11},{10,... | collective-permute-start | bytes 196616 | tf_op jit(solution)/shard_map/ppermute | solution.py:237
  23.3 6.8 %collective-permute-start.2 = (bf16[2,8,16,128]{3,2,1,0:T(8,128)(2,1)S(1)}, bf16[2,8,16,128]{3,2,1,0:T(8,128)(2,1)S(1)}, u32[]{:S(2)}, u32[]{:S(2)}) collective-permute-start(bf16[2,8,16,128]{3,2,1,0:T(8,128)(2,1)S(1)} %get-tuple-element.50), channel_id=1, source_target_pairs={{0,10},{1,11},{2,8},{3,9},{4,14},{5,15},{6,12},{7,13},{8,2},{9,3},... | collective-permute-start | bytes 196616 | tf_op jit(solution)/shard_map/ppermute | solution.py:237
  33.1 6.8 %collective-permute-start.8 = (bf16[4,16,4096]{2,1,0:T(8,128)(2,1)S(1)}, bf16[4,16,4096]{2,1,0:T(8,128)(2,1)S(1)}, u32[]{:S(2)}, u32[]{:S(2)}) collective-permute-start(bf16[4,16,4096]{2,1,0:T(8,128)(2,1)S(1)} %get-tuple-element.23), channel_id=1, source_target_pairs={{0,1},{1,0},{2,3},{3,2},{4,5},{5,4},{6,7},{7,6},{8,9},{9,8},{10,11... | collective-permute-start | bytes 1572872 | tf_op jit(solution)/shard_map/ppermute | solution.py:208
  33.1 11.1 %collective-permute-start.12 = (bf16[4,16,4096]{2,1,0:T(8,128)(2,1)S(1)}, bf16[4,16,4096]{2,1,0:T(8,128)(2,1)S(1)}, u32[]{:S(2)}, u32[]{:S(2)}) collective-permute-start(bf16[4,16,4096]{2,1,0:T(8,128)(2,1)S(1)} %get-tuple-element.25), channel_id=1, source_target_pairs={{0,1},{1,0},{2,3},{3,2},{4,5},{5,4},{6,7},{7,6},{8,9},{9,8},{10,11... | collective-permute-start | bytes 1572872 | tf_op jit(solution)/shard_map/ppermute | solution.py:208
  33.6 3.4 %copy-start.1 = (bf16[1024,4096]{1,0:T(8,128)(2,1)S(1)}, bf16[1024,4096]{1,0:T(8,128)(2,1)}, u32[]{:S(2)}) copy-start(bf16[1024,4096]{1,0:T(8,128)(2,1)} %copy-done) | copy-start | bytes 25165828
  39.3 6.3 %collective-permute-start.13 = (bf16[4,16,4096]{2,1,0:T(8,128)(2,1)S(1)}, bf16[4,16,4096]{2,1,0:T(8,128)(2,1)S(1)}, u32[]{:S(2)}, u32[]{:S(2)}) collective-permute-start(bf16[4,16,4096]{2,1,0:T(8,128)(2,1)S(1)} %get-tuple-element.28), channel_id=1, source_target_pairs={{0,1},{1,0},{2,3},{3,2},{4,5},{5,4},{6,7},{7,6},{8,9},{9,8},{10,11... | collective-permute-start | bytes 1572872 | tf_op jit(solution)/shard_map/ppermute | solution.py:208
  39.4 4.2 %collective-permute-start.18 = (bf16[4,16,4096]{2,1,0:T(8,128)(2,1)S(1)}, bf16[4,16,4096]{2,1,0:T(8,128)(2,1)S(1)}, u32[]{:S(2)}, u32[]{:S(2)}) collective-permute-start(bf16[4,16,4096]{2,1,0:T(8,128)(2,1)S(1)} %get-tuple-element.32), channel_id=1, source_target_pairs={{0,1},{1,0},{2,3},{3,2},{4,5},{5,4},{6,7},{7,6},{8,9},{9,8},{10,11... | collective-permute-start | bytes 1572872 | tf_op jit(solution)/shard_map/ppermute | solution.py:208
  40.1 8.9 %collective-permute-start.9 = (bf16[16,4096]{1,0:T(8,128)(2,1)S(1)}, bf16[16,4096]{1,0:T(8,128)(2,1)S(1)}, u32[]{:S(2)}, u32[]{:S(2)}) collective-permute-start(bf16[16,4096]{1,0:T(8,128)(2,1)S(1)} %get-tuple-element.42), channel_id=1, source_target_pairs={{0,2},{1,3},{2,0},{3,1},{4,6},{5,7},{6,4},{7,5},{8,10},{9,11},{10,... | collective-permute-start | bytes 393224 | tf_op jit(solution)/shard_map/ppermute | solution.py:208
  41.6 9.6 %collective-permute-start.11 = (bf16[16,4096]{1,0:T(8,128)(2,1)S(1)}, bf16[16,4096]{1,0:T(8,128)(2,1)S(1)}, u32[]{:S(2)}, u32[]{:S(2)}) collective-permute-start(bf16[16,4096]{1,0:T(8,128)(2,1)S(1)} %get-tuple-element.43), channel_id=1, source_target_pairs={{0,6},{1,7},{2,4},{3,5},{4,2},{5,3},{6,0},{7,1},{8,14},{9,15},{10,... | collective-permute-start | bytes 393224 | tf_op jit(solution)/shard_map/ppermute | solution.py:208
  43.6 7.7 %collective-permute-start.10 = (bf16[16,4096]{1,0:T(8,128)(2,1)S(1)}, bf16[16,4096]{1,0:T(8,128)(2,1)S(1)}, u32[]{:S(2)}, u32[]{:S(2)}) collective-permute-start(bf16[16,4096]{1,0:T(8,128)(2,1)S(1)} %get-tuple-element.44), channel_id=1, source_target_pairs={{0,4},{1,5},{2,6},{3,7},{4,0},{5,1},{6,2},{7,3},{8,12},{9,13},{10,... | collective-permute-start | bytes 393224 | tf_op jit(solution)/shard_map/ppermute | solution.py:208
  44.2 11.2 %collective-permute-start.19 = (bf16[16,4096]{1,0:T(8,128)(2,1)S(1)}, bf16[16,4096]{1,0:T(8,128)(2,1)S(1)}, u32[]{:S(2)}, u32[]{:S(2)}) collective-permute-start(bf16[16,4096]{1,0:T(8,128)(2,1)S(1)} %get-tuple-element.45), channel_id=1, source_target_pairs={{0,2},{1,3},{2,0},{3,1},{4,6},{5,7},{6,4},{7,5},{8,10},{9,11},{10,... | collective-permute-start | bytes 393224 | tf_op jit(solution)/shard_map/ppermute | solution.py:208
  45.6 11.6 %collective-permute-start.21 = (bf16[16,4096]{1,0:T(8,128)(2,1)S(1)}, bf16[16,4096]{1,0:T(8,128)(2,1)S(1)}, u32[]{:S(2)}, u32[]{:S(2)}) collective-permute-start(bf16[16,4096]{1,0:T(8,128)(2,1)S(1)} %get-tuple-element.46), channel_id=1, source_target_pairs={{0,6},{1,7},{2,4},{3,5},{4,2},{5,3},{6,0},{7,1},{8,14},{9,15},{10,... | collective-permute-start | bytes 393224 | tf_op jit(solution)/shard_map/ppermute | solution.py:208
  49.0 9.7 %collective-permute-start.20 = (bf16[16,4096]{1,0:T(8,128)(2,1)S(1)}, bf16[16,4096]{1,0:T(8,128)(2,1)S(1)}, u32[]{:S(2)}, u32[]{:S(2)}) collective-permute-start(bf16[16,4096]{1,0:T(8,128)(2,1)S(1)} %get-tuple-element.47), channel_id=1, source_target_pairs={{0,4},{1,5},{2,6},{3,7},{4,0},{5,1},{6,2},{7,3},{8,12},{9,13},{10,... | collective-permute-start | bytes 393224 | tf_op jit(solution)/shard_map/ppermute | solution.py:208
  51.3 21.0 %collective-permute-start.17 = (bf16[16,4096]{1,0:T(8,128)(2,1)S(1)}, bf16[16,4096]{1,0:T(8,128)(2,1)S(1)}, u32[]{:S(2)}, u32[]{:S(2)}) collective-permute-start(bf16[16,4096]{1,0:T(8,128)(2,1)S(1)} %fusion.5), channel_id=1, source_target_pairs={{0,8},{1,9},{2,10},{3,11},{4,12},{5,13},{6,14},{7,15},{8,0},{9,1},... | collective-permute-start | bytes 393224 | tf_op jit(solution)/shard_map/ppermute | solution.py:237
  53.5 9.4 %collective-permute-start.14 = (bf16[16,8192]{1,0:T(8,128)(2,1)S(1)}, bf16[16,8192]{1,0:T(8,128)(2,1)S(1)}, u32[]{:S(2)}, u32[]{:S(2)}) collective-permute-start(bf16[16,8192]{1,0:T(8,128)(2,1)S(1)} %get-tuple-element.33), channel_id=1, source_target_pairs={{0,2},{1,3},{2,0},{3,1},{4,6},{5,7},{6,4},{7,5},{8,10},{9,11},{10,... | collective-permute-start | bytes 786440 | tf_op jit(solution)/shard_map/ppermute | solution.py:208
  55.4 13.1 %collective-permute-start.16 = (bf16[16,8192]{1,0:T(8,128)(2,1)S(1)}, bf16[16,8192]{1,0:T(8,128)(2,1)S(1)}, u32[]{:S(2)}, u32[]{:S(2)}) collective-permute-start(bf16[16,8192]{1,0:T(8,128)(2,1)S(1)} %get-tuple-element.34), channel_id=1, source_target_pairs={{0,6},{1,7},{2,4},{3,5},{4,2},{5,3},{6,0},{7,1},{8,14},{9,15},{10,... | collective-permute-start | bytes 786440 | tf_op jit(solution)/shard_map/ppermute | solution.py:208
  57.2 15.0 %collective-permute-start.15 = (bf16[16,8192]{1,0:T(8,128)(2,1)S(1)}, bf16[16,8192]{1,0:T(8,128)(2,1)S(1)}, u32[]{:S(2)}, u32[]{:S(2)}) collective-permute-start(bf16[16,8192]{1,0:T(8,128)(2,1)S(1)} %get-tuple-element.35), channel_id=1, source_target_pairs={{0,4},{1,5},{2,6},{3,7},{4,0},{5,1},{6,2},{7,3},{8,12},{9,13},{10,... | collective-permute-start | bytes 786440 | tf_op jit(solution)/shard_map/ppermute | solution.py:208
  58.8 13.6 %collective-permute-start.22 = (bf16[16,4096]{1,0:T(8,128)(2,1)S(1)}, bf16[16,4096]{1,0:T(8,128)(2,1)S(1)}, u32[]{:S(2)}, u32[]{:S(2)}) collective-permute-start(bf16[16,4096]{1,0:T(8,128)(2,1)S(1)} %fusion.3), channel_id=1, source_target_pairs={{0,8},{1,9},{2,10},{3,11},{4,12},{5,13},{6,14},{7,15},{8,0},{9,1},... | collective-permute-start | bytes 393224 | tf_op jit(solution)/shard_map/ppermute | solution.py:237
  (3 other events, 4.7 us)

commit v3 on v2

v3 whole, which is shorter than its diff:
```python
import functools
import math

import jax
import jax.numpy as jnp
from jax import lax
from jax.experimental import pallas as pl
from jax.experimental.pallas import tpu as pltpu
from jax.sharding import PartitionSpec as P

QH = 64
KVH = 4
HD = 128
DECODE_STEPS = 2
GRID_ROWS = 8
GROUP = QH // KVH
BLOCK_HEADS = QH // GRID_ROWS
CHUNKS = 2
TILE_N = 1024
PAGE = 128
TOGETHER = 4
NEAR_GRANT = 24
MIB = 1 << 20


def attention_kernel(
    lengths_ref, query_ref, fresh_ref, cache_ref, out_ref, cached, lengths, fresh, sems, small_sems
):
    slots, capacity, width = cached.shape[1:]
    factor = 1.0 / math.sqrt(HD)
    rows = KVH * DECODE_STEPS * GROUP
    head_rows = rows // KVH
    pages = capacity // PAGE

    def copy(which, slot, page):
        span = pl.ds(page * PAGE, PAGE)
        return pltpu.make_async_copy(
            cache_ref.at[which, slot, span], cached.at[which, slot, span], sems.at[which, slot, page]
        )

    def page_copies(slot, first, used, act):
        for page in range(first, pages):

            @pl.when(page < used)
            def _(page=page):
                for which in range(2):
                    act(copy(which, slot, page))

    lengths_copy = pltpu.make_async_copy(lengths_ref, lengths, small_sems.at[0])
    fresh_copy = pltpu.make_async_copy(fresh_ref, fresh, small_sems.at[1])
    lengths_copy.start()
    fresh_copy.start()
    for slot in range(slots):
        for which in range(2):
            copy(which, slot, 0).start()
    lengths_copy.wait()

    def used_pages(group):
        longest = lengths[group[0]]
        for slot in group[1:]:
            longest = jnp.maximum(longest, lengths[slot])
        used = (longest + DECODE_STEPS + PAGE - 1) // PAGE
        return jnp.where(used >= 3, pages, used)

    groups = [range(first, first + TOGETHER) for first in range(0, slots, TOGETHER)]
    for group in groups:
        used = used_pages(group)
        for slot in group:
            page_copies(slot, 1, used, lambda copy: copy.start())
    own = (
        lax.broadcasted_iota(jnp.int32, (rows, width), 0) // head_rows
        == lax.broadcasted_iota(jnp.int32, (rows, width), 1) // HD
    )
    window_row = lax.broadcasted_iota(jnp.int32, (32, width), 0)
    fresh_copy.wait()

    def patch(slot):
        length = lengths[slot]
        base = pl.multiple_of(jnp.minimum((length // 16) * 16, capacity - 32), 16)
        for which in range(2):
            window = cached[which, slot, pl.ds(base, 32), :].astype(jnp.float32)
            for t in range(DECODE_STEPS):
                row = fresh[t, which].astype(jnp.float32)[slot : slot + 1]
                window = jnp.where(window_row + base == length + t, row, window)
            cached[which, slot, pl.ds(base, 32), :] = window.astype(jnp.bfloat16)

    def mix(group, count):
        position = lax.broadcasted_iota(jnp.int32, (rows, count), 1)
        step = lax.broadcasted_iota(jnp.int32, (rows, count), 0) // GROUP % DECODE_STEPS
        visible = position - step
        scores = []
        for slot in group:
            query = jnp.concatenate([query_ref[slot]] * KVH, axis=1)
            query = jnp.where(own, query, jnp.zeros((), query.dtype))
            scores.append(
                lax.dot_general(
                    query,
                    cached[0, slot, :count, :],
                    (((1,), (1,)), ((), ())),
                    preferred_element_type=jnp.float32,
                )
            )
        weights = []
        for slot, score in zip(group, scores):
            score = jnp.where(visible <= lengths[slot], score * factor, -jnp.inf)
            weight = jnp.exp(score - score.max(-1, keepdims=True))
            weights.append(weight * (1.0 / weight.sum(-1, keepdims=True)))
        for slot, weight in zip(group, weights):
            mixed = jnp.dot(
                weight.astype(jnp.bfloat16),
                cached[1, slot, :count, :],
                preferred_element_type=jnp.float32,
            )
            for head in range(KVH):
                own_rows = slice(head * head_rows, (head + 1) * head_rows)
                own_lanes = slice(head * HD, (head + 1) * HD)
                out_ref[slot, own_rows, :] = mixed[own_rows, own_lanes].astype(jnp.bfloat16)

    for group in groups:
        used = used_pages(group)
        for slot in group:
            for which in range(2):
                copy(which, slot, 0).wait()
            page_copies(slot, 1, used, lambda copy: copy.wait())
        for slot in group:
            patch(slot)
        for count in (1, 2, pages):
            pl.when(used == count)(functools.partial(mix, group, count * PAGE))


def in_hbm(array):
    return pltpu.with_memory_space_constraint(array, pltpu.HBM)


def attend(queries, fresh_kv, cache, lengths):
    slots, capacity, width = cache.shape[1:]
    rows = KVH * DECODE_STEPS * GROUP
    query = queries.reshape(DECODE_STEPS, slots, KVH, GROUP, HD)
    query = jnp.transpose(query, (1, 2, 0, 3, 4)).reshape(slots, rows, HD)
    vmem = pl.BlockSpec(memory_space=pltpu.VMEM)
    hbm = pl.BlockSpec(memory_space=pltpu.HBM)
    return pl.pallas_call(
        attention_kernel,
        out_shape=jax.ShapeDtypeStruct((slots, rows, HD), jnp.bfloat16),
        in_specs=[hbm, vmem, hbm, hbm],
        out_specs=vmem,
        scratch_shapes=[
            pltpu.VMEM((2, slots, capacity, width), jnp.bfloat16),
            pltpu.SMEM(lengths.shape, lengths.dtype),
            pltpu.VMEM(fresh_kv.shape, fresh_kv.dtype),
            pltpu.SemaphoreType.DMA((2, slots, capacity // PAGE)),
            pltpu.SemaphoreType.DMA((2,)),
        ],
        compiler_params=pltpu.CompilerParams(vmem_limit_bytes=40 * MIB),
        name="attention",
    )(in_hbm(lengths), query, in_hbm(fresh_kv), in_hbm(cache))


def order_rows(x_refs, ordered):
    row = 0
    for core in range(2):
        for x_ref in x_refs:
            shifts, _, _, slot_rows, _ = x_ref.shape
            for shift in range(shifts):
                for head in range(BLOCK_HEADS):
                    ordered[row : row + slot_rows, head * HD : (head + 1) * HD] = x_ref[
                        shift, core, head
                    ]
                row += slot_rows


def multiply(ordered, w_ref, start, tile, out_refs, first):
    product = jnp.dot(
        ordered[...], w_ref[:, start : start + tile], preferred_element_type=jnp.float32
    ).astype(jnp.bfloat16)
    half = ordered.shape[0] // 2
    for i, out_ref in enumerate(out_refs):
        out_ref[:, :, first : first + tile] = product[i * half : (i + 1) * half].reshape(
            out_ref.shape[:2] + (tile,)
        )


def near_kernel(*refs):
    x_refs, source_ref = refs[:4], refs[4]
    out_refs, held_ref, ordered, sems = refs[5:7], refs[7], refs[8], refs[9]
    width = held_ref.shape[1]
    tile = width // sems.shape[0]

    def copy(i):
        span = pl.ds(i * tile, tile)
        return pltpu.make_async_copy(source_ref.at[0, :, span], held_ref.at[:, span], sems.at[i])

    for i in range(sems.shape[0]):
        copy(i).start()
    order_rows(x_refs, ordered)
    for i in range(sems.shape[0]):
        copy(i).wait()
        multiply(ordered, held_ref, i * tile, tile, out_refs, i * tile)


def project_near(pieces, weight):
    shifts, _, _, slot_rows, _ = pieces[0].shape
    _, depth, width = weight.shape
    shape = jax.ShapeDtypeStruct((4, shifts * slot_rows, width), jnp.bfloat16)
    vmem = pl.BlockSpec(memory_space=pltpu.VMEM)
    return pl.pallas_call(
        near_kernel,
        in_specs=[vmem] * 4 + [pl.BlockSpec(memory_space=pl.ANY)],
        out_specs=[vmem] * 3,
        scratch_shapes=[
            pltpu.VMEM((8 * shifts * slot_rows, depth), jnp.bfloat16),
            pltpu.SemaphoreType.DMA((max(1, width // TILE_N),)),
        ],
        out_shape=[shape] * 2 + [jax.ShapeDtypeStruct((depth, width), weight.dtype)],
        compiler_params=pltpu.CompilerParams(vmem_limit_bytes=NEAR_GRANT * MIB),
        cost_estimate=pl.CostEstimate(
            flops=16 * shifts * slot_rows * depth * width,
            bytes_accessed=4 * depth * width,
            transcendentals=0,
        ),
        name="project_near",
    )(*pieces, in_hbm(weight))


def far_kernel(*refs):
    x_refs, w_ref, out_refs, ordered = refs[:4], refs[4], refs[5:-1], refs[-1]
    part = out_refs[0].shape[2]
    tile = min(TILE_N, part)
    order_rows(x_refs, ordered)
    for chunk in range(len(out_refs) // 2):
        for first in range(0, part, tile):
            pair = out_refs[2 * chunk : 2 * chunk + 2]
            multiply(ordered, w_ref, chunk * part + first, tile, pair, first)


def project_far(pieces, weight):
    shifts, _, _, slot_rows, _ = pieces[0].shape
    depth, width = weight.shape
    rows = 8 * shifts * slot_rows
    shape = jax.ShapeDtypeStruct((4, shifts * slot_rows, width // CHUNKS), jnp.bfloat16)
    vmem = pl.BlockSpec(memory_space=pltpu.VMEM)
    return pl.pallas_call(
        far_kernel,
        in_specs=[vmem] * 5,
        out_specs=[vmem] * (2 * CHUNKS),
        scratch_shapes=[pltpu.VMEM((rows, depth), jnp.bfloat16)],
        out_shape=[shape] * (2 * CHUNKS),
        compiler_params=pltpu.CompilerParams(vmem_limit_bytes=24 * MIB),
        cost_estimate=pl.CostEstimate(
            flops=2 * rows * depth * width, bytes_accessed=2 * depth * width, transcendentals=0
        ),
        name="project_far",
    )(*pieces, weight)


def swap(value, distance):
    devices = lax.axis_size("tile")
    return lax.ppermute(value, "tile", [(i, i ^ distance) for i in range(devices)])


def widen(value):
    return value.astype(jnp.float32)


def direct(total):
    sent = total.astype(jnp.bfloat16)
    arrived = [swap(sent[i], 2 * i) for i in range(1, 4)]
    return total[0] + sum(widen(value) for value in arrived)


def stepwise(total):
    total = total.reshape((2, 2) + total.shape[1:])
    total = total[:, 0] + widen(swap(total[:, 1].astype(jnp.bfloat16), 2))
    return total[0] + widen(swap(total[1].astype(jnp.bfloat16), 4))


def per_device(queries, fresh_kv, cache, lengths, out_weight):
    slots = cache.shape[1]
    devices = lax.axis_size("tile")
    cols = devices // GRID_ROWS
    col_width = out_weight.shape[2]
    slot_rows = DECODE_STEPS * slots
    own = lax.axis_index("tile")
    own_block = own // GRID_ROWS
    own_square = own // 2 % 4
    own_core = own % 2

    def send(value, shift, distance):
        def target(i):
            block, row = i // GRID_ROWS, i % GRID_ROWS
            return (block + shift) % cols * GRID_ROWS + (row ^ distance)

        return lax.ppermute(value, "tile", [(i, target(i)) for i in range(devices)])

    attended = attend(queries, fresh_kv, cache, lengths)
    blocks = attended.reshape(slots, KVH, DECODE_STEPS, GROUP // BLOCK_HEADS, BLOCK_HEADS, HD)
    blocks = jnp.transpose(blocks, (3, 1, 4, 2, 0, 5))
    blocks = blocks.reshape(2, 4, BLOCK_HEADS, slot_rows, HD)
    kept = jnp.where(own_core == 0, blocks[0], blocks[1])
    given = jnp.where(own_core == 0, blocks[1], blocks[0])
    cat = jnp.stack([kept, swap(given, 1)], axis=1)
    cat, weight = lax.optimization_barrier((cat, out_weight))
    cat = [
        lax.dynamic_index_in_dim(cat, jnp.bitwise_xor(own_square, distance), 0, False)
        for distance in range(4)
    ]
    far = [
        jnp.stack([send(cat[i], shift, 2 * i) for shift in range(1, cols)]) for i in range(4)
    ]
    near = [(send(cat[i], 0, 2 * i) if i else cat[0])[None] for i in range(4)]
    near_keep, near_give, weight = project_near(near, weight)
    far, weight = lax.optimization_barrier((far, weight))
    partial = project_far(far, weight)
    near_total = widen(near_keep) + widen(swap(near_give, 1))
    backs = []
    for chunk in range(CHUNKS):
        keep, give = partial[2 * chunk : 2 * chunk + 2]
        sums = direct(widen(keep) + widen(swap(give, 1))).astype(jnp.bfloat16)
        sums = sums.reshape(cols - 1, slot_rows, -1)
        backs.append(jnp.stack([send(sums[s - 1], cols - s, 0) for s in range(1, cols)]))
    near = direct(near_total).astype(jnp.bfloat16)
    stacked = jnp.concatenate([near[None], jnp.concatenate(backs, axis=-1)])
    blocks = [
        lax.dynamic_index_in_dim(stacked, lax.rem(j - own_block + cols, cols), 0, False)
        for j in range(cols)
    ]
    return jnp.concatenate(blocks, axis=-1).reshape(DECODE_STEPS, slots, cols * col_width)


def solution(mesh):
    return jax.shard_map(
        per_device,
        mesh=mesh,
        in_specs=(
            P(None, ("groups", "tile"), None),
            P(None, None, ("groups", "tile"), None),
            P(None, ("groups", "tile"), None, None),
            P(("groups", "tile")),
            P("tile", None, None),
        ),
        out_specs=P(None, ("groups", "tile"), None),
        check_vma=False,
    )
```

time: 73.6 us -> 69.5 us (0.944)
  waiting for transfers between devices: 15.8 us -> 23.3 us
  local copies, waits for them, and re-layouts: 6.81 us -> 2.13 us
  starting transfers between devices: 30.7 us -> 26.9 us
  Pallas kernels: 17.7 us -> 14.1 us
  other arithmetic: 1.89 us -> 2.73 us
    ppermute x14 -> x13, waiting for transfers between devices: 15.6 us -> 22.4 us  [swap(): lax.ppermute(value, 'tile', [(i, i ^ distance) for i in range(devices)])]
    unnamed x8 -> x2, local copies, waits for them, and re-layouts: 5.46 us -> 0.78 us
    ppermute x14 -> x13, starting transfers between devices: 14.7 us -> 11.9 us  [swap(): lax.ppermute(value, 'tile', [(i, i ^ distance) for i in range(devices)])]
    pallas_call x1, Pallas kernels: 7.16 us -> 5.27 us  [attend(): pl.pallas_call(attention_kernel, out_shape=jax.ShapeDtypeStruct((slots, r...]
    pallas_call x3 -> x2, Pallas kernels: 10.6 us -> 8.8 us  [the longest x1 6.44 us: project_near(): pl.pallas_call(near_kernel, in_specs=[vmem] * 4 + [pl.BlockSpec(memory_sp...]
    ppermute x9, starting transfers between devices: 16 us -> 15.1 us  [send(): return lax.ppermute(value, 'tile', [(i, target(i)) for i in range(devices)])]
    convert_element_type x3 -> x2, other arithmetic: 0.38 us -> 1.31 us  [direct(): sent = total.astype(jnp.bfloat16)]
  transfers between devices with their start and end apart: 23 -> 22, of which waited for: 7 -> 8; matrix products, arithmetic and copies ran while one was open for 1% -> 3% of each run, Pallas kernels for 11% -> 9%
where the time goes in v3:
time: 69.5 us; the launch traced here: 69.3 us
  starting transfers between devices  26.9 us (39%)
  waiting for transfers between devices  23.3 us (34%)
  Pallas kernels  14.1 us (20%)
  other arithmetic  2.73 us (4%)
  local copies, waits for them, and re-layouts  2.13 us (3%)
    ppermute x13, waiting for transfers between devices, swap(): lax.ppermute(value, 'tile', [(i, i ^ distance) for i in range(devices)])  22.4 us
    ppermute x9, starting transfers between devices, send(): return lax.ppermute(value, 'tile', [(i, target(i)) for i in range(devices)])  15.1 us
    ppermute x13, starting transfers between devices, swap(): lax.ppermute(value, 'tile', [(i, i ^ distance) for i in range(devices)])  11.9 us
    pallas_call x1, Pallas kernels, project_near(): pl.pallas_call(near_kernel, in_specs=[vmem] * 4 + [pl.BlockSpec(memory_sp...  6.44 us
    pallas_call x1, Pallas kernels, attend(): pl.pallas_call(attention_kernel, out_shape=jax.ShapeDtypeStruct((slots, r...  5.27 us
    pallas_call x1, Pallas kernels, project_far(): pl.pallas_call(far_kernel, in_specs=[vmem] * 5, out_specs=[vmem] * (2 * C...  2.36 us
  transfers between devices with their start and end apart: 22, of which 8 were waited for; matrix products, arithmetic and copies ran while one was open for 3% of the time, Pallas kernels for 9%

profile of v3, /device:TPU:0, one launch (start us, length us, event | category | flops | bytes accessed | tf_op | source)
XLA Modules:
  0.0 69.3 jit_solution(16511223748673240116)
XLA Ops:
  0.0 1.0 %copy.6 = bf16[2,8,4,16,128]{4,3,0,2,1:T(8,128)(2,1)S(1)} copy(bf16[2,8,4,16,128]{4,1,3,2,0:T(8,128)(2,1)} %bitcast.84) | data formatting | bytes 524288 | tf_op jit(solution)/shard_map/reshape | solution.py:138
  1.0 5.3 %attention.1 = bf16[8,128,128]{2,1,0:T(8,128)(2,1)S(1)} custom-call(s32[8]{0:T(128)} %lengths_ref.1, bf16[8,128,128]{2,1,0:T(8,128)(2,1)S(1)} %bitcast.74, bf16[2,2,8,512]{3,2,1,0:T(8,128)(2,1)} %fresh_ref.1, bf16[2,8,512,512]{3,2,1,0:T(8,128)(2,1)} %cache_ref.1), custom_call_target="tpu_custom_call" | custom-call | tf_op jit(solution)/shard_map/attention/pallas_call | solution.py:142
  7.0 1.0 %collective-permute-done = bf16[4,8,16,128]{3,2,1,0:T(8,128)(2,1)S(1)} collective-permute-done((bf16[4,8,16,128]{3,2,1,0:T(8,128)(2,1)S(1)}, bf16[4,8,16,128]{3,2,1,0:T(8,128)(2,1)S(1)}, u32[]{:S(2)}, u32[]{:S(2)}) %collective-permute-start) | collective-permute-done | bytes 131104 | tf_op jit(solution)/shard_map/ppermute | solution.py:258
  8.1 3.9 %collective-permute-start.3 = (bf16[2,8,16,128]{3,2,1,0:T(8,128)(2,1)S(1)}, bf16[2,8,16,128]{3,2,1,0:T(8,128)(2,1)S(1)}, u32[]{:S(2)}, u32[]{:S(2)}) collective-permute-start(bf16[2,8,16,128]{3,2,1,0:T(8,128)(2,1)S(1)} %get-tuple-element.50), channel_id=1, source_target_pairs={{0,6},{1,7},{2,4},{3,5},{4,2},{5,3},{6,0},{7,1},{8,14},{9,15},{10,... | collective-permute-start | bytes 196616 | tf_op jit(solution)/shard_map/ppermute | solution.py:293
  12.0 1.4 %collective-permute-start.2 = (bf16[2,8,16,128]{3,2,1,0:T(8,128)(2,1)S(1)}, bf16[2,8,16,128]{3,2,1,0:T(8,128)(2,1)S(1)}, u32[]{:S(2)}, u32[]{:S(2)}) collective-permute-start(bf16[2,8,16,128]{3,2,1,0:T(8,128)(2,1)S(1)} %get-tuple-element.51), channel_id=1, source_target_pairs={{0,4},{1,5},{2,6},{3,7},{4,0},{5,1},{6,2},{7,3},{8,12},{9,13},{10,... | collective-permute-start | bytes 196616 | tf_op jit(solution)/shard_map/ppermute | solution.py:293
  13.5 4.0 %collective-permute-start.11 = (bf16[2,8,16,128]{3,2,1,0:T(8,128)(2,1)S(1)}, bf16[2,8,16,128]{3,2,1,0:T(8,128)(2,1)S(1)}, u32[]{:S(2)}, u32[]{:S(2)}) collective-permute-start(bf16[2,8,16,128]{3,2,1,0:T(8,128)(2,1)S(1)} %get-tuple-element.50), channel_id=1, source_target_pairs={{0,14},{1,15},{2,12},{3,13},{4,10},{5,11},{6,8},{7,9},{8,6},{9,7},... | collective-permute-start | bytes 196616 | tf_op jit(solution)/shard_map/ppermute | solution.py:293
  17.5 1.2 %collective-permute-start.10 = (bf16[2,8,16,128]{3,2,1,0:T(8,128)(2,1)S(1)}, bf16[2,8,16,128]{3,2,1,0:T(8,128)(2,1)S(1)}, u32[]{:S(2)}, u32[]{:S(2)}) collective-permute-start(bf16[2,8,16,128]{3,2,1,0:T(8,128)(2,1)S(1)} %get-tuple-element.51), channel_id=1, source_target_pairs={{0,12},{1,13},{2,14},{3,15},{4,8},{5,9},{6,10},{7,11},{8,4},{9,5},... | collective-permute-start | bytes 196616 | tf_op jit(solution)/shard_map/ppermute | solution.py:293
  18.7 2.4 %collective-permute-start.8 = (bf16[2,8,16,128]{3,2,1,0:T(8,128)(2,1)S(1)}, bf16[2,8,16,128]{3,2,1,0:T(8,128)(2,1)S(1)}, u32[]{:S(2)}, u32[]{:S(2)}) collective-permute-start(bf16[2,8,16,128]{3,2,1,0:T(8,128)(2,1)S(1)} %bitcast.75), channel_id=1, source_target_pairs={{0,8},{1,9},{2,10},{3,11},{4,12},{5,13},{6,14},{7,15},{8,0},{9,1},... | collective-permute-start | bytes 196616 | tf_op jit(solution)/shard_map/ppermute | solution.py:293
  21.2 6.4 %project_near.1 = (bf16[4,16,8192]{2,1,0:T(8,128)(2,1)S(1)}, bf16[4,16,8192]{2,1,0:T(8,128)(2,1)S(1)}, bf16[1024,8192]{1,0:T(8,128)(2,1)S(1)}) custom-call(bf16[1,2,8,16,128]{4,3,2,1,0:T(8,128)(2,1)S(1)} %get-tuple-element.53.refs_0_, bf16[1,2,8,16,128]{4,3,2,1,0:T(8,128)(2,1)S(1)} %bitcast.82, bf16[1,2,8,16,128]{4,3,2,1,0:T(8,128)(2,1)S(1)} %bitcast.80, ...), custom_call_target="tpu_custom_call" | custom-call | flops 2147483648 | bytes 33554432 | tf_op jit(solution)/shard_map/project_near/pallas_call | solution.py:206
  28.5 2.4 %project_far.1 = (bf16[4,16,4096]{2,1,0:T(8,128)(2,1)S(1)}, bf16[4,16,4096]{2,1,0:T(8,128)(2,1)}, bf16[4,16,4096]{2,1,0:T(8,128)(2,1)S(1)}, bf16[4,16,4096]{2,1,0:T(8,128)(2,1)S(1)}) custom-call(bf16[1,2,8,16,128]{4,3,2,1,0:T(8,128)(2,1)S(1)} %bitcast.81, bf16[1,2,8,16,128]{4,3,2,1,0:T(8,128)(2,1)S(1)} %bitcast.78, bf16[1,2,8,16,128]{4,3,2,1,0:T(8,128)(2,1)S(1)} %bitcast.77, ...), custom_call_target="tpu_custom_call" | custom-call | flops 2147483648 | bytes 16777216 | tf_op jit(solution)/shard_map/project_far/pallas_call | solution.py:242
  32.2 2.1 %collective-permute-done.12 = bf16[4,16,4096]{2,1,0:T(8,128)(2,1)} collective-permute-done((bf16[4,16,4096]{2,1,0:T(8,128)(2,1)}, bf16[4,16,4096]{2,1,0:T(8,128)(2,1)}, u32[]{:S(2)}, u32[]{:S(2)}) %collective-permute-start.12) | collective-permute-done | bytes 524320 | tf_op jit(solution)/shard_map/ppermute | solution.py:258
  34.3 1.2 %fusion.7 = (bf16[4,16,4096]{2,1,0:T(8,128)(2,1)S(1)}, f32[4,16,4096]{2,1,0:T(8,128)S(1)}) fusion(bf16[4,16,4096]{2,1,0:T(8,128)(2,1)} %collective-permute-done.12, bf16[4,16,4096]{2,1,0:T(8,128)(2,1)S(1)} %get-tuple-element.29), kind=kLoop, calls=%fused_computation.34 | loop fusion | flops 1048576 | bytes 2621440 | tf_op jit(solution)/shard_map/convert_element_type | solution.py:266
  35.5 1.2 %collective-permute-start.13 = (bf16[16,4096]{1,0:T(8,128)(2,1)S(1)}, bf16[16,4096]{1,0:T(8,128)(2,1)S(1)}, u32[]{:S(2)}, u32[]{:S(2)}) collective-permute-start(bf16[16,4096]{1,0:T(8,128)(2,1)S(1)} %get-tuple-element.44), channel_id=1, source_target_pairs={{0,2},{1,3},{2,0},{3,1},{4,6},{5,7},{6,4},{7,5},{8,10},{9,11},{10,... | collective-permute-start | bytes 393224 | tf_op jit(solution)/shard_map/ppermute | solution.py:258
  37.4 1.7 %collective-permute-start.14 = (bf16[16,4096]{1,0:T(8,128)(2,1)S(1)}, bf16[16,4096]{1,0:T(8,128)(2,1)S(1)}, u32[]{:S(2)}, u32[]{:S(2)}) collective-permute-start(bf16[16,4096]{1,0:T(8,128)(2,1)S(1)} %get-tuple-element.46), channel_id=1, source_target_pairs={{0,4},{1,5},{2,6},{3,7},{4,0},{5,1},{6,2},{7,3},{8,12},{9,13},{10,... | collective-permute-start | bytes 393224 | tf_op jit(solution)/shard_map/ppermute | solution.py:258
  39.3 1.2 %collective-permute-start.18 = (bf16[16,4096]{1,0:T(8,128)(2,1)S(1)}, bf16[16,4096]{1,0:T(8,128)(2,1)S(1)}, u32[]{:S(2)}, u32[]{:S(2)}) collective-permute-start(bf16[16,4096]{1,0:T(8,128)(2,1)S(1)} %get-tuple-element.47), channel_id=1, source_target_pairs={{0,2},{1,3},{2,0},{3,1},{4,6},{5,7},{6,4},{7,5},{8,10},{9,11},{10,... | collective-permute-start | bytes 393224 | tf_op jit(solution)/shard_map/ppermute | solution.py:258
  40.4 4.3 %collective-permute-done.13 = bf16[16,4096]{1,0:T(8,128)(2,1)S(1)} collective-permute-done((bf16[16,4096]{1,0:T(8,128)(2,1)S(1)}, bf16[16,4096]{1,0:T(8,128)(2,1)S(1)}, u32[]{:S(2)}, u32[]{:S(2)}) %collective-permute-start.13) | collective-permute-done | bytes 131104 | tf_op jit(solution)/shard_map/ppermute | solution.py:258
  45.6 1.8 %collective-permute-start.19 = (bf16[16,4096]{1,0:T(8,128)(2,1)S(1)}, bf16[16,4096]{1,0:T(8,128)(2,1)S(1)}, u32[]{:S(2)}, u32[]{:S(2)}) collective-permute-start(bf16[16,4096]{1,0:T(8,128)(2,1)S(1)} %get-tuple-element.49), channel_id=1, source_target_pairs={{0,4},{1,5},{2,6},{3,7},{4,0},{5,1},{6,2},{7,3},{8,12},{9,13},{10,... | collective-permute-start | bytes 393224 | tf_op jit(solution)/shard_map/ppermute | solution.py:258
  47.4 1.2 %collective-permute-start.16 = (bf16[16,4096]{1,0:T(8,128)(2,1)S(1)}, bf16[16,4096]{1,0:T(8,128)(2,1)S(1)}, u32[]{:S(2)}, u32[]{:S(2)}) collective-permute-start(bf16[16,4096]{1,0:T(8,128)(2,1)S(1)} %fusion.6), channel_id=1, source_target_pairs={{0,8},{1,9},{2,10},{3,11},{4,12},{5,13},{6,14},{7,15},{8,0},{9,1},... | collective-permute-start | bytes 393224 | tf_op jit(solution)/shard_map/ppermute | solution.py:293
  49.0 1.0 %collective-permute-start.5 = (bf16[16,8192]{1,0:T(8,128)(2,1)S(1)}, bf16[16,8192]{1,0:T(8,128)(2,1)S(1)}, u32[]{:S(2)}, u32[]{:S(2)}) collective-permute-start(bf16[16,8192]{1,0:T(8,128)(2,1)S(1)} %get-tuple-element.35), channel_id=1, source_target_pairs={{0,2},{1,3},{2,0},{3,1},{4,6},{5,7},{6,4},{7,5},{8,10},{9,11},{10,... | collective-permute-start | bytes 786440 | tf_op jit(solution)/shard_map/ppermute | solution.py:258
  50.0 2.5 %collective-permute-start.7 = (bf16[16,8192]{1,0:T(8,128)(2,1)S(1)}, bf16[16,8192]{1,0:T(8,128)(2,1)S(1)}, u32[]{:S(2)}, u32[]{:S(2)}) collective-permute-start(bf16[16,8192]{1,0:T(8,128)(2,1)S(1)} %get-tuple-element.36), channel_id=1, source_target_pairs={{0,6},{1,7},{2,4},{3,5},{4,2},{5,3},{6,0},{7,1},{8,14},{9,15},{10,... | collective-permute-start | bytes 786440 | tf_op jit(solution)/shard_map/ppermute | solution.py:258
  52.5 3.0 %collective-permute-done.20 = bf16[16,4096]{1,0:T(8,128)(2,1)S(1)} collective-permute-done((bf16[16,4096]{1,0:T(8,128)(2,1)S(1)}, bf16[16,4096]{1,0:T(8,128)(2,1)S(1)}, u32[]{:S(2)}, u32[]{:S(2)}) %collective-permute-start.20) | collective-permute-done | bytes 131104 | tf_op jit(solution)/shard_map/ppermute | solution.py:258
  55.6 2.7 %collective-permute-done.19 = bf16[16,4096]{1,0:T(8,128)(2,1)S(1)} collective-permute-done((bf16[16,4096]{1,0:T(8,128)(2,1)S(1)}, bf16[16,4096]{1,0:T(8,128)(2,1)S(1)}, u32[]{:S(2)}, u32[]{:S(2)}) %collective-permute-start.19) | collective-permute-done | bytes 131104 | tf_op jit(solution)/shard_map/ppermute | solution.py:258
  59.1 6.4 %collective-permute-done.7 = bf16[16,8192]{1,0:T(8,128)(2,1)S(1)} collective-permute-done((bf16[16,8192]{1,0:T(8,128)(2,1)S(1)}, bf16[16,8192]{1,0:T(8,128)(2,1)S(1)}, u32[]{:S(2)}, u32[]{:S(2)}) %collective-permute-start.7) | collective-permute-done | bytes 262176 | tf_op jit(solution)/shard_map/ppermute | solution.py:258
  65.5 2.8 %collective-permute-done.6 = bf16[16,8192]{1,0:T(8,128)(2,1)S(1)} collective-permute-done((bf16[16,8192]{1,0:T(8,128)(2,1)S(1)}, bf16[16,8192]{1,0:T(8,128)(2,1)S(1)}, u32[]{:S(2)}, u32[]{:S(2)}) %collective-permute-start.6) | collective-permute-done | bytes 262176 | tf_op jit(solution)/shard_map/ppermute | solution.py:258
  (42 shorter events, 7.0 us)
Async XLA Ops:
  6.5 1.5 %collective-permute-start = (bf16[4,8,16,128]{3,2,1,0:T(8,128)(2,1)S(1)}, bf16[4,8,16,128]{3,2,1,0:T(8,128)(2,1)S(1)}, u32[]{:S(2)}, u32[]{:S(2)}) collective-permute-start(bf16[4,8,16,128]{3,2,1,0:T(8,128)(2,1)S(1)} %get-tuple-element.55), channel_id=1, source_target_pairs={{0,1},{1,0},{2,3},{3,2},{4,5},{5,4},{6,7},{7,6},{8,9},{9,8},{10,11... | collective-permute-start | bytes 393224 | tf_op jit(solution)/shard_map/ppermute | solution.py:258
  8.1 10.7 %collective-permute-start.3 = (bf16[2,8,16,128]{3,2,1,0:T(8,128)(2,1)S(1)}, bf16[2,8,16,128]{3,2,1,0:T(8,128)(2,1)S(1)}, u32[]{:S(2)}, u32[]{:S(2)}) collective-permute-start(bf16[2,8,16,128]{3,2,1,0:T(8,128)(2,1)S(1)} %get-tuple-element.50), channel_id=1, source_target_pairs={{0,6},{1,7},{2,4},{3,5},{4,2},{5,3},{6,0},{7,1},{8,14},{9,15},{10,... | collective-permute-start | bytes 196616 | tf_op jit(solution)/shard_map/ppermute | solution.py:293
  12.0 6.7 %collective-permute-start.2 = (bf16[2,8,16,128]{3,2,1,0:T(8,128)(2,1)S(1)}, bf16[2,8,16,128]{3,2,1,0:T(8,128)(2,1)S(1)}, u32[]{:S(2)}, u32[]{:S(2)}) collective-permute-start(bf16[2,8,16,128]{3,2,1,0:T(8,128)(2,1)S(1)} %get-tuple-element.51), channel_id=1, source_target_pairs={{0,4},{1,5},{2,6},{3,7},{4,0},{5,1},{6,2},{7,3},{8,12},{9,13},{10,... | collective-permute-start | bytes 196616 | tf_op jit(solution)/shard_map/ppermute | solution.py:293
  13.4 7.7 %collective-permute-start.1 = (bf16[2,8,16,128]{3,2,1,0:T(8,128)(2,1)S(1)}, bf16[2,8,16,128]{3,2,1,0:T(8,128)(2,1)S(1)}, u32[]{:S(2)}, u32[]{:S(2)}) collective-permute-start(bf16[2,8,16,128]{3,2,1,0:T(8,128)(2,1)S(1)} %get-tuple-element.52), channel_id=1, source_target_pairs={{0,2},{1,3},{2,0},{3,1},{4,6},{5,7},{6,4},{7,5},{8,10},{9,11},{10,... | collective-permute-start | bytes 196616 | tf_op jit(solution)/shard_map/ppermute | solution.py:293
  13.5 15.0 %collective-permute-start.11 = (bf16[2,8,16,128]{3,2,1,0:T(8,128)(2,1)S(1)}, bf16[2,8,16,128]{3,2,1,0:T(8,128)(2,1)S(1)}, u32[]{:S(2)}, u32[]{:S(2)}) collective-permute-start(bf16[2,8,16,128]{3,2,1,0:T(8,128)(2,1)S(1)} %get-tuple-element.50), channel_id=1, source_target_pairs={{0,14},{1,15},{2,12},{3,13},{4,10},{5,11},{6,8},{7,9},{8,6},{9,7},... | collective-permute-start | bytes 196616 | tf_op jit(solution)/shard_map/ppermute | solution.py:293
  17.5 11.0 %collective-permute-start.10 = (bf16[2,8,16,128]{3,2,1,0:T(8,128)(2,1)S(1)}, bf16[2,8,16,128]{3,2,1,0:T(8,128)(2,1)S(1)}, u32[]{:S(2)}, u32[]{:S(2)}) collective-permute-start(bf16[2,8,16,128]{3,2,1,0:T(8,128)(2,1)S(1)} %get-tuple-element.51), channel_id=1, source_target_pairs={{0,12},{1,13},{2,14},{3,15},{4,8},{5,9},{6,10},{7,11},{8,4},{9,5},... | collective-permute-start | bytes 196616 | tf_op jit(solution)/shard_map/ppermute | solution.py:293
  18.7 9.8 %collective-permute-start.9 = (bf16[2,8,16,128]{3,2,1,0:T(8,128)(2,1)S(1)}, bf16[2,8,16,128]{3,2,1,0:T(8,128)(2,1)S(1)}, u32[]{:S(2)}, u32[]{:S(2)}) collective-permute-start(bf16[2,8,16,128]{3,2,1,0:T(8,128)(2,1)S(1)} %get-tuple-element.52), channel_id=1, source_target_pairs={{0,10},{1,11},{2,8},{3,9},{4,14},{5,15},{6,12},{7,13},{8,2},{9,3},... | collective-permute-start | bytes 196616 | tf_op jit(solution)/shard_map/ppermute | solution.py:293
  18.7 9.8 %collective-permute-start.8 = (bf16[2,8,16,128]{3,2,1,0:T(8,128)(2,1)S(1)}, bf16[2,8,16,128]{3,2,1,0:T(8,128)(2,1)S(1)}, u32[]{:S(2)}, u32[]{:S(2)}) collective-permute-start(bf16[2,8,16,128]{3,2,1,0:T(8,128)(2,1)S(1)} %bitcast.75), channel_id=1, source_target_pairs={{0,8},{1,9},{2,10},{3,11},{4,12},{5,13},{6,14},{7,15},{8,0},{9,1},... | collective-permute-start | bytes 196616 | tf_op jit(solution)/shard_map/ppermute | solution.py:293
  30.9 0.8 %copy-start = (bf16[4,16,4096]{2,1,0:T(8,128)(2,1)}, bf16[4,16,4096]{2,1,0:T(8,128)(2,1)S(1)}, u32[]{:S(2)}) copy-start(bf16[4,16,4096]{2,1,0:T(8,128)(2,1)S(1)} %get-tuple-element.32) | copy-start | bytes 1572868
  31.7 2.6 %collective-permute-start.12 = (bf16[4,16,4096]{2,1,0:T(8,128)(2,1)}, bf16[4,16,4096]{2,1,0:T(8,128)(2,1)}, u32[]{:S(2)}, u32[]{:S(2)}) collective-permute-start(bf16[4,16,4096]{2,1,0:T(8,128)(2,1)} %get-tuple-element.30), channel_id=1, source_target_pairs={{0,1},{1,0},{2,3},{3,2},{4,5},{5,4},{6,7},{7,6},{8,9},{9,8},{10,11... | collective-permute-start | bytes 1572872 | tf_op jit(solution)/shard_map/ppermute | solution.py:258
  31.7 7.4 %collective-permute-start.17 = (bf16[4,16,4096]{2,1,0:T(8,128)(2,1)}, bf16[4,16,4096]{2,1,0:T(8,128)(2,1)S(1)}, u32[]{:S(2)}, u32[]{:S(2)}) collective-permute-start(bf16[4,16,4096]{2,1,0:T(8,128)(2,1)} %copy-done), channel_id=1, source_target_pairs={{0,1},{1,0},{2,3},{3,2},{4,5},{5,4},{6,7},{7,6},{8,9},{9,8},{10,11... | collective-permute-start | bytes 1572872 | tf_op jit(solution)/shard_map/ppermute | solution.py:258
  32.2 16.4 %collective-permute-start.4 = (bf16[4,16,8192]{2,1,0:T(8,128)(2,1)S(1)}, bf16[4,16,8192]{2,1,0:T(8,128)(2,1)S(1)}, u32[]{:S(2)}, u32[]{:S(2)}) collective-permute-start(bf16[4,16,8192]{2,1,0:T(8,128)(2,1)S(1)} %get-tuple-element.22), channel_id=1, source_target_pairs={{0,1},{1,0},{2,3},{3,2},{4,5},{5,4},{6,7},{7,6},{8,9},{9,8},{10,11... | collective-permute-start | bytes 3145736 | tf_op jit(solution)/shard_map/ppermute | solution.py:258
  35.5 9.2 %collective-permute-start.13 = (bf16[16,4096]{1,0:T(8,128)(2,1)S(1)}, bf16[16,4096]{1,0:T(8,128)(2,1)S(1)}, u32[]{:S(2)}, u32[]{:S(2)}) collective-permute-start(bf16[16,4096]{1,0:T(8,128)(2,1)S(1)} %get-tuple-element.44), channel_id=1, source_target_pairs={{0,2},{1,3},{2,0},{3,1},{4,6},{5,7},{6,4},{7,5},{8,10},{9,11},{10,... | collective-permute-start | bytes 393224 | tf_op jit(solution)/shard_map/ppermute | solution.py:258
  36.7 8.9 %collective-permute-start.15 = (bf16[16,4096]{1,0:T(8,128)(2,1)S(1)}, bf16[16,4096]{1,0:T(8,128)(2,1)S(1)}, u32[]{:S(2)}, u32[]{:S(2)}) collective-permute-start(bf16[16,4096]{1,0:T(8,128)(2,1)S(1)} %get-tuple-element.45), channel_id=1, source_target_pairs={{0,6},{1,7},{2,4},{3,5},{4,2},{5,3},{6,0},{7,1},{8,14},{9,15},{10,... | collective-permute-start | bytes 393224 | tf_op jit(solution)/shard_map/ppermute | solution.py:258
  37.4 9.9 %collective-permute-start.14 = (bf16[16,4096]{1,0:T(8,128)(2,1)S(1)}, bf16[16,4096]{1,0:T(8,128)(2,1)S(1)}, u32[]{:S(2)}, u32[]{:S(2)}) collective-permute-start(bf16[16,4096]{1,0:T(8,128)(2,1)S(1)} %get-tuple-element.46), channel_id=1, source_target_pairs={{0,4},{1,5},{2,6},{3,7},{4,0},{5,1},{6,2},{7,3},{8,12},{9,13},{10,... | collective-permute-start | bytes 393224 | tf_op jit(solution)/shard_map/ppermute | solution.py:258
  39.3 10.7 %collective-permute-start.18 = (bf16[16,4096]{1,0:T(8,128)(2,1)S(1)}, bf16[16,4096]{1,0:T(8,128)(2,1)S(1)}, u32[]{:S(2)}, u32[]{:S(2)}) collective-permute-start(bf16[16,4096]{1,0:T(8,128)(2,1)S(1)} %get-tuple-element.47), channel_id=1, source_target_pairs={{0,2},{1,3},{2,0},{3,1},{4,6},{5,7},{6,4},{7,5},{8,10},{9,11},{10,... | collective-permute-start | bytes 393224 | tf_op jit(solution)/shard_map/ppermute | solution.py:258
  44.7 10.8 %collective-permute-start.20 = (bf16[16,4096]{1,0:T(8,128)(2,1)S(1)}, bf16[16,4096]{1,0:T(8,128)(2,1)S(1)}, u32[]{:S(2)}, u32[]{:S(2)}) collective-permute-start(bf16[16,4096]{1,0:T(8,128)(2,1)S(1)} %get-tuple-element.48), channel_id=1, source_target_pairs={{0,6},{1,7},{2,4},{3,5},{4,2},{5,3},{6,0},{7,1},{8,14},{9,15},{10,... | collective-permute-start | bytes 393224 | tf_op jit(solution)/shard_map/ppermute | solution.py:258
  45.6 12.7 %collective-permute-start.19 = (bf16[16,4096]{1,0:T(8,128)(2,1)S(1)}, bf16[16,4096]{1,0:T(8,128)(2,1)S(1)}, u32[]{:S(2)}, u32[]{:S(2)}) collective-permute-start(bf16[16,4096]{1,0:T(8,128)(2,1)S(1)} %get-tuple-element.49), channel_id=1, source_target_pairs={{0,4},{1,5},{2,6},{3,7},{4,0},{5,1},{6,2},{7,3},{8,12},{9,13},{10,... | collective-permute-start | bytes 393224 | tf_op jit(solution)/shard_map/ppermute | solution.py:258
  47.4 21.0 %collective-permute-start.16 = (bf16[16,4096]{1,0:T(8,128)(2,1)S(1)}, bf16[16,4096]{1,0:T(8,128)(2,1)S(1)}, u32[]{:S(2)}, u32[]{:S(2)}) collective-permute-start(bf16[16,4096]{1,0:T(8,128)(2,1)S(1)} %fusion.6), channel_id=1, source_target_pairs={{0,8},{1,9},{2,10},{3,11},{4,12},{5,13},{6,14},{7,15},{8,0},{9,1},... | collective-permute-start | bytes 393224 | tf_op jit(solution)/shard_map/ppermute | solution.py:293
  49.0 10.1 %collective-permute-start.5 = (bf16[16,8192]{1,0:T(8,128)(2,1)S(1)}, bf16[16,8192]{1,0:T(8,128)(2,1)S(1)}, u32[]{:S(2)}, u32[]{:S(2)}) collective-permute-start(bf16[16,8192]{1,0:T(8,128)(2,1)S(1)} %get-tuple-element.35), channel_id=1, source_target_pairs={{0,2},{1,3},{2,0},{3,1},{4,6},{5,7},{6,4},{7,5},{8,10},{9,11},{10,... | collective-permute-start | bytes 786440 | tf_op jit(solution)/shard_map/ppermute | solution.py:258
  50.0 15.5 %collective-permute-start.7 = (bf16[16,8192]{1,0:T(8,128)(2,1)S(1)}, bf16[16,8192]{1,0:T(8,128)(2,1)S(1)}, u32[]{:S(2)}, u32[]{:S(2)}) collective-permute-start(bf16[16,8192]{1,0:T(8,128)(2,1)S(1)} %get-tuple-element.36), channel_id=1, source_target_pairs={{0,6},{1,7},{2,4},{3,5},{4,2},{5,3},{6,0},{7,1},{8,14},{9,15},{10,... | collective-permute-start | bytes 786440 | tf_op jit(solution)/shard_map/ppermute | solution.py:258
  55.5 12.7 %collective-permute-start.6 = (bf16[16,8192]{1,0:T(8,128)(2,1)S(1)}, bf16[16,8192]{1,0:T(8,128)(2,1)S(1)}, u32[]{:S(2)}, u32[]{:S(2)}) collective-permute-start(bf16[16,8192]{1,0:T(8,128)(2,1)S(1)} %get-tuple-element.37), channel_id=1, source_target_pairs={{0,4},{1,5},{2,6},{3,7},{4,0},{5,1},{6,2},{7,3},{8,12},{9,13},{10,... | collective-permute-start | bytes 786440 | tf_op jit(solution)/shard_map/ppermute | solution.py:258
  58.3 10.1 %collective-permute-start.21 = (bf16[16,4096]{1,0:T(8,128)(2,1)S(1)}, bf16[16,4096]{1,0:T(8,128)(2,1)S(1)}, u32[]{:S(2)}, u32[]{:S(2)}) collective-permute-start(bf16[16,4096]{1,0:T(8,128)(2,1)S(1)} %fusion.4), channel_id=1, source_target_pairs={{0,8},{1,9},{2,10},{3,11},{4,12},{5,13},{6,14},{7,15},{8,0},{9,1},... | collective-permute-start | bytes 393224 | tf_op jit(solution)/shard_map/ppermute | solution.py:293

commit v4 on v3

--- a/solution.py
+++ b/solution.py
@@ -15,7 +15,8 @@
 GRID_ROWS = 8
 GROUP = QH // KVH
 BLOCK_HEADS = QH // GRID_ROWS
-CHUNKS = 2
+CHUNKS = 1
+SENDS = 2
 TILE_N = 1024
 PAGE = 128
 TOGETHER = 4
@@ -262,16 +263,14 @@
     return value.astype(jnp.float32)
 
 
-def direct(total):
-    sent = total.astype(jnp.bfloat16)
-    arrived = [swap(sent[i], 2 * i) for i in range(1, 4)]
-    return total[0] + sum(widen(value) for value in arrived)
-
-
-def stepwise(total):
-    total = total.reshape((2, 2) + total.shape[1:])
-    total = total[:, 0] + widen(swap(total[:, 1].astype(jnp.bfloat16), 2))
-    return total[0] + widen(swap(total[1].astype(jnp.bfloat16), 4))
+def pair_sums(keep, arrived):
+    sums = [widen(keep[i]) + widen(arrived[i]) for i in range(4)]
+    return sums[0], [value.astype(jnp.bfloat16) for value in sums[1:]]
+
+
+def direct(own, sent):
+    arrived = [swap(value, 2 * (i + 1)) for i, value in enumerate(sent)]
+    return (own + sum(widen(value) for value in arrived)).astype(jnp.bfloat16)
 
 
 def per_device(queries, fresh_kv, cache, lengths, out_weight):
@@ -309,16 +308,19 @@
     ]
     near = [(send(cat[i], 0, 2 * i) if i else cat[0])[None] for i in range(4)]
     near_keep, near_give, weight = project_near(near, weight)
-    far, weight = lax.optimization_barrier((far, weight))
+    far, weight, near_give = lax.optimization_barrier((far, weight, near_give))
     partial = project_far(far, weight)
-    near_total = widen(near_keep) + widen(swap(near_give, 1))
+    near = pair_sums(near_keep, swap(near_give, 1))
+    far = pair_sums(partial[0], swap(partial[1], 1))
+    far, near = lax.optimization_barrier((far, near))
     backs = []
-    for chunk in range(CHUNKS):
-        keep, give = partial[2 * chunk : 2 * chunk + 2]
-        sums = direct(widen(keep) + widen(swap(give, 1))).astype(jnp.bfloat16)
+    width = col_width // SENDS
+    for first in range(0, col_width, width):
+        lanes = slice(first, first + width)
+        sums = direct(far[0][:, lanes], [value[:, lanes] for value in far[1]])
         sums = sums.reshape(cols - 1, slot_rows, -1)
         backs.append(jnp.stack([send(sums[s - 1], cols - s, 0) for s in range(1, cols)]))
-    near = direct(near_total).astype(jnp.bfloat16)
+    near = direct(*near)
     stacked = jnp.concatenate([near[None], jnp.concatenate(backs, axis=-1)])
     blocks = [
         lax.dynamic_index_in_dim(stacked, lax.rem(j - own_block + cols, cols), 0, False)

time: 69.5 us -> 68.5 us (0.986)
  waiting for transfers between devices: 23.3 us -> 26.4 us
  starting transfers between devices: 26.9 us -> 25.4 us
  other arithmetic: 2.73 us -> 1.61 us
  local copies, waits for them, and re-layouts: 2.13 us -> 1.29 us
    ppermute x13 -> x12, starting transfers between devices: 11.9 us -> 9.49 us  [swap(): lax.ppermute(value, 'tile', [(i, i ^ distance) for i in range(devices)])]
    ppermute x9, waiting for transfers between devices: 0.93 us -> 2.54 us  [send(): return lax.ppermute(value, 'tile', [(i, target(i)) for i in range(devices)])]
    ppermute x13 -> x12, waiting for transfers between devices: 22.4 us -> 23.9 us  [swap(): lax.ppermute(value, 'tile', [(i, i ^ distance) for i in range(devices)])]
    convert_element_type x4 -> x3, other arithmetic: 1.43 us -> 0.58 us  [the longest x2 0.46 us: pair_sums(): return (sums[0], [value.astype(jnp.bfloat16) for value in sums[1:]])]
    ppermute x9, starting transfers between devices: 15.1 us -> 15.9 us  [send(): return lax.ppermute(value, 'tile', [(i, target(i)) for i in range(devices)])]
    unnamed x2 -> x0, local copies, waits for them, and re-layouts: 0.78 us -> none
  transfers between devices with their start and end apart: 22 -> 21, of which waited for: 8 -> 10; matrix products, arithmetic and copies ran while one was open for 3% -> 1% of each run, Pallas kernels for 9% -> 13%
where the time goes in v4:
time: 68.5 us
  waiting for transfers between devices  26.4 us (39%)
  starting transfers between devices  25.4 us (37%)
  Pallas kernels  13.7 us (20%)
  other arithmetic  1.61 us (2%)
  local copies, waits for them, and re-layouts  1.29 us (2%)
    ppermute x12, waiting for transfers between devices, swap(): lax.ppermute(value, 'tile', [(i, i ^ distance) for i in range(devices)])  23.9 us
    ppermute x9, starting transfers between devices, send(): return lax.ppermute(value, 'tile', [(i, target(i)) for i in range(devices)])  15.9 us
    ppermute x12, starting transfers between devices, swap(): lax.ppermute(value, 'tile', [(i, i ^ distance) for i in range(devices)])  9.49 us
    pallas_call x1, Pallas kernels, project_near(): pl.pallas_call(near_kernel, in_specs=[vmem] * 4 + [pl.BlockSpec(memory_sp...  6.44 us
    pallas_call x1, Pallas kernels, attend(): pl.pallas_call(attention_kernel, out_shape=jax.ShapeDtypeStruct((slots, r...  4.9 us
    ppermute x9, waiting for transfers between devices, send(): return lax.ppermute(value, 'tile', [(i, target(i)) for i in range(devices)])  2.54 us
    pallas_call x1, Pallas kernels, project_far(): pl.pallas_call(far_kernel, in_specs=[vmem] * 5, out_specs=[vmem] * (2 * C...  2.36 us
  transfers between devices with their start and end apart: 21, of which 10 were waited for; matrix products, arithmetic and copies ran while one was open for 1% of the time, Pallas kernels for 13%

profile of v4, /device:TPU:0, one launch (start us, length us, event | category | flops | bytes accessed | tf_op | source)
XLA Modules:
  0.0 68.5 jit_solution(5911731527611027934)
XLA Ops:
  0.0 1.0 %copy.6 = bf16[2,8,4,16,128]{4,3,0,2,1:T(8,128)(2,1)S(1)} copy(bf16[2,8,4,16,128]{4,1,3,2,0:T(8,128)(2,1)} %bitcast.62) | data formatting | bytes 524288 | tf_op jit(solution)/shard_map/reshape | solution.py:139
  1.0 4.9 %attention.1 = bf16[8,128,128]{2,1,0:T(8,128)(2,1)S(1)} custom-call(s32[8]{0:T(128)} %lengths_ref.1, bf16[8,128,128]{2,1,0:T(8,128)(2,1)S(1)} %bitcast.52, bf16[2,2,8,512]{3,2,1,0:T(8,128)(2,1)} %fresh_ref.1, bf16[2,8,512,512]{3,2,1,0:T(8,128)(2,1)} %cache_ref.1), custom_call_target="tpu_custom_call" | custom-call | tf_op jit(solution)/shard_map/attention/pallas_call | solution.py:143
  6.5 1.0 %collective-permute-done = bf16[4,8,16,128]{3,2,1,0:T(8,128)(2,1)S(1)} collective-permute-done((bf16[4,8,16,128]{3,2,1,0:T(8,128)(2,1)S(1)}, bf16[4,8,16,128]{3,2,1,0:T(8,128)(2,1)S(1)}, u32[]{:S(2)}, u32[]{:S(2)}) %collective-permute-start) | collective-permute-done | bytes 131104 | tf_op jit(solution)/shard_map/ppermute | solution.py:259
  7.6 4.4 %collective-permute-start.5 = (bf16[2,8,16,128]{3,2,1,0:T(8,128)(2,1)S(1)}, bf16[2,8,16,128]{3,2,1,0:T(8,128)(2,1)S(1)}, u32[]{:S(2)}, u32[]{:S(2)}) collective-permute-start(bf16[2,8,16,128]{3,2,1,0:T(8,128)(2,1)S(1)} %get-tuple-element.67), channel_id=1, source_target_pairs={{0,2},{1,3},{2,0},{3,1},{4,6},{5,7},{6,4},{7,5},{8,10},{9,11},{10,... | collective-permute-start | bytes 196616 | tf_op jit(solution)/shard_map/ppermute | solution.py:292
  12.0 1.1 %collective-permute-start.6 = (bf16[2,8,16,128]{3,2,1,0:T(8,128)(2,1)S(1)}, bf16[2,8,16,128]{3,2,1,0:T(8,128)(2,1)S(1)}, u32[]{:S(2)}, u32[]{:S(2)}) collective-permute-start(bf16[2,8,16,128]{3,2,1,0:T(8,128)(2,1)S(1)} %get-tuple-element.66), channel_id=1, source_target_pairs={{0,4},{1,5},{2,6},{3,7},{4,0},{5,1},{6,2},{7,3},{8,12},{9,13},{10,... | collective-permute-start | bytes 196616 | tf_op jit(solution)/shard_map/ppermute | solution.py:292
  13.5 3.4 %collective-permute-start.2 = (bf16[2,8,16,128]{3,2,1,0:T(8,128)(2,1)S(1)}, bf16[2,8,16,128]{3,2,1,0:T(8,128)(2,1)S(1)}, u32[]{:S(2)}, u32[]{:S(2)}) collective-permute-start(bf16[2,8,16,128]{3,2,1,0:T(8,128)(2,1)S(1)} %get-tuple-element.67), channel_id=1, source_target_pairs={{0,10},{1,11},{2,8},{3,9},{4,14},{5,15},{6,12},{7,13},{8,2},{9,3},... | collective-permute-start | bytes 196616 | tf_op jit(solution)/shard_map/ppermute | solution.py:292
  17.0 1.4 %collective-permute-start.3 = (bf16[2,8,16,128]{3,2,1,0:T(8,128)(2,1)S(1)}, bf16[2,8,16,128]{3,2,1,0:T(8,128)(2,1)S(1)}, u32[]{:S(2)}, u32[]{:S(2)}) collective-permute-start(bf16[2,8,16,128]{3,2,1,0:T(8,128)(2,1)S(1)} %get-tuple-element.66), channel_id=1, source_target_pairs={{0,12},{1,13},{2,14},{3,15},{4,8},{5,9},{6,10},{7,11},{8,4},{9,5},... | collective-permute-start | bytes 196616 | tf_op jit(solution)/shard_map/ppermute | solution.py:292
  18.3 2.2 %collective-permute-start.4 = (bf16[2,8,16,128]{3,2,1,0:T(8,128)(2,1)S(1)}, bf16[2,8,16,128]{3,2,1,0:T(8,128)(2,1)S(1)}, u32[]{:S(2)}, u32[]{:S(2)}) collective-permute-start(bf16[2,8,16,128]{3,2,1,0:T(8,128)(2,1)S(1)} %get-tuple-element.65), channel_id=1, source_target_pairs={{0,14},{1,15},{2,12},{3,13},{4,10},{5,11},{6,8},{7,9},{8,6},{9,7},... | collective-permute-start | bytes 196616 | tf_op jit(solution)/shard_map/ppermute | solution.py:292
  20.5 6.4 %project_near.1 = (bf16[4,16,8192]{2,1,0:T(8,128)(2,1)S(1)}, bf16[4,16,8192]{2,1,0:T(8,128)(2,1)S(1)}, bf16[1024,8192]{1,0:T(8,128)(2,1)S(1)}) custom-call(bf16[1,2,8,16,128]{4,3,2,1,0:T(8,128)(2,1)S(1)} %get-tuple-element.68.refs_0_, bf16[1,2,8,16,128]{4,3,2,1,0:T(8,128)(2,1)S(1)} %bitcast.57, bf16[1,2,8,16,128]{4,3,2,1,0:T(8,128)(2,1)S(1)} %bitcast.59, ...), custom_call_target="tpu_custom_call" | custom-call | flops 2147483648 | bytes 33554432 | tf_op jit(solution)/shard_map/project_near/pallas_call | solution.py:207
  27.0 2.5 %collective-permute-done.1 = bf16[2,8,16,128]{3,2,1,0:T(8,128)(2,1)S(1)} collective-permute-done((bf16[2,8,16,128]{3,2,1,0:T(8,128)(2,1)S(1)}, bf16[2,8,16,128]{3,2,1,0:T(8,128)(2,1)S(1)}, u32[]{:S(2)}, u32[]{:S(2)}) %collective-permute-start.1) | collective-permute-done | bytes 65568 | tf_op jit(solution)/shard_map/ppermute | solution.py:292
  29.5 2.4 %project_far.1 = (bf16[4,16,8192]{2,1,0:T(8,128)(2,1)S(1)}, bf16[4,16,8192]{2,1,0:T(8,128)(2,1)S(1)}) custom-call(bf16[1,2,8,16,128]{4,3,2,1,0:T(8,128)(2,1)S(1)} %bitcast.58, bf16[1,2,8,16,128]{4,3,2,1,0:T(8,128)(2,1)S(1)} %bitcast.54, bf16[1,2,8,16,128]{4,3,2,1,0:T(8,128)(2,1)S(1)} %bitcast.55, bf16[1,2,8,16,128]{4,3,2,1,0:T(8,128)(2,1)S(1)} %bitcast.56, ...), custom_call_target="tpu_custom_call" | custom-call | flops 2147483648 | bytes 16777216 | tf_op jit(solution)/shard_map/project_far/pallas_call | solution.py:243
  32.7 2.0 %collective-permute-done.8 = bf16[4,16,8192]{2,1,0:T(8,128)(2,1)S(1)} collective-permute-done((bf16[4,16,8192]{2,1,0:T(8,128)(2,1)S(1)}, bf16[4,16,8192]{2,1,0:T(8,128)(2,1)S(1)}, u32[]{:S(2)}, u32[]{:S(2)}) %collective-permute-start.8) | collective-permute-done | bytes 1048608 | tf_op jit(solution)/shard_map/ppermute | solution.py:259
  35.6 0.8 %collective-permute-start.14 = (bf16[16,4096]{1,0:T(8,128)(2,1)S(1)}, bf16[16,4096]{1,0:T(8,128)(2,1)S(1)}, u32[]{:S(2)}, u32[]{:S(2)}) collective-permute-start(bf16[16,4096]{1,0:T(8,128)(2,1)S(1)} %get-tuple-element.61), channel_id=1, source_target_pairs={{0,4},{1,5},{2,6},{3,7},{4,0},{5,1},{6,2},{7,3},{8,12},{9,13},{10,... | collective-permute-start | bytes 393224 | tf_op jit(solution)/shard_map/ppermute | solution.py:259
  36.4 2.3 %collective-permute-start.15 = (bf16[16,4096]{1,0:T(8,128)(2,1)S(1)}, bf16[16,4096]{1,0:T(8,128)(2,1)S(1)}, u32[]{:S(2)}, u32[]{:S(2)}) collective-permute-start(bf16[16,4096]{1,0:T(8,128)(2,1)S(1)} %get-tuple-element.63), channel_id=1, source_target_pairs={{0,6},{1,7},{2,4},{3,5},{4,2},{5,3},{6,0},{7,1},{8,14},{9,15},{10,... | collective-permute-start | bytes 393224 | tf_op jit(solution)/shard_map/ppermute | solution.py:259
  40.0 0.9 %collective-permute-done.13 = bf16[16,4096]{1,0:T(8,128)(2,1)S(1)} collective-permute-done((bf16[16,4096]{1,0:T(8,128)(2,1)S(1)}, bf16[16,4096]{1,0:T(8,128)(2,1)S(1)}, u32[]{:S(2)}, u32[]{:S(2)}) %collective-permute-start.13) | collective-permute-done | bytes 131104 | tf_op jit(solution)/shard_map/ppermute | solution.py:259
  40.8 1.4 %collective-permute-start.19 = (bf16[16,4096]{1,0:T(8,128)(2,1)S(1)}, bf16[16,4096]{1,0:T(8,128)(2,1)S(1)}, u32[]{:S(2)}, u32[]{:S(2)}) collective-permute-start(bf16[16,4096]{1,0:T(8,128)(2,1)S(1)} %get-tuple-element.64), channel_id=1, source_target_pairs={{0,6},{1,7},{2,4},{3,5},{4,2},{5,3},{6,0},{7,1},{8,14},{9,15},{10,... | collective-permute-start | bytes 393224 | tf_op jit(solution)/shard_map/ppermute | solution.py:259
  42.2 1.3 %collective-permute-start.10 = (bf16[16,8192]{1,0:T(8,128)(2,1)S(1)}, bf16[16,8192]{1,0:T(8,128)(2,1)S(1)}, u32[]{:S(2)}, u32[]{:S(2)}) collective-permute-start(bf16[16,8192]{1,0:T(8,128)(2,1)S(1)} %get-tuple-element.40), channel_id=1, source_target_pairs={{0,2},{1,3},{2,0},{3,1},{4,6},{5,7},{6,4},{7,5},{8,10},{9,11},{10,... | collective-permute-start | bytes 786440 | tf_op jit(solution)/shard_map/ppermute | solution.py:259
  43.6 2.3 %collective-permute-done.15 = bf16[16,4096]{1,0:T(8,128)(2,1)S(1)} collective-permute-done((bf16[16,4096]{1,0:T(8,128)(2,1)S(1)}, bf16[16,4096]{1,0:T(8,128)(2,1)S(1)}, u32[]{:S(2)}, u32[]{:S(2)}) %collective-permute-start.15) | collective-permute-done | bytes 131104 | tf_op jit(solution)/shard_map/ppermute | solution.py:259
  46.0 1.9 %collective-permute-done.17 = bf16[16,4096]{1,0:T(8,128)(2,1)S(1)} collective-permute-done((bf16[16,4096]{1,0:T(8,128)(2,1)S(1)}, bf16[16,4096]{1,0:T(8,128)(2,1)S(1)}, u32[]{:S(2)}, u32[]{:S(2)}) %collective-permute-start.17) | collective-permute-done | bytes 131104 | tf_op jit(solution)/shard_map/ppermute | solution.py:259
  48.7 2.8 %collective-permute-done.19 = bf16[16,4096]{1,0:T(8,128)(2,1)S(1)} collective-permute-done((bf16[16,4096]{1,0:T(8,128)(2,1)S(1)}, bf16[16,4096]{1,0:T(8,128)(2,1)S(1)}, u32[]{:S(2)}, u32[]{:S(2)}) %collective-permute-start.19) | collective-permute-done | bytes 131104 | tf_op jit(solution)/shard_map/ppermute | solution.py:259
  51.6 1.2 %collective-permute-start.16 = (bf16[16,4096]{1,0:T(8,128)(2,1)S(1)}, bf16[16,4096]{1,0:T(8,128)(2,1)S(1)}, u32[]{:S(2)}, u32[]{:S(2)}) collective-permute-start(bf16[16,4096]{1,0:T(8,128)(2,1)S(1)} %get-tuple-element.57), channel_id=1, source_target_pairs={{0,8},{1,9},{2,10},{3,11},{4,12},{5,13},{6,14},{7,15},{8,0},{9,1},... | collective-permute-start | bytes 393224 | tf_op jit(solution)/shard_map/ppermute | solution.py:292
  52.8 1.8 %collective-permute-start.20 = (bf16[16,4096]{1,0:T(8,128)(2,1)S(1)}, bf16[16,4096]{1,0:T(8,128)(2,1)S(1)}, u32[]{:S(2)}, u32[]{:S(2)}) collective-permute-start(bf16[16,4096]{1,0:T(8,128)(2,1)S(1)} %get-tuple-element.58), channel_id=1, source_target_pairs={{0,8},{1,9},{2,10},{3,11},{4,12},{5,13},{6,14},{7,15},{8,0},{9,1},... | collective-permute-start | bytes 393224 | tf_op jit(solution)/shard_map/ppermute | solution.py:292
  54.9 6.8 %collective-permute-done.11 = bf16[16,8192]{1,0:T(8,128)(2,1)S(1)} collective-permute-done((bf16[16,8192]{1,0:T(8,128)(2,1)S(1)}, bf16[16,8192]{1,0:T(8,128)(2,1)S(1)}, u32[]{:S(2)}, u32[]{:S(2)}) %collective-permute-start.11) | collective-permute-done | bytes 262176 | tf_op jit(solution)/shard_map/ppermute | solution.py:259
  61.8 5.7 %collective-permute-done.12 = bf16[16,8192]{1,0:T(8,128)(2,1)S(1)} collective-permute-done((bf16[16,8192]{1,0:T(8,128)(2,1)S(1)}, bf16[16,8192]{1,0:T(8,128)(2,1)S(1)}, u32[]{:S(2)}, u32[]{:S(2)}) %collective-permute-start.12) | collective-permute-done | bytes 262176 | tf_op jit(solution)/shard_map/ppermute | solution.py:259
  (36 shorter events, 6.3 us)
Async XLA Ops:
  6.1 1.4 %collective-permute-start = (bf16[4,8,16,128]{3,2,1,0:T(8,128)(2,1)S(1)}, bf16[4,8,16,128]{3,2,1,0:T(8,128)(2,1)S(1)}, u32[]{:S(2)}, u32[]{:S(2)}) collective-permute-start(bf16[4,8,16,128]{3,2,1,0:T(8,128)(2,1)S(1)} %get-tuple-element.70), channel_id=1, source_target_pairs={{0,1},{1,0},{2,3},{3,2},{4,5},{5,4},{6,7},{7,6},{8,9},{9,8},{10,11... | collective-permute-start | bytes 393224 | tf_op jit(solution)/shard_map/ppermute | solution.py:259
  7.6 10.7 %collective-permute-start.5 = (bf16[2,8,16,128]{3,2,1,0:T(8,128)(2,1)S(1)}, bf16[2,8,16,128]{3,2,1,0:T(8,128)(2,1)S(1)}, u32[]{:S(2)}, u32[]{:S(2)}) collective-permute-start(bf16[2,8,16,128]{3,2,1,0:T(8,128)(2,1)S(1)} %get-tuple-element.67), channel_id=1, source_target_pairs={{0,2},{1,3},{2,0},{3,1},{4,6},{5,7},{6,4},{7,5},{8,10},{9,11},{10,... | collective-permute-start | bytes 196616 | tf_op jit(solution)/shard_map/ppermute | solution.py:292
  12.0 8.5 %collective-permute-start.6 = (bf16[2,8,16,128]{3,2,1,0:T(8,128)(2,1)S(1)}, bf16[2,8,16,128]{3,2,1,0:T(8,128)(2,1)S(1)}, u32[]{:S(2)}, u32[]{:S(2)}) collective-permute-start(bf16[2,8,16,128]{3,2,1,0:T(8,128)(2,1)S(1)} %get-tuple-element.66), channel_id=1, source_target_pairs={{0,4},{1,5},{2,6},{3,7},{4,0},{5,1},{6,2},{7,3},{8,12},{9,13},{10,... | collective-permute-start | bytes 196616 | tf_op jit(solution)/shard_map/ppermute | solution.py:292
  13.0 7.5 %collective-permute-start.7 = (bf16[2,8,16,128]{3,2,1,0:T(8,128)(2,1)S(1)}, bf16[2,8,16,128]{3,2,1,0:T(8,128)(2,1)S(1)}, u32[]{:S(2)}, u32[]{:S(2)}) collective-permute-start(bf16[2,8,16,128]{3,2,1,0:T(8,128)(2,1)S(1)} %get-tuple-element.65), channel_id=1, source_target_pairs={{0,6},{1,7},{2,4},{3,5},{4,2},{5,3},{6,0},{7,1},{8,14},{9,15},{10,... | collective-permute-start | bytes 196616 | tf_op jit(solution)/shard_map/ppermute | solution.py:292
  13.5 13.4 %collective-permute-start.2 = (bf16[2,8,16,128]{3,2,1,0:T(8,128)(2,1)S(1)}, bf16[2,8,16,128]{3,2,1,0:T(8,128)(2,1)S(1)}, u32[]{:S(2)}, u32[]{:S(2)}) collective-permute-start(bf16[2,8,16,128]{3,2,1,0:T(8,128)(2,1)S(1)} %get-tuple-element.67), channel_id=1, source_target_pairs={{0,10},{1,11},{2,8},{3,9},{4,14},{5,15},{6,12},{7,13},{8,2},{9,3},... | collective-permute-start | bytes 196616 | tf_op jit(solution)/shard_map/ppermute | solution.py:292
  17.0 10.0 %collective-permute-start.3 = (bf16[2,8,16,128]{3,2,1,0:T(8,128)(2,1)S(1)}, bf16[2,8,16,128]{3,2,1,0:T(8,128)(2,1)S(1)}, u32[]{:S(2)}, u32[]{:S(2)}) collective-permute-start(bf16[2,8,16,128]{3,2,1,0:T(8,128)(2,1)S(1)} %get-tuple-element.66), channel_id=1, source_target_pairs={{0,12},{1,13},{2,14},{3,15},{4,8},{5,9},{6,10},{7,11},{8,4},{9,5},... | collective-permute-start | bytes 196616 | tf_op jit(solution)/shard_map/ppermute | solution.py:292
  18.3 8.6 %collective-permute-start.4 = (bf16[2,8,16,128]{3,2,1,0:T(8,128)(2,1)S(1)}, bf16[2,8,16,128]{3,2,1,0:T(8,128)(2,1)S(1)}, u32[]{:S(2)}, u32[]{:S(2)}) collective-permute-start(bf16[2,8,16,128]{3,2,1,0:T(8,128)(2,1)S(1)} %get-tuple-element.65), channel_id=1, source_target_pairs={{0,14},{1,15},{2,12},{3,13},{4,10},{5,11},{6,8},{7,9},{8,6},{9,7},... | collective-permute-start | bytes 196616 | tf_op jit(solution)/shard_map/ppermute | solution.py:292
  20.5 9.0 %collective-permute-start.1 = (bf16[2,8,16,128]{3,2,1,0:T(8,128)(2,1)S(1)}, bf16[2,8,16,128]{3,2,1,0:T(8,128)(2,1)S(1)}, u32[]{:S(2)}, u32[]{:S(2)}) collective-permute-start(bf16[2,8,16,128]{3,2,1,0:T(8,128)(2,1)S(1)} %bitcast.53), channel_id=1, source_target_pairs={{0,8},{1,9},{2,10},{3,11},{4,12},{5,13},{6,14},{7,15},{8,0},{9,1},... | collective-permute-start | bytes 196616 | tf_op jit(solution)/shard_map/ppermute | solution.py:292
  29.5 2.9 %collective-permute-start.9 = (bf16[4,16,8192]{2,1,0:T(8,128)(2,1)S(1)}, bf16[4,16,8192]{2,1,0:T(8,128)(2,1)S(1)}, u32[]{:S(2)}, u32[]{:S(2)}) collective-permute-start(bf16[4,16,8192]{2,1,0:T(8,128)(2,1)S(1)} %get-tuple-element.38), channel_id=1, source_target_pairs={{0,1},{1,0},{2,3},{3,2},{4,5},{5,4},{6,7},{7,6},{8,9},{9,8},{10,11... | collective-permute-start | bytes 3145736 | tf_op jit(solution)/shard_map/ppermute | solution.py:259
  31.9 2.9 %collective-permute-start.8 = (bf16[4,16,8192]{2,1,0:T(8,128)(2,1)S(1)}, bf16[4,16,8192]{2,1,0:T(8,128)(2,1)S(1)}, u32[]{:S(2)}, u32[]{:S(2)}) collective-permute-start(bf16[4,16,8192]{2,1,0:T(8,128)(2,1)S(1)} %get-tuple-element.36), channel_id=1, source_target_pairs={{0,1},{1,0},{2,3},{3,2},{4,5},{5,4},{6,7},{7,6},{8,9},{9,8},{10,11... | collective-permute-start | bytes 3145736 | tf_op jit(solution)/shard_map/ppermute | solution.py:259
  35.0 5.8 %collective-permute-start.13 = (bf16[16,4096]{1,0:T(8,128)(2,1)S(1)}, bf16[16,4096]{1,0:T(8,128)(2,1)S(1)}, u32[]{:S(2)}, u32[]{:S(2)}) collective-permute-start(bf16[16,4096]{1,0:T(8,128)(2,1)S(1)} %get-tuple-element.59), channel_id=1, source_target_pairs={{0,2},{1,3},{2,0},{3,1},{4,6},{5,7},{6,4},{7,5},{8,10},{9,11},{10,... | collective-permute-start | bytes 393224 | tf_op jit(solution)/shard_map/ppermute | solution.py:259
  35.6 6.7 %collective-permute-start.14 = (bf16[16,4096]{1,0:T(8,128)(2,1)S(1)}, bf16[16,4096]{1,0:T(8,128)(2,1)S(1)}, u32[]{:S(2)}, u32[]{:S(2)}) collective-permute-start(bf16[16,4096]{1,0:T(8,128)(2,1)S(1)} %get-tuple-element.61), channel_id=1, source_target_pairs={{0,4},{1,5},{2,6},{3,7},{4,0},{5,1},{6,2},{7,3},{8,12},{9,13},{10,... | collective-permute-start | bytes 393224 | tf_op jit(solution)/shard_map/ppermute | solution.py:259
  36.4 9.4 %collective-permute-start.15 = (bf16[16,4096]{1,0:T(8,128)(2,1)S(1)}, bf16[16,4096]{1,0:T(8,128)(2,1)S(1)}, u32[]{:S(2)}, u32[]{:S(2)}) collective-permute-start(bf16[16,4096]{1,0:T(8,128)(2,1)S(1)} %get-tuple-element.63), channel_id=1, source_target_pairs={{0,6},{1,7},{2,4},{3,5},{4,2},{5,3},{6,0},{7,1},{8,14},{9,15},{10,... | collective-permute-start | bytes 393224 | tf_op jit(solution)/shard_map/ppermute | solution.py:259
  38.7 9.2 %collective-permute-start.17 = (bf16[16,4096]{1,0:T(8,128)(2,1)S(1)}, bf16[16,4096]{1,0:T(8,128)(2,1)S(1)}, u32[]{:S(2)}, u32[]{:S(2)}) collective-permute-start(bf16[16,4096]{1,0:T(8,128)(2,1)S(1)} %get-tuple-element.60), channel_id=1, source_target_pairs={{0,2},{1,3},{2,0},{3,1},{4,6},{5,7},{6,4},{7,5},{8,10},{9,11},{10,... | collective-permute-start | bytes 393224 | tf_op jit(solution)/shard_map/ppermute | solution.py:259
  39.2 9.5 %collective-permute-start.18 = (bf16[16,4096]{1,0:T(8,128)(2,1)S(1)}, bf16[16,4096]{1,0:T(8,128)(2,1)S(1)}, u32[]{:S(2)}, u32[]{:S(2)}) collective-permute-start(bf16[16,4096]{1,0:T(8,128)(2,1)S(1)} %get-tuple-element.62), channel_id=1, source_target_pairs={{0,4},{1,5},{2,6},{3,7},{4,0},{5,1},{6,2},{7,3},{8,12},{9,13},{10,... | collective-permute-start | bytes 393224 | tf_op jit(solution)/shard_map/ppermute | solution.py:259
  40.8 10.7 %collective-permute-start.19 = (bf16[16,4096]{1,0:T(8,128)(2,1)S(1)}, bf16[16,4096]{1,0:T(8,128)(2,1)S(1)}, u32[]{:S(2)}, u32[]{:S(2)}) collective-permute-start(bf16[16,4096]{1,0:T(8,128)(2,1)S(1)} %get-tuple-element.64), channel_id=1, source_target_pairs={{0,6},{1,7},{2,4},{3,5},{4,2},{5,3},{6,0},{7,1},{8,14},{9,15},{10,... | collective-permute-start | bytes 393224 | tf_op jit(solution)/shard_map/ppermute | solution.py:259
  42.2 12.7 %collective-permute-start.10 = (bf16[16,8192]{1,0:T(8,128)(2,1)S(1)}, bf16[16,8192]{1,0:T(8,128)(2,1)S(1)}, u32[]{:S(2)}, u32[]{:S(2)}) collective-permute-start(bf16[16,8192]{1,0:T(8,128)(2,1)S(1)} %get-tuple-element.40), channel_id=1, source_target_pairs={{0,2},{1,3},{2,0},{3,1},{4,6},{5,7},{6,4},{7,5},{8,10},{9,11},{10,... | collective-permute-start | bytes 786440 | tf_op jit(solution)/shard_map/ppermute | solution.py:259
  45.8 15.9 %collective-permute-start.11 = (bf16[16,8192]{1,0:T(8,128)(2,1)S(1)}, bf16[16,8192]{1,0:T(8,128)(2,1)S(1)}, u32[]{:S(2)}, u32[]{:S(2)}) collective-permute-start(bf16[16,8192]{1,0:T(8,128)(2,1)S(1)} %get-tuple-element.41), channel_id=1, source_target_pairs={{0,4},{1,5},{2,6},{3,7},{4,0},{5,1},{6,2},{7,3},{8,12},{9,13},{10,... | collective-permute-start | bytes 786440 | tf_op jit(solution)/shard_map/ppermute | solution.py:259
  48.0 19.5 %collective-permute-start.12 = (bf16[16,8192]{1,0:T(8,128)(2,1)S(1)}, bf16[16,8192]{1,0:T(8,128)(2,1)S(1)}, u32[]{:S(2)}, u32[]{:S(2)}) collective-permute-start(bf16[16,8192]{1,0:T(8,128)(2,1)S(1)} %get-tuple-element.42), channel_id=1, source_target_pairs={{0,6},{1,7},{2,4},{3,5},{4,2},{5,3},{6,0},{7,1},{8,14},{9,15},{10,... | collective-permute-start | bytes 786440 | tf_op jit(solution)/shard_map/ppermute | solution.py:259
  51.6 16.0 %collective-permute-start.16 = (bf16[16,4096]{1,0:T(8,128)(2,1)S(1)}, bf16[16,4096]{1,0:T(8,128)(2,1)S(1)}, u32[]{:S(2)}, u32[]{:S(2)}) collective-permute-start(bf16[16,4096]{1,0:T(8,128)(2,1)S(1)} %get-tuple-element.57), channel_id=1, source_target_pairs={{0,8},{1,9},{2,10},{3,11},{4,12},{5,13},{6,14},{7,15},{8,0},{9,1},... | collective-permute-start | bytes 393224 | tf_op jit(solution)/shard_map/ppermute | solution.py:292
  52.8 14.8 %collective-permute-start.20 = (bf16[16,4096]{1,0:T(8,128)(2,1)S(1)}, bf16[16,4096]{1,0:T(8,128)(2,1)S(1)}, u32[]{:S(2)}, u32[]{:S(2)}) collective-permute-start(bf16[16,4096]{1,0:T(8,128)(2,1)S(1)} %get-tuple-element.58), channel_id=1, source_target_pairs={{0,8},{1,9},{2,10},{3,11},{4,12},{5,13},{6,14},{7,15},{8,0},{9,1},... | collective-permute-start | bytes 393224 | tf_op jit(solution)/shard_map/ppermute | solution.py:292

commit v5 on v4

--- a/solution.py
+++ b/solution.py
@@ -16,7 +16,7 @@
 GROUP = QH // KVH
 BLOCK_HEADS = QH // GRID_ROWS
 CHUNKS = 1
-SENDS = 2
+SENDS = 1
 TILE_N = 1024
 PAGE = 128
 TOGETHER = 4
@@ -313,6 +313,7 @@
     near = pair_sums(near_keep, swap(near_give, 1))
     far = pair_sums(partial[0], swap(partial[1], 1))
     far, near = lax.optimization_barrier((far, near))
+    near = direct(*near)
     backs = []
     width = col_width // SENDS
     for first in range(0, col_width, width):
@@ -320,7 +321,6 @@
         sums = direct(far[0][:, lanes], [value[:, lanes] for value in far[1]])
         sums = sums.reshape(cols - 1, slot_rows, -1)
         backs.append(jnp.stack([send(sums[s - 1], cols - s, 0) for s in range(1, cols)]))
-    near = direct(*near)
     stacked = jnp.concatenate([near[None], jnp.concatenate(backs, axis=-1)])
     blocks = [
         lax.dynamic_index_in_dim(stacked, lax.rem(j - own_block + cols, cols), 0, False)

time: 68.5 us -> 68.4 us (level)
  starting transfers between devices: 25.4 us -> 20 us
  waiting for transfers between devices: 26.4 us -> 30.3 us
  Pallas kernels: 13.7 us -> 14.7 us
    ppermute x12 -> x9, waiting for transfers between devices: 23.9 us -> 28.4 us  [swap(): lax.ppermute(value, 'tile', [(i, i ^ distance) for i in range(devices)])]
    ppermute x12 -> x9, starting transfers between devices: 9.49 us -> 6.08 us  [swap(): lax.ppermute(value, 'tile', [(i, i ^ distance) for i in range(devices)])]
    ppermute x9 -> x8, starting transfers between devices: 15.9 us -> 14 us  [send(): return lax.ppermute(value, 'tile', [(i, target(i)) for i in range(devices)])]
    pallas_call x1, Pallas kernels: 4.9 us -> 5.88 us  [attend(): pl.pallas_call(attention_kernel, out_shape=jax.ShapeDtypeStruct((slots, r...]
    ppermute x9 -> x8, waiting for transfers between devices: 2.54 us -> 1.81 us  [send(): return lax.ppermute(value, 'tile', [(i, target(i)) for i in range(devices)])]
  transfers between devices with their start and end apart: 21 -> 17, of which waited for: 10 -> 8; matrix products, arithmetic and copies ran while one was open for 1% -> 1% of each run, Pallas kernels for 13% -> 13%
where the time goes in v5:
time: 68.4 us; the launch traced here: 68.1 us
  waiting for transfers between devices  30.3 us (44%)
  starting transfers between devices  20 us (29%)
  Pallas kernels  14.7 us (21%)
  other arithmetic  1.78 us (3%)
  local copies, waits for them, and re-layouts  1.19 us (2%)
    ppermute x9, waiting for transfers between devices, swap(): lax.ppermute(value, 'tile', [(i, i ^ distance) for i in range(devices)])  28.4 us
    ppermute x8, starting transfers between devices, send(): return lax.ppermute(value, 'tile', [(i, target(i)) for i in range(devices)])  14 us
    pallas_call x1, Pallas kernels, project_near(): pl.pallas_call(near_kernel, in_specs=[vmem] * 4 + [pl.BlockSpec(memory_sp...  6.44 us
    ppermute x9, starting transfers between devices, swap(): lax.ppermute(value, 'tile', [(i, i ^ distance) for i in range(devices)])  6.08 us
    pallas_call x1, Pallas kernels, attend(): pl.pallas_call(attention_kernel, out_shape=jax.ShapeDtypeStruct((slots, r...  5.88 us
    pallas_call x1, Pallas kernels, project_far(): pl.pallas_call(far_kernel, in_specs=[vmem] * 5, out_specs=[vmem] * (2 * C...  2.36 us
    ppermute x8, waiting for transfers between devices, send(): return lax.ppermute(value, 'tile', [(i, target(i)) for i in range(devices)])  1.81 us
  transfers between devices with their start and end apart: 17, of which 8 were waited for; matrix products, arithmetic and copies ran while one was open for 1% of the time, Pallas kernels for 13%

profile of v5, /device:TPU:0, one launch (start us, length us, event | category | flops | bytes accessed | tf_op | source)
XLA Modules:
  0.0 68.1 jit_solution(17102747052310196571)
XLA Ops:
  0.0 1.0 %copy.6 = bf16[2,8,4,16,128]{4,3,0,2,1:T(8,128)(2,1)S(1)} copy(bf16[2,8,4,16,128]{4,1,3,2,0:T(8,128)(2,1)} %bitcast.62) | data formatting | bytes 524288 | tf_op jit(solution)/shard_map/reshape | solution.py:139
  1.0 5.9 %attention.1 = bf16[8,128,128]{2,1,0:T(8,128)(2,1)S(1)} custom-call(s32[8]{0:T(128)} %lengths_ref.1, bf16[8,128,128]{2,1,0:T(8,128)(2,1)S(1)} %bitcast.51, bf16[2,2,8,512]{3,2,1,0:T(8,128)(2,1)} %fresh_ref.1, bf16[2,8,512,512]{3,2,1,0:T(8,128)(2,1)} %cache_ref.1), custom_call_target="tpu_custom_call" | custom-call | tf_op jit(solution)/shard_map/attention/pallas_call | solution.py:143
  7.2 1.3 %collective-permute-done = bf16[4,8,16,128]{3,2,1,0:T(8,128)(2,1)S(1)} collective-permute-done((bf16[4,8,16,128]{3,2,1,0:T(8,128)(2,1)S(1)}, bf16[4,8,16,128]{3,2,1,0:T(8,128)(2,1)S(1)}, u32[]{:S(2)}, u32[]{:S(2)}) %collective-permute-start) | collective-permute-done | bytes 131104 | tf_op jit(solution)/shard_map/ppermute | solution.py:259
  8.6 2.9 %collective-permute-start.5 = (bf16[2,8,16,128]{3,2,1,0:T(8,128)(2,1)S(1)}, bf16[2,8,16,128]{3,2,1,0:T(8,128)(2,1)S(1)}, u32[]{:S(2)}, u32[]{:S(2)}) collective-permute-start(bf16[2,8,16,128]{3,2,1,0:T(8,128)(2,1)S(1)} %get-tuple-element.59), channel_id=1, source_target_pairs={{0,2},{1,3},{2,0},{3,1},{4,6},{5,7},{6,4},{7,5},{8,10},{9,11},{10,... | collective-permute-start | bytes 196616 | tf_op jit(solution)/shard_map/ppermute | solution.py:292
  11.5 1.2 %collective-permute-start.6 = (bf16[2,8,16,128]{3,2,1,0:T(8,128)(2,1)S(1)}, bf16[2,8,16,128]{3,2,1,0:T(8,128)(2,1)S(1)}, u32[]{:S(2)}, u32[]{:S(2)}) collective-permute-start(bf16[2,8,16,128]{3,2,1,0:T(8,128)(2,1)S(1)} %get-tuple-element.58), channel_id=1, source_target_pairs={{0,4},{1,5},{2,6},{3,7},{4,0},{5,1},{6,2},{7,3},{8,12},{9,13},{10,... | collective-permute-start | bytes 196616 | tf_op jit(solution)/shard_map/ppermute | solution.py:292
  13.0 4.0 %collective-permute-start.2 = (bf16[2,8,16,128]{3,2,1,0:T(8,128)(2,1)S(1)}, bf16[2,8,16,128]{3,2,1,0:T(8,128)(2,1)S(1)}, u32[]{:S(2)}, u32[]{:S(2)}) collective-permute-start(bf16[2,8,16,128]{3,2,1,0:T(8,128)(2,1)S(1)} %get-tuple-element.59), channel_id=1, source_target_pairs={{0,10},{1,11},{2,8},{3,9},{4,14},{5,15},{6,12},{7,13},{8,2},{9,3},... | collective-permute-start | bytes 196616 | tf_op jit(solution)/shard_map/ppermute | solution.py:292
  17.0 0.9 %collective-permute-start.3 = (bf16[2,8,16,128]{3,2,1,0:T(8,128)(2,1)S(1)}, bf16[2,8,16,128]{3,2,1,0:T(8,128)(2,1)S(1)}, u32[]{:S(2)}, u32[]{:S(2)}) collective-permute-start(bf16[2,8,16,128]{3,2,1,0:T(8,128)(2,1)S(1)} %get-tuple-element.58), channel_id=1, source_target_pairs={{0,12},{1,13},{2,14},{3,15},{4,8},{5,9},{6,10},{7,11},{8,4},{9,5},... | collective-permute-start | bytes 196616 | tf_op jit(solution)/shard_map/ppermute | solution.py:292
  18.0 2.9 %collective-permute-start.4 = (bf16[2,8,16,128]{3,2,1,0:T(8,128)(2,1)S(1)}, bf16[2,8,16,128]{3,2,1,0:T(8,128)(2,1)S(1)}, u32[]{:S(2)}, u32[]{:S(2)}) collective-permute-start(bf16[2,8,16,128]{3,2,1,0:T(8,128)(2,1)S(1)} %get-tuple-element.57), channel_id=1, source_target_pairs={{0,14},{1,15},{2,12},{3,13},{4,10},{5,11},{6,8},{7,9},{8,6},{9,7},... | collective-permute-start | bytes 196616 | tf_op jit(solution)/shard_map/ppermute | solution.py:292
  20.9 6.4 %project_near.1 = (bf16[4,16,8192]{2,1,0:T(8,128)(2,1)S(1)}, bf16[4,16,8192]{2,1,0:T(8,128)(2,1)S(1)}, bf16[1024,8192]{1,0:T(8,128)(2,1)S(1)}) custom-call(bf16[1,2,8,16,128]{4,3,2,1,0:T(8,128)(2,1)S(1)} %get-tuple-element.60.refs_0_, bf16[1,2,8,16,128]{4,3,2,1,0:T(8,128)(2,1)S(1)} %bitcast.56, bf16[1,2,8,16,128]{4,3,2,1,0:T(8,128)(2,1)S(1)} %bitcast.58, ...), custom_call_target="tpu_custom_call" | custom-call | flops 2147483648 | bytes 33554432 | tf_op jit(solution)/shard_map/project_near/pallas_call | solution.py:207
  27.4 1.8 %collective-permute-done.1 = bf16[2,8,16,128]{3,2,1,0:T(8,128)(2,1)S(1)} collective-permute-done((bf16[2,8,16,128]{3,2,1,0:T(8,128)(2,1)S(1)}, bf16[2,8,16,128]{3,2,1,0:T(8,128)(2,1)S(1)}, u32[]{:S(2)}, u32[]{:S(2)}) %collective-permute-start.1) | collective-permute-done | bytes 65568 | tf_op jit(solution)/shard_map/ppermute | solution.py:292
  29.2 2.4 %project_far.1 = (bf16[4,16,8192]{2,1,0:T(8,128)(2,1)S(1)}, bf16[4,16,8192]{2,1,0:T(8,128)(2,1)S(1)}) custom-call(bf16[1,2,8,16,128]{4,3,2,1,0:T(8,128)(2,1)S(1)} %bitcast.57, bf16[1,2,8,16,128]{4,3,2,1,0:T(8,128)(2,1)S(1)} %bitcast.53, bf16[1,2,8,16,128]{4,3,2,1,0:T(8,128)(2,1)S(1)} %bitcast.54, bf16[1,2,8,16,128]{4,3,2,1,0:T(8,128)(2,1)S(1)} %bitcast.55, ...), custom_call_target="tpu_custom_call" | custom-call | flops 2147483648 | bytes 16777216 | tf_op jit(solution)/shard_map/project_far/pallas_call | solution.py:243
  32.3 2.0 %collective-permute-done.8 = bf16[4,16,8192]{2,1,0:T(8,128)(2,1)S(1)} collective-permute-done((bf16[4,16,8192]{2,1,0:T(8,128)(2,1)S(1)}, bf16[4,16,8192]{2,1,0:T(8,128)(2,1)S(1)}, u32[]{:S(2)}, u32[]{:S(2)}) %collective-permute-start.8) | collective-permute-done | bytes 1048608 | tf_op jit(solution)/shard_map/ppermute | solution.py:259
  34.6 0.7 collective-permute-start.13
  35.3 0.6 collective-permute-start.14
  35.9 2.3 %collective-permute-start.15 = (bf16[16,8192]{1,0:T(8,128)(2,1)S(1)}, bf16[16,8192]{1,0:T(8,128)(2,1)S(1)}, u32[]{:S(2)}, u32[]{:S(2)}) collective-permute-start(bf16[16,8192]{1,0:T(8,128)(2,1)S(1)} %get-tuple-element.46), channel_id=1, source_target_pairs={{0,6},{1,7},{2,4},{3,5},{4,2},{5,3},{6,0},{7,1},{8,14},{9,15},{10,... | collective-permute-start | bytes 786440 | tf_op jit(solution)/shard_map/ppermute | solution.py:259
  38.8 0.6 collective-permute-start.11
  39.4 4.7 %collective-permute-done.13 = bf16[16,8192]{1,0:T(8,128)(2,1)S(1)} collective-permute-done((bf16[16,8192]{1,0:T(8,128)(2,1)S(1)}, bf16[16,8192]{1,0:T(8,128)(2,1)S(1)}, u32[]{:S(2)}, u32[]{:S(2)}) %collective-permute-start.13) | collective-permute-done | bytes 262176 | tf_op jit(solution)/shard_map/ppermute | solution.py:259
  44.1 0.7 collective-permute-start.12
  44.7 6.3 %collective-permute-done.15 = bf16[16,8192]{1,0:T(8,128)(2,1)S(1)} collective-permute-done((bf16[16,8192]{1,0:T(8,128)(2,1)S(1)}, bf16[16,8192]{1,0:T(8,128)(2,1)S(1)}, u32[]{:S(2)}, u32[]{:S(2)}) %collective-permute-start.15) | collective-permute-done | bytes 262176 | tf_op jit(solution)/shard_map/ppermute | solution.py:259
  51.1 1.7 %collective-permute-start.16 = (bf16[16,8192]{1,0:T(8,128)(2,1)S(1)}, bf16[16,8192]{1,0:T(8,128)(2,1)S(1)}, u32[]{:S(2)}, u32[]{:S(2)}) collective-permute-start(bf16[16,8192]{1,0:T(8,128)(2,1)S(1)} %add_convert_fusion), channel_id=1, source_target_pairs={{0,8},{1,9},{2,10},{3,11},{4,12},{5,13},{6,14},{7,15},{8,0},{9,1},... | collective-permute-start | bytes 786440 | tf_op jit(solution)/shard_map/ppermute | solution.py:292
  52.8 1.7 %collective-permute-done.10 = bf16[16,8192]{1,0:T(8,128)(2,1)S(1)} collective-permute-done((bf16[16,8192]{1,0:T(8,128)(2,1)S(1)}, bf16[16,8192]{1,0:T(8,128)(2,1)S(1)}, u32[]{:S(2)}, u32[]{:S(2)}) %collective-permute-start.10) | collective-permute-done | bytes 262176 | tf_op jit(solution)/shard_map/ppermute | solution.py:259
  54.5 6.9 %collective-permute-done.11 = bf16[16,8192]{1,0:T(8,128)(2,1)S(1)} collective-permute-done((bf16[16,8192]{1,0:T(8,128)(2,1)S(1)}, bf16[16,8192]{1,0:T(8,128)(2,1)S(1)}, u32[]{:S(2)}, u32[]{:S(2)}) %collective-permute-start.11) | collective-permute-done | bytes 262176 | tf_op jit(solution)/shard_map/ppermute | solution.py:259
  61.4 5.6 %collective-permute-done.12 = bf16[16,8192]{1,0:T(8,128)(2,1)S(1)} collective-permute-done((bf16[16,8192]{1,0:T(8,128)(2,1)S(1)}, bf16[16,8192]{1,0:T(8,128)(2,1)S(1)}, u32[]{:S(2)}, u32[]{:S(2)}) %collective-permute-start.12) | collective-permute-done | bytes 262176 | tf_op jit(solution)/shard_map/ppermute | solution.py:259
  67.3 0.8 %pad_maximum_fusion = bf16[2,8,16384]{2,1,0:T(8,128)(2,1)} fusion(bf16[2,8,8192]{2,1,0:T(8,128)(2,1)S(1)} %get-tuple-element.56, bf16[2,8,8192]{2,1,0:T(8,128)(2,1)S(1)} %get-tuple-element.55), kind=kLoop, calls=%fused_computation.4 | loop fusion | flops 1048576 | bytes 1048576 | tf_op jit(solution)/shard_map/concatenate | solution.py:329
  (24 shorter events, 2.8 us)
Async XLA Ops:
  7.1 1.4 %collective-permute-start = (bf16[4,8,16,128]{3,2,1,0:T(8,128)(2,1)S(1)}, bf16[4,8,16,128]{3,2,1,0:T(8,128)(2,1)S(1)}, u32[]{:S(2)}, u32[]{:S(2)}) collective-permute-start(bf16[4,8,16,128]{3,2,1,0:T(8,128)(2,1)S(1)} %get-tuple-element.62), channel_id=1, source_target_pairs={{0,1},{1,0},{2,3},{3,2},{4,5},{5,4},{6,7},{7,6},{8,9},{9,8},{10,11... | collective-permute-start | bytes 393224 | tf_op jit(solution)/shard_map/ppermute | solution.py:259
  8.6 9.4 %collective-permute-start.5 = (bf16[2,8,16,128]{3,2,1,0:T(8,128)(2,1)S(1)}, bf16[2,8,16,128]{3,2,1,0:T(8,128)(2,1)S(1)}, u32[]{:S(2)}, u32[]{:S(2)}) collective-permute-start(bf16[2,8,16,128]{3,2,1,0:T(8,128)(2,1)S(1)} %get-tuple-element.59), channel_id=1, source_target_pairs={{0,2},{1,3},{2,0},{3,1},{4,6},{5,7},{6,4},{7,5},{8,10},{9,11},{10,... | collective-permute-start | bytes 196616 | tf_op jit(solution)/shard_map/ppermute | solution.py:292
  11.5 9.4 %collective-permute-start.6 = (bf16[2,8,16,128]{3,2,1,0:T(8,128)(2,1)S(1)}, bf16[2,8,16,128]{3,2,1,0:T(8,128)(2,1)S(1)}, u32[]{:S(2)}, u32[]{:S(2)}) collective-permute-start(bf16[2,8,16,128]{3,2,1,0:T(8,128)(2,1)S(1)} %get-tuple-element.58), channel_id=1, source_target_pairs={{0,4},{1,5},{2,6},{3,7},{4,0},{5,1},{6,2},{7,3},{8,12},{9,13},{10,... | collective-permute-start | bytes 196616 | tf_op jit(solution)/shard_map/ppermute | solution.py:292
  12.7 8.2 %collective-permute-start.7 = (bf16[2,8,16,128]{3,2,1,0:T(8,128)(2,1)S(1)}, bf16[2,8,16,128]{3,2,1,0:T(8,128)(2,1)S(1)}, u32[]{:S(2)}, u32[]{:S(2)}) collective-permute-start(bf16[2,8,16,128]{3,2,1,0:T(8,128)(2,1)S(1)} %get-tuple-element.57), channel_id=1, source_target_pairs={{0,6},{1,7},{2,4},{3,5},{4,2},{5,3},{6,0},{7,1},{8,14},{9,15},{10,... | collective-permute-start | bytes 196616 | tf_op jit(solution)/shard_map/ppermute | solution.py:292
  13.0 14.3 %collective-permute-start.2 = (bf16[2,8,16,128]{3,2,1,0:T(8,128)(2,1)S(1)}, bf16[2,8,16,128]{3,2,1,0:T(8,128)(2,1)S(1)}, u32[]{:S(2)}, u32[]{:S(2)}) collective-permute-start(bf16[2,8,16,128]{3,2,1,0:T(8,128)(2,1)S(1)} %get-tuple-element.59), channel_id=1, source_target_pairs={{0,10},{1,11},{2,8},{3,9},{4,14},{5,15},{6,12},{7,13},{8,2},{9,3},... | collective-permute-start | bytes 196616 | tf_op jit(solution)/shard_map/ppermute | solution.py:292
  17.0 10.3 %collective-permute-start.3 = (bf16[2,8,16,128]{3,2,1,0:T(8,128)(2,1)S(1)}, bf16[2,8,16,128]{3,2,1,0:T(8,128)(2,1)S(1)}, u32[]{:S(2)}, u32[]{:S(2)}) collective-permute-start(bf16[2,8,16,128]{3,2,1,0:T(8,128)(2,1)S(1)} %get-tuple-element.58), channel_id=1, source_target_pairs={{0,12},{1,13},{2,14},{3,15},{4,8},{5,9},{6,10},{7,11},{8,4},{9,5},... | collective-permute-start | bytes 196616 | tf_op jit(solution)/shard_map/ppermute | solution.py:292
  18.0 9.4 %collective-permute-start.4 = (bf16[2,8,16,128]{3,2,1,0:T(8,128)(2,1)S(1)}, bf16[2,8,16,128]{3,2,1,0:T(8,128)(2,1)S(1)}, u32[]{:S(2)}, u32[]{:S(2)}) collective-permute-start(bf16[2,8,16,128]{3,2,1,0:T(8,128)(2,1)S(1)} %get-tuple-element.57), channel_id=1, source_target_pairs={{0,14},{1,15},{2,12},{3,13},{4,10},{5,11},{6,8},{7,9},{8,6},{9,7},... | collective-permute-start | bytes 196616 | tf_op jit(solution)/shard_map/ppermute | solution.py:292
  20.9 8.3 %collective-permute-start.1 = (bf16[2,8,16,128]{3,2,1,0:T(8,128)(2,1)S(1)}, bf16[2,8,16,128]{3,2,1,0:T(8,128)(2,1)S(1)}, u32[]{:S(2)}, u32[]{:S(2)}) collective-permute-start(bf16[2,8,16,128]{3,2,1,0:T(8,128)(2,1)S(1)} %bitcast.52), channel_id=1, source_target_pairs={{0,8},{1,9},{2,10},{3,11},{4,12},{5,13},{6,14},{7,15},{8,0},{9,1},... | collective-permute-start | bytes 196616 | tf_op jit(solution)/shard_map/ppermute | solution.py:292
  29.2 2.9 %collective-permute-start.9 = (bf16[4,16,8192]{2,1,0:T(8,128)(2,1)S(1)}, bf16[4,16,8192]{2,1,0:T(8,128)(2,1)S(1)}, u32[]{:S(2)}, u32[]{:S(2)}) collective-permute-start(bf16[4,16,8192]{2,1,0:T(8,128)(2,1)S(1)} %get-tuple-element.38), channel_id=1, source_target_pairs={{0,1},{1,0},{2,3},{3,2},{4,5},{5,4},{6,7},{7,6},{8,9},{9,8},{10,11... | collective-permute-start | bytes 3145736 | tf_op jit(solution)/shard_map/ppermute | solution.py:259
  31.5 2.9 %collective-permute-start.8 = (bf16[4,16,8192]{2,1,0:T(8,128)(2,1)S(1)}, bf16[4,16,8192]{2,1,0:T(8,128)(2,1)S(1)}, u32[]{:S(2)}, u32[]{:S(2)}) collective-permute-start(bf16[4,16,8192]{2,1,0:T(8,128)(2,1)S(1)} %get-tuple-element.36), channel_id=1, source_target_pairs={{0,1},{1,0},{2,3},{3,2},{4,5},{5,4},{6,7},{7,6},{8,9},{9,8},{10,11... | collective-permute-start | bytes 3145736 | tf_op jit(solution)/shard_map/ppermute | solution.py:259
  34.6 9.4 %collective-permute-start.13 = (bf16[16,8192]{1,0:T(8,128)(2,1)S(1)}, bf16[16,8192]{1,0:T(8,128)(2,1)S(1)}, u32[]{:S(2)}, u32[]{:S(2)}) collective-permute-start(bf16[16,8192]{1,0:T(8,128)(2,1)S(1)} %get-tuple-element.44), channel_id=1, source_target_pairs={{0,2},{1,3},{2,0},{3,1},{4,6},{5,7},{6,4},{7,5},{8,10},{9,11},{10,... | collective-permute-start | bytes 786440 | tf_op jit(solution)/shard_map/ppermute | solution.py:259
  35.3 9.4 %collective-permute-start.14 = (bf16[16,8192]{1,0:T(8,128)(2,1)S(1)}, bf16[16,8192]{1,0:T(8,128)(2,1)S(1)}, u32[]{:S(2)}, u32[]{:S(2)}) collective-permute-start(bf16[16,8192]{1,0:T(8,128)(2,1)S(1)} %get-tuple-element.45), channel_id=1, source_target_pairs={{0,4},{1,5},{2,6},{3,7},{4,0},{5,1},{6,2},{7,3},{8,12},{9,13},{10,... | collective-permute-start | bytes 786440 | tf_op jit(solution)/shard_map/ppermute | solution.py:259
  35.9 15.1 %collective-permute-start.15 = (bf16[16,8192]{1,0:T(8,128)(2,1)S(1)}, bf16[16,8192]{1,0:T(8,128)(2,1)S(1)}, u32[]{:S(2)}, u32[]{:S(2)}) collective-permute-start(bf16[16,8192]{1,0:T(8,128)(2,1)S(1)} %get-tuple-element.46), channel_id=1, source_target_pairs={{0,6},{1,7},{2,4},{3,5},{4,2},{5,3},{6,0},{7,1},{8,14},{9,15},{10,... | collective-permute-start | bytes 786440 | tf_op jit(solution)/shard_map/ppermute | solution.py:259
  38.2 16.3 %collective-permute-start.10 = (bf16[16,8192]{1,0:T(8,128)(2,1)S(1)}, bf16[16,8192]{1,0:T(8,128)(2,1)S(1)}, u32[]{:S(2)}, u32[]{:S(2)}) collective-permute-start(bf16[16,8192]{1,0:T(8,128)(2,1)S(1)} %get-tuple-element.40), channel_id=1, source_target_pairs={{0,2},{1,3},{2,0},{3,1},{4,6},{5,7},{6,4},{7,5},{8,10},{9,11},{10,... | collective-permute-start | bytes 786440 | tf_op jit(solution)/shard_map/ppermute | solution.py:259
  38.8 22.6 %collective-permute-start.11 = (bf16[16,8192]{1,0:T(8,128)(2,1)S(1)}, bf16[16,8192]{1,0:T(8,128)(2,1)S(1)}, u32[]{:S(2)}, u32[]{:S(2)}) collective-permute-start(bf16[16,8192]{1,0:T(8,128)(2,1)S(1)} %get-tuple-element.41), channel_id=1, source_target_pairs={{0,4},{1,5},{2,6},{3,7},{4,0},{5,1},{6,2},{7,3},{8,12},{9,13},{10,... | collective-permute-start | bytes 786440 | tf_op jit(solution)/shard_map/ppermute | solution.py:259
  44.1 22.9 %collective-permute-start.12 = (bf16[16,8192]{1,0:T(8,128)(2,1)S(1)}, bf16[16,8192]{1,0:T(8,128)(2,1)S(1)}, u32[]{:S(2)}, u32[]{:S(2)}) collective-permute-start(bf16[16,8192]{1,0:T(8,128)(2,1)S(1)} %get-tuple-element.42), channel_id=1, source_target_pairs={{0,6},{1,7},{2,4},{3,5},{4,2},{5,3},{6,0},{7,1},{8,14},{9,15},{10,... | collective-permute-start | bytes 786440 | tf_op jit(solution)/shard_map/ppermute | solution.py:259
  51.1 16.0 %collective-permute-start.16 = (bf16[16,8192]{1,0:T(8,128)(2,1)S(1)}, bf16[16,8192]{1,0:T(8,128)(2,1)S(1)}, u32[]{:S(2)}, u32[]{:S(2)}) collective-permute-start(bf16[16,8192]{1,0:T(8,128)(2,1)S(1)} %add_convert_fusion), channel_id=1, source_target_pairs={{0,8},{1,9},{2,10},{3,11},{4,12},{5,13},{6,14},{7,15},{8,0},{9,1},... | collective-permute-start | bytes 786440 | tf_op jit(solution)/shard_map/ppermute | solution.py:292
